TPU v7x, 256 devices: a whole 4x4x8 slice. The times are simulated.
256 devices in a mesh: tile: 32 (over y, z_hi, core), head: 8 (over z_lo, x).
Axes of the slice: x: 4, y: 4, z: 8 (z_hi: 4, z_lo: 2; z = z_hi * 2 + z_lo), core: 2. Of those that a mesh axis runs over, the one named last changes fastest.
Arguments:
- video_q: bfloat16 [16384, 3072], P('tile', 'head'), may hold values from -16 to 16
- video_k: bfloat16 [16384, 3072], P('tile', 'head'), may hold values from -16 to 16
- video_v: bfloat16 [16384, 3072], P('tile', 'head'), may hold values from -12 to 12
- text_q: bfloat16 [256, 3072], P('tile', 'head'), may hold values from -16 to 16
- text_k: bfloat16 [256, 3072], P('tile', 'head'), may hold values from -10 to 10
- text_v: bfloat16 [256, 3072], P('tile', 'head'), may hold values from -12 to 12
- video_proj: bfloat16 [3072, 3072], P('head'), may hold values from -0.109375 to 0.109375
- text_proj: bfloat16 [3072, 3072], P('head'), may hold values from -0.109375 to 0.109375
- window_mask: int32 [64, 27], P('tile'), may hold values from 0 to 1, as said below
- text_length: int32 [1], replicated, may hold values from 64 to 256
Outputs:
- video_out: bfloat16 [16384, 3072], P('tile', 'head')
- text_out: bfloat16 [256, 3072], P('tile', 'head')
Inputs may be any that keep to these rules, and one draw needn't show every extreme that they name: window_mask[s, 9 a + 3 b + c] is 1 only if the tile at frame, row and column offsets a - 1, b - 1, c - 1 from tile s lies inside the grid of 2 x 4 x 8 tiles; the centre entry 13 is always 1.
All inputs are finite; a program needn't handle non-finite values.
Results may differ from a plain program's by a relative error of at most 0.013.
Values may be sent and summed in bfloat16 or wider, within the bound.
No kernel may reach another device: no remote copies, remote signals or barrier semaphores. Data moves between devices by JAX's collectives and lax.ppermute only.
A program may use at most 128 MiB of HBM per device.

v0:
```python
import math

import jax
import jax.numpy as jnp
from jax import lax
from jax.sharding import PartitionSpec as P

HD = 128
TILE_TOK = 256
GT = 2
BH = 1
DH = 4
BW = 1


NEG_FILL = -1e30


def side_by_side(arrays, axis, dim, along):
    both = jnp.concatenate(arrays, axis=along)
    out, at, gathered = (lax.all_gather(both, axis, axis=dim, tiled=True), 0, [])
    for a in arrays:
        gathered.append(lax.slice_in_dim(out, at, at + a.shape[along], axis=along))
        at += a.shape[along]
    return tuple(gathered)


def from_behind(block, axis, distance):
    devices = range(lax.axis_size(axis))
    route = [(i - distance, i) for i in devices if i - distance in devices]
    return lax.ppermute(block, axis, route)


def from_everyone(shard, axis):
    size = lax.axis_size(axis)
    return lax.all_to_all(
        jnp.broadcast_to(shard[None], (size, *shard.shape)), axis, 0, 0, tiled=True
    )


def of_everyone(shard, axis):
    everything = from_everyone(shard, axis)
    return jnp.max(everything, axis=0)


def in_blocks(shard, dim, size):
    before, after = (shard.shape[:dim], shard.shape[dim + 1 :])
    return jnp.moveaxis(shard.reshape(*before, size, -1, *after), dim, 0)


def sum_at_owner(shard, axis, dim):
    size = lax.axis_size(axis)
    pieces = lax.all_to_all(in_blocks(shard, dim, size), axis, 0, 0, tiled=True)
    return jnp.sum(pieces, axis=0)


def side_by_side_2(arrays, axis, dim, along):
    widths = [math.prod(a.shape[along:]) for a in arrays]
    both = jnp.concatenate(
        [a.reshape(*a.shape[:along], w) for a, w in zip(arrays, widths)], axis=along
    )
    out = sum_at_owner(both, axis, dim)
    pieces = jnp.split(out, [sum(widths[:k]) for k in range(1, len(widths))], axis=along)
    return tuple((b.reshape(*out.shape[:along], *a.shape[along:]) for a, b in zip(arrays, pieces)))


def summed_on_arrival(shard, axis, dim):
    pieces = in_blocks(shard, dim, lax.axis_size(axis))
    arrived = lax.all_to_all(pieces, axis, split_axis=0, concat_axis=0, tiled=True)
    return arrived.astype(jnp.float32).sum(axis=0)


def sent_together(arrays, axis, dim, along):
    both = jnp.concatenate(arrays, axis=along)
    out, at, gathered = (summed_on_arrival(both, axis, dim), 0, [])
    for a in arrays:
        gathered.append(lax.slice_in_dim(out, at, at + a.shape[along], axis=along))
        at += a.shape[along]
    return tuple(gathered)


def attend_tile(
    queries, window_keys, window_values, key_live, text_keys, text_values, text_live, score_scale
):
    near_scores = (
        jnp.einsum("qhd,khd->hqk", queries, window_keys, preferred_element_type=jnp.float32)
        * score_scale
    )
    near_scores = jnp.where(key_live[None, None, :], near_scores, NEG_FILL)
    text_scores = (
        jnp.einsum("qhd,khd->hqk", queries, text_keys, preferred_element_type=jnp.float32)
        * score_scale
    )
    text_scores = jnp.where(text_live[None, None, :], text_scores, NEG_FILL)
    row_peak = jnp.maximum(jnp.max(near_scores, axis=-1), jnp.max(text_scores, axis=-1))
    near_weights = jnp.exp(near_scores - row_peak[..., None])
    text_weights = jnp.exp(text_scores - row_peak[..., None])
    weight_sum = jnp.sum(near_weights, axis=-1) + jnp.sum(text_weights, axis=-1)
    weighted = jnp.einsum(
        "hqk,khd->hqd",
        near_weights.astype(jnp.bfloat16),
        window_values,
        preferred_element_type=jnp.float32,
    )
    weighted = weighted + jnp.einsum(
        "hqk,khd->hqd",
        text_weights.astype(jnp.bfloat16),
        text_values,
        preferred_element_type=jnp.float32,
    )
    result = weighted / weight_sum[..., None]
    return jnp.transpose(result, (1, 0, 2)).reshape(queries.shape[0], -1).astype(jnp.bfloat16)


def per_device(
    video_q,
    video_k,
    video_v,
    text_q,
    text_k,
    text_v,
    video_proj,
    text_proj,
    window_mask,
    text_length,
):
    row_count, feat_width = video_q.shape
    head_count = feat_width // HD
    tile_count = row_count // TILE_TOK
    text_local = text_k.shape[0]
    across = lax.axis_size("tile") // DH
    score_scale = 1.0 / math.sqrt(HD)
    all_queries, all_keys, all_values = side_by_side((text_q, text_k, text_v), "tile", 0, 1)
    text_count = all_queries.shape[0]
    text_limit = text_length[0]
    text_live = jnp.arange(text_count, dtype=jnp.int32) < text_limit
    own_block = jnp.stack([video_k, video_v]).reshape(2, GT, BH, BW, TILE_TOK, feat_width)
    padded = own_block
    for axis_dim, stride in ((3, 1), (2, across)):
        extent = padded.shape[axis_dim]
        from_below = from_behind(padded, "tile", stride)
        from_above = from_behind(padded, "tile", -stride)
        padded = jnp.concatenate([from_below, padded, from_above], axis=axis_dim)
    tiled_queries = video_q.reshape(tile_count, TILE_TOK, head_count, HD)
    text_keys = all_keys.reshape(text_count, head_count, HD)
    text_values = all_values.reshape(text_count, head_count, HD)
    results = []
    for local_tile in range(tile_count):
        tile_frame = local_tile // (BH * BW)
        tile_row = local_tile // BW % BH
        tile_col = local_tile % BW
        window = padded.reshape(2, GT * 9 * TILE_TOK, head_count, HD)
        pieces = []
        for abs_frame in range(GT):
            frame_gap = abs_frame - tile_frame + 1
            pieces.append(window_mask[local_tile, 9 * frame_gap : 9 * frame_gap + 9])
        key_live = jnp.repeat(jnp.concatenate(pieces) > 0, TILE_TOK)
        results.append(
            attend_tile(
                tiled_queries[local_tile],
                window[0],
                window[1],
                key_live,
                text_keys,
                text_values,
                text_live,
                score_scale,
            )
        )
    video_attn = jnp.concatenate(results, axis=0)
    first_row = lax.axis_index("tile") * text_local
    own_live = first_row + jnp.arange(text_local, dtype=jnp.int32) < text_limit
    text_queries = all_queries.reshape(text_count, head_count, HD)
    near_scores = (
        jnp.einsum(
            "qhd,khd->hqk",
            text_queries,
            video_k.reshape(row_count, head_count, HD),
            preferred_element_type=jnp.float32,
        )
        * score_scale
    )
    own_scores = (
        jnp.einsum(
            "qhd,khd->hqk",
            text_queries,
            text_k.reshape(text_local, head_count, HD),
            preferred_element_type=jnp.float32,
        )
        * score_scale
    )
    own_scores = jnp.where(own_live[None, None, :], own_scores, NEG_FILL)
    row_peak = jnp.maximum(jnp.max(near_scores, axis=-1), jnp.max(own_scores, axis=-1))
    near_weights = jnp.exp(near_scores - row_peak[..., None])
    own_weights = jnp.exp(own_scores - row_peak[..., None])
    weight_sum = jnp.sum(near_weights, axis=-1) + jnp.sum(own_weights, axis=-1)
    weighted = jnp.einsum(
        "hqk,khd->hqd",
        near_weights,
        video_v.reshape(row_count, head_count, HD).astype(jnp.float32),
        precision=lax.Precision.HIGHEST,
    )
    weighted = weighted + jnp.einsum(
        "hqk,khd->hqd",
        own_weights,
        text_v.reshape(text_local, head_count, HD).astype(jnp.float32),
        precision=lax.Precision.HIGHEST,
    )
    global_peak = of_everyone(row_peak, "tile")
    factor = jnp.exp(row_peak - global_peak)
    own_sum, own_acc = side_by_side_2(
        (weight_sum * factor, weighted * factor[..., None]), "tile", 1, 2
    )
    own_rows = own_acc / own_sum[..., None]
    text_attn = (
        jnp.transpose(own_rows, (1, 0, 2)).reshape(text_local, feat_width).astype(jnp.bfloat16)
    )
    video_part = jnp.dot(video_attn, video_proj, preferred_element_type=jnp.float32)
    text_part = jnp.dot(text_attn, text_proj, preferred_element_type=jnp.float32)
    video_sum, text_sum = sent_together(
        (video_part.astype(jnp.bfloat16), text_part.astype(jnp.bfloat16)), "head", 1, 0
    )
    return (video_sum.astype(jnp.bfloat16), text_sum.astype(jnp.bfloat16))


def solution(mesh):
    placed = (
        P("tile", "head"),
        P("tile", "head"),
        P("tile", "head"),
        P("tile", "head"),
        P("tile", "head"),
        P("tile", "head"),
        P("head", None),
        P("head", None),
        P("tile", None),
        P(),
    )
    return jax.shard_map(
        per_device,
        mesh=mesh,
        in_specs=placed,
        out_specs=(P("tile", "head"), P("tile", "head")),
        check_vma=False,
    )
```

profile of v0, /device:TPU:32, one launch (start us, length us, event | category | flops | bytes accessed | tf_op | source)
XLA Modules:
  0.0 289.7 jit_solution(8929491650253092196)
XLA Ops:
  0.7 2.2 pad_maximum_fusion.3
  2.9 1.3 collective-permute-start.1
  4.2 3.9 %collective-permute-start = (bf16[2,2,1,1,256,384]{5,4,3,2,1,0:T(8,128)(2,1)}, bf16[2,2,1,1,256,384]{5,4,3,2,1,0:T(8,128)(2,1)}, u32[]{:S(2)}, u32[]{:S(2)}) collective-permute-start(bf16[2,2,1,1,256,384]{5,4,3,2,1,0:T(8,128)(2,1)} %pad_maximum_fusion.3), channel_id=1, source_target_pairs={{0,8},{8,16},{16,24},{24,32},{32,40},{40,48},{48,56},{56,64},{64,7... | collective-permute-start | bytes 2359304 | tf_op jit(solution)/shard_map/ppermute | solution.py:31
  9.5 54.8 %all_gather.3 = bf16[256,1152]{1,0:T(8,128)(2,1)S(1)} all-gather(bf16[8,1152]{1,0:T(8,128)(2,1)S(1)} %pad_maximum_fusion.4), channel_id=1, replica_groups=mesh['tile'=32,'head'=8] {'tile'}, dimensions={0}, use_global_device_ids=true | all-gather | bytes 608256 | tf_op jit(solution)/shard_map/all_gather | solution.py:21
  65.1 1.9 copy.159
  68.1 2.6 fusion.80
  71.4 4.8 %all-to-all-start = ((f32[32,3,256]{2,1,0:T(4,128)}), f32[32,3,256]{2,1,0:T(4,128)}, u32[]{:S(2)}, u32[]{:S(2)}) async-start(f32[32,3,256]{2,1,0:T(4,128)} %broadcast_in_dim.85), calls=%async_computation | async-start | bytes 262144 | tf_op jit(solution)/shard_map/all_to_all | solution.py:36
  77.4 3.1 %pad_maximum_fusion.2 = bf16[2,2,1,3,256,384]{5,4,3,2,1,0:T(8,128)(2,1)} fusion(bf16[2,2,1,1,256,384]{5,4,3,2,1,0:T(8,128)(2,1)} %collective-permute-done.1, bf16[1,2,1,1,256,384]{5,4,3,2,1,0:T(8,128)(2,1)S(1)} %bitcast.135, bf16[1,2,1,1,256,384]{5,4,3,2,1,0:T(8,128)(2,1)S(1)} %bitcast.131, bf16[2,2,1,1,256,384]{5,4,3,2,1,0:T(8,128)(2,1)} %collective-permute-done), kind=kLoop, calls=%fused_computation.25 | loop fusion | flops 3538944 | bytes 4718592 | tf_op jit(solution)/shard_map/concatenate | solution.py:143
  80.5 1.3 collective-permute-start.3
  81.8 6.0 %collective-permute-start.2 = (bf16[2,2,1,3,256,384]{5,4,3,2,1,0:T(8,128)(2,1)}, bf16[2,2,1,3,256,384]{5,4,3,2,1,0:T(8,128)(2,1)}, u32[]{:S(2)}, u32[]{:S(2)}) collective-permute-start(bf16[2,2,1,3,256,384]{5,4,3,2,1,0:T(8,128)(2,1)} %pad_maximum_fusion.2), channel_id=1, source_target_pairs={{0,64},{8,72},{16,80},{24,88},{32,96},{40,104},{48,112},{56,120},{... | collective-permute-start | bytes 7077896 | tf_op jit(solution)/shard_map/ppermute | solution.py:31
  89.5 1.8 fusion.17
  93.7 1.4 copy.166
  95.2 2.4 fusion.24
  98.9 10.0 %all-to-all-start.1 = ((f32[32,3,8,129]{3,2,1,0:T(8,128)}), f32[32,3,8,129]{3,2,1,0:T(8,128)}, u32[]{:S(2)}, u32[]{:S(2)}) async-start(f32[32,3,8,129]{3,2,1,0:T(8,128)} %maximum_bitcast_fusion), calls=%async_computation.1 | async-start | bytes 1572864 | tf_op jit(solution)/shard_map/all_to_all | solution.py:53
  113.2 1.9 fusion.83
  115.1 35.6 %all-to-all-done.1 = f32[32,3,8,129]{3,2,1,0:T(8,128)} async-done(((f32[32,3,8,129]{3,2,1,0:T(8,128)}), f32[32,3,8,129]{3,2,1,0:T(8,128)}, u32[]{:S(2)}, u32[]{:S(2)}) %all-to-all-start.1) | async-done | bytes 396320 | tf_op jit(solution)/shard_map/all_to_all | solution.py:53
  150.7 1.8 reduce_sum.78
  153.3 2.8 convolution_convert_fusion.1
  156.1 4.0 %pad_maximum_fusion = bf16[2,2,3,3,256,384]{5,4,3,2,1,0:T(8,128)(2,1)S(1)} fusion(bf16[2,2,1,3,256,384]{5,4,3,2,1,0:T(8,128)(2,1)} %collective-permute-done.3, bf16[2,2,1,1,256,384]{5,4,3,2,1,0:T(8,128)(2,1)} %collective-permute-done.1, bf16[1,2,1,1,256,384]{5,4,3,2,1,0:T(8,128)(2,1)} %bitcast.134, bf16[1,2,1,1,256,384]{5,4,3,2,1,0:T(8,128)(2,1)S(1)} %bitcast.132, ...), kind=kLoop, calls=%fused_computation.12 | loop fusion | flops 17694720 | bytes 14155776 | tf_op jit(solution)/shard_map/concatenate | solution.py:143
  160.1 3.7 %fusion.77 = (bf16[1,2,3,3,256,384]{5,4,3,2,1,0:T(8,128)(2,1)}, bf16[1,2,3,3,256,384]{5,4,3,2,1,0:T(8,128)(2,1)}) fusion(bf16[2,2,3,3,256,384]{5,4,3,2,1,0:T(8,128)(2,1)S(1)} %pad_maximum_fusion), kind=kLoop, calls=%fused_computation.93 | loop fusion | bytes 14155776 | tf_op jit(solution)/shard_map/slice | solution.py:162
  163.9 10.1 %squeeze.31 = bf16[4608,3,128]{2,1,0:T(4,128)(2,1)} reshape(bf16[1,2,3,3,256,384]{5,4,3,2,1,0:T(8,128)(2,1)} %get-tuple-element.5) | data formatting | bytes 7077888 | tf_op jit(solution)/shard_map/squeeze | solution.py:161
  174.0 9.5 %bitcast_reduce_fusion = (f32[3,256]{1,0:T(4,128)S(1)}, f32[3,4608,256]{2,1,0:T(8,128)}) fusion(pred[4608]{0:T(1024)(128)(4,1)S(1)} %copy-done.16, bf16[256,3,128]{0,2,1:T(8,128)(2,1)S(1)} %bitcast.147, bf16[4608,3,128]{2,1,0:T(4,128)(2,1)} %squeeze.31), kind=kOutput, calls=%fused_computation.1 | convolution fusion | flops 916585728 | bytes 17899008 | tf_op jit(solution)/shard_map/qhd,khd->hqk/dot_general | solution.py:86
  184.5 8.0 %bitcast_reduce_fusion.1 = (f32[3,256]{1,0:T(4,128)S(1)}, f32[3,4608,256]{2,1,0:T(8,128)}) fusion(pred[4608]{0:T(1024)(128)(4,1)S(1)} %broadcast_in_dim.75, bf16[256,3,128]{0,2,1:T(8,128)(2,1)S(1)} %bitcast.145, bf16[4608,3,128]{2,1,0:T(4,128)(2,1)S(1)} %copy-done.4), kind=kOutput, calls=%fused_computation.4 | convolution fusion | flops 916585728 | bytes 17899008 | tf_op jit(solution)/shard_map/qhd,khd->hqk/dot_general | solution.py:86
  194.2 10.0 %squeeze.34 = bf16[4608,3,128]{2,1,0:T(4,128)(2,1)} reshape(bf16[1,2,3,3,256,384]{5,4,3,2,1,0:T(8,128)(2,1)} %get-tuple-element.4) | data formatting | bytes 7077888 | tf_op jit(solution)/shard_map/squeeze | solution.py:162
  204.3 8.0 %copy.147 = bf16[4608,3,128]{0,2,1:T(8,128)(2,1)} copy(bf16[4608,3,128]{2,1,0:T(4,128)(2,1)} %squeeze.34) | data formatting | bytes 7077888 | tf_op jit(solution)/shard_map/squeeze | solution.py:162
  212.3 7.2 %fusion.4 = f32[3,256]{1,0:T(4,128)S(1)} fusion(f32[3,4608,256]{2,1,0:T(8,128)} %get-tuple-element.20, f32[3,256]{1,0:T(4,128)S(1)} %max.38, pred[4608]{0:T(1024)(128)(4,1)S(1)} %copy-done.17), kind=kLoop, calls=%fused_computation.10 | loop fusion | flops 14155008 | bytes 14166528 | tf_op jit(solution)/shard_map/reduce_sum | solution.py:98
  219.6 8.0 %fusion.2 = f32[3,256]{1,0:T(4,128)S(1)} fusion(f32[3,4608,256]{2,1,0:T(8,128)} %get-tuple-element.24, f32[3,256]{1,0:T(4,128)S(1)} %max.37, pred[4608]{0:T(1024)(128)(4,1)S(1)} %broadcast_in_dim.75), kind=kLoop, calls=%fused_computation.8 | loop fusion | flops 14155008 | bytes 14166528 | tf_op jit(solution)/shard_map/reduce_sum | solution.py:98
  227.7 8.6 %fusion.41 = bf16[256,3,128]{0,2,1:T(8,128)(2,1)S(1)} fusion(f32[3,256,128]{1,2,0:T(8,128)S(1)} %fusion.55, bf16[4608,3,128]{0,2,1:T(8,128)(2,1)S(1)} %copy-done.5, f32[3,4608,256]{2,1,0:T(8,128)} %get-tuple-element.20, f32[3,256]{1,0:T(4,128)S(1)} %max.38, pred[4608]{0:T(1024)(128)(4,1)S(1)} %copy-done.17, f32[256,3]{0,1:T(4,128)S(1)} %add_bitcast_fusion), kind=kOutput, calls=%fused_computation.46 | convolution fusion | flops 920420352 | bytes 18295296 | tf_op jit(solution)/shard_map/hqk,khd->hqd/dot_general | solution.py:99
  236.3 4.0 %fusion.47 = bf16[256,3,128]{0,2,1:T(8,128)(2,1)S(1)} fusion(f32[3,256,128]{1,2,0:T(8,128)S(1)} %copy-done.13, bf16[4608,3,128]{0,2,1:T(8,128)(2,1)S(1)} %copy-done.5, f32[3,4608,256]{2,1,0:T(8,128)S(1)} %bitcast.127, f32[3,256]{1,0:T(4,128)S(1)} %max.37, pred[4608]{0:T(1024)(128)(4,1)S(1)} %broadcast_in_dim.75, f32[256,3]{0,1:T(4,128)S(1)} %add_bitcast_fusion.1), kind=kOutput, calls=%fused_computation.48 | convolution fusion | flops 920420352 | bytes 18295296 | tf_op jit(solution)/shard_map/hqk,khd->hqd/dot_general | solution.py:99
  240.4 1.8 convolution_convert_fusion
  242.8 43.0 %all_to_all.15 = bf16[8,520,384]{2,1,0:T(8,128)(2,1)} all-to-all(bf16[8,520,384]{2,1,0:T(8,128)(2,1)S(1)} %bitcast.129), channel_id=1, replica_groups=mesh['tile'=32,'head'=8] {'head'}, dimensions={0} | all-to-all | bytes 6389760 | tf_op jit(solution)/shard_map/all_to_all | solution.py:69
  285.8 2.5 reduce
  (98 shorter events, 19.7 us)
Async XLA Ops:
  0.6 239.8 %copy-start = (bf16[384,3072]{1,0:T(8,128)(2,1)S(1)}, bf16[384,3072]{1,0:T(8,128)(2,1)}, u32[]{:S(2)}) copy-start(bf16[384,3072]{1,0:T(8,128)(2,1)} %param.16) | copy-start | bytes 7077892
  0.6 76.8 %copy-start.3 = (bf16[512,384]{1,0:T(8,128)(2,1)S(1)}, bf16[512,384]{1,0:T(8,128)(2,1)}, u32[]{:S(2)}) copy-start(bf16[512,384]{1,0:T(8,128)(2,1)} %param.12) | copy-start | bytes 1179652
  0.7 76.8 %copy-start.2 = (bf16[512,384]{1,0:T(8,128)(2,1)S(1)}, bf16[512,384]{1,0:T(8,128)(2,1)}, u32[]{:S(2)}) copy-start(bf16[512,384]{1,0:T(8,128)(2,1)} %param.11) | copy-start | bytes 1179652
  0.7 75.5 %copy-start.15 = (bf16[8,384]{1,0:T(8,128)(2,1)S(1)}, bf16[8,384]{1,0:T(8,128)(2,1)}, u32[]{:S(2)}) copy-start(bf16[8,384]{1,0:T(8,128)(2,1)} %param.15) | copy-start | bytes 18436
  2.9 74.5 %collective-permute-start.1 = (bf16[2,2,1,1,256,384]{5,4,3,2,1,0:T(8,128)(2,1)}, bf16[2,2,1,1,256,384]{5,4,3,2,1,0:T(8,128)(2,1)}, u32[]{:S(2)}, u32[]{:S(2)}) collective-permute-start(bf16[2,2,1,1,256,384]{5,4,3,2,1,0:T(8,128)(2,1)} %pad_maximum_fusion.3), channel_id=1, source_target_pairs={{8,0},{16,8},{24,16},{32,24},{40,32},{48,40},{56,48},{64,56},{72,6... | collective-permute-start | bytes 2359304 | tf_op jit(solution)/shard_map/ppermute | solution.py:31
  4.2 73.2 %collective-permute-start = (bf16[2,2,1,1,256,384]{5,4,3,2,1,0:T(8,128)(2,1)}, bf16[2,2,1,1,256,384]{5,4,3,2,1,0:T(8,128)(2,1)}, u32[]{:S(2)}, u32[]{:S(2)}) collective-permute-start(bf16[2,2,1,1,256,384]{5,4,3,2,1,0:T(8,128)(2,1)} %pad_maximum_fusion.3), channel_id=1, source_target_pairs={{0,8},{8,16},{16,24},{24,32},{32,40},{40,48},{48,56},{56,64},{64,7... | collective-permute-start | bytes 2359304 | tf_op jit(solution)/shard_map/ppermute | solution.py:31
  65.1 22.7 %copy-start.21 = (s32[2,27]{1,0:T(2,128)S(1)}, s32[2,27]{1,0:T(2,128)}, u32[]{:S(2)}) copy-start(s32[2,27]{1,0:T(2,128)} %param.18) | copy-start | bytes 652
  71.4 20.0 %all-to-all-start = ((f32[32,3,256]{2,1,0:T(4,128)}), f32[32,3,256]{2,1,0:T(4,128)}, u32[]{:S(2)}, u32[]{:S(2)}) async-start(f32[32,3,256]{2,1,0:T(4,128)} %broadcast_in_dim.85), calls=%async_computation | async-start | bytes 262144 | tf_op jit(solution)/shard_map/all_to_all | solution.py:36
  80.5 75.6 %collective-permute-start.3 = (bf16[2,2,1,3,256,384]{5,4,3,2,1,0:T(8,128)(2,1)}, bf16[2,2,1,3,256,384]{5,4,3,2,1,0:T(8,128)(2,1)}, u32[]{:S(2)}, u32[]{:S(2)}) collective-permute-start(bf16[2,2,1,3,256,384]{5,4,3,2,1,0:T(8,128)(2,1)} %pad_maximum_fusion.2), channel_id=1, source_target_pairs={{64,0},{72,8},{80,16},{88,24},{96,32},{104,40},{112,48},{120,56},{... | collective-permute-start | bytes 7077896 | tf_op jit(solution)/shard_map/ppermute | solution.py:31
  81.8 74.3 %collective-permute-start.2 = (bf16[2,2,1,3,256,384]{5,4,3,2,1,0:T(8,128)(2,1)}, bf16[2,2,1,3,256,384]{5,4,3,2,1,0:T(8,128)(2,1)}, u32[]{:S(2)}, u32[]{:S(2)}) collective-permute-start(bf16[2,2,1,3,256,384]{5,4,3,2,1,0:T(8,128)(2,1)} %pad_maximum_fusion.2), channel_id=1, source_target_pairs={{0,64},{8,72},{16,80},{24,88},{32,96},{40,104},{48,112},{56,120},{... | collective-permute-start | bytes 7077896 | tf_op jit(solution)/shard_map/ppermute | solution.py:31
  97.6 13.3 %copy-start.9 = (bf16[256,384]{1,0:T(8,128)(2,1)S(1)}, bf16[256,384]{1,0:T(8,128)(2,1)}, u32[]{:S(2)}) copy-start(bf16[256,384]{1,0:T(8,128)(2,1)} %get-tuple-element.6) | copy-start | bytes 589828
  97.6 13.5 %copy-start.8 = (bf16[256,384]{1,0:T(8,128)(2,1)S(1)}, bf16[256,384]{1,0:T(8,128)(2,1)}, u32[]{:S(2)}) copy-start(bf16[256,384]{1,0:T(8,128)(2,1)} %get-tuple-element.7) | copy-start | bytes 589828
  98.9 51.9 %all-to-all-start.1 = ((f32[32,3,8,129]{3,2,1,0:T(8,128)}), f32[32,3,8,129]{3,2,1,0:T(8,128)}, u32[]{:S(2)}, u32[]{:S(2)}) async-start(f32[32,3,8,129]{3,2,1,0:T(8,128)} %maximum_bitcast_fusion), calls=%async_computation.1 | async-start | bytes 1572864 | tf_op jit(solution)/shard_map/all_to_all | solution.py:53
  110.9 2.3 copy-start.11
  111.1 2.1 copy-start.7
  163.8 10.1 %copy-start.12 = (bf16[256,384]{0,1:T(8,128)(2,1)S(1)}, bf16[256,384]{0,1:T(8,128)(2,1)}, u32[]{:S(2)}) copy-start(bf16[256,384]{0,1:T(8,128)(2,1)} %copy-done.11) | copy-start | bytes 589828
  163.9 10.1 %copy-start.16 = (pred[4608]{0:T(1024)(128)(4,1)S(1)}, pred[4608]{0:T(1024)(128)(4,1)}, u32[]{:S(2)}) copy-start(pred[4608]{0:T(1024)(128)(4,1)} %broadcast_in_dim.81) | copy-start | bytes 13828
  173.9 9.5 %copy-start.1 = (f32[3,256,256]{1,2,0:T(8,128)S(1)}, f32[3,256,256]{1,2,0:T(8,128)}, u32[]{:S(2)}) copy-start(f32[3,256,256]{1,2,0:T(8,128)} %get-tuple-element.22) | copy-start | bytes 2359300
  173.9 10.3 %copy-start.6 = (bf16[256,384]{0,1:T(8,128)(2,1)S(1)}, bf16[256,384]{0,1:T(8,128)(2,1)}, u32[]{:S(2)}) copy-start(bf16[256,384]{0,1:T(8,128)(2,1)} %copy.148) | copy-start | bytes 589828
  173.9 10.5 %copy-start.4 = (bf16[4608,3,128]{2,1,0:T(4,128)(2,1)S(1)}, bf16[4608,3,128]{2,1,0:T(4,128)(2,1)}, u32[]{:S(2)}) copy-start(bf16[4608,3,128]{2,1,0:T(4,128)(2,1)} %squeeze.31) | copy-start | bytes 10616836
  174.0 10.5 %copy-start.10 = (bf16[256,384]{0,1:T(8,128)(2,1)S(1)}, bf16[256,384]{0,1:T(8,128)(2,1)}, u32[]{:S(2)}) copy-start(bf16[256,384]{0,1:T(8,128)(2,1)} %copy.184) | copy-start | bytes 589828
  184.5 8.0 %copy-start.18 = (f32[3,256]{1,0:T(4,128)S(1)}, f32[3,256]{1,0:T(4,128)}, u32[]{:S(2)}) copy-start(f32[3,256]{1,0:T(4,128)} %get-tuple-element.25) | copy-start | bytes 9220
  204.3 8.0 %copy-start.17 = (pred[4608]{0:T(1024)(128)(4,1)S(1)}, pred[4608]{0:T(1024)(128)(4,1)}, u32[]{:S(2)}) copy-start(pred[4608]{0:T(1024)(128)(4,1)} %broadcast_in_dim.81) | copy-start | bytes 13828
  219.5 8.1 %copy-start.19 = (f32[3,256]{1,0:T(4,128)S(1)}, f32[3,256]{1,0:T(4,128)}, u32[]{:S(2)}) copy-start(f32[3,256]{1,0:T(4,128)} %fusion.53) | copy-start | bytes 9220
  219.5 8.1 %copy-start.20 = (f32[3,256]{1,0:T(4,128)S(1)}, f32[3,256]{1,0:T(4,128)}, u32[]{:S(2)}) copy-start(f32[3,256]{1,0:T(4,128)} %fusion.51) | copy-start | bytes 9220
  219.5 8.1 %copy-start.5 = (bf16[4608,3,128]{0,2,1:T(8,128)(2,1)S(1)}, bf16[4608,3,128]{0,2,1:T(8,128)(2,1)}, u32[]{:S(2)}) copy-start(bf16[4608,3,128]{0,2,1:T(8,128)(2,1)} %copy.147) | copy-start | bytes 10616836
  219.5 16.7 %slice-start = ((s8[14155776]{0:T(1024)(128)(4,1)}), s8[4194304]{0:T(1024)(128)(4,1)S(1)}, s32[]{:S(2)}) async-start(s8[14155776]{0:T(1024)(128)(4,1)} %bitcast.126), calls=%async_computation.3 | async-start | bytes 8388608
  219.5 16.7 %slice-start.1 = ((s8[14155776]{0:T(1024)(128)(4,1)}), s8[4194304]{0:T(1024)(128)(4,1)S(1)}, s32[]{:S(2)}) async-start(s8[14155776]{0:T(1024)(128)(4,1)} %bitcast.126), calls=%async_computation.4 | async-start | bytes 8388608
  227.6 8.7 %slice-start.2 = ((s8[14155776]{0:T(1024)(128)(4,1)}), s8[4194304]{0:T(1024)(128)(4,1)S(1)}, s32[]{:S(2)}) async-start(s8[14155776]{0:T(1024)(128)(4,1)} %bitcast.126), calls=%async_computation.5 | async-start | bytes 8388608
  227.6 8.7 %slice-start.3 = ((s8[14155776]{0:T(1024)(128)(4,1)}), s8[1572864]{0:T(1024)(128)(4,1)S(1)}, s32[]{:S(2)}) async-start(s8[14155776]{0:T(1024)(128)(4,1)} %bitcast.126), calls=%async_computation.6 | async-start | bytes 3145728
  227.6 8.7 %copy-start.13 = (f32[3,256,128]{1,2,0:T(8,128)S(1)}, f32[3,256,128]{1,2,0:T(8,128)}, u32[]{:S(2)}) copy-start(f32[3,256,128]{1,2,0:T(8,128)} %fusion.57) | copy-start | bytes 1179652
  240.4 1.9 copy-start.14
where the time goes:
time: 292 us; the launch traced here: 290 us
  blocking collectives  97.8 us (33%)
  matrix products  46.3 us (16%)
  local copies, waits for them, and re-layouts  44.3 us (15%)
  other arithmetic  36.7 us (13%)
  waiting for transfers between devices  35.6 us (12%)
  starting transfers between devices  27.2 us (9%)
    all_gather x1, blocking collectives, side_by_side(): lax.all_gather(both, axis, axis=dim, tiled=True)  54.8 us
    all_to_all x1, blocking collectives, summed_on_arrival(): lax.all_to_all(pieces, axis, split_axis=0, concat_axis=0, tiled=True)  43 us
    all_to_all x1, waiting for transfers between devices, sum_at_owner(): pieces = lax.all_to_all(in_blocks(shard, dim, size), axis, 0, 0, tiled=True)  35.6 us
    squeeze x2, local copies, waits for them, and re-layouts, per_device(): window[1]  18 us
    dot_general x2, matrix products, attend_tile(): jnp.einsum('qhd,khd->hqk', queries, window_keys, preferred_element_type=j...  17.5 us
    reduce_sum x4, other arithmetic, attend_tile(): weight_sum = jnp.sum(near_weights, axis=-1) + jnp.sum(text_weights, axis=-1)  16.7 us
    dot_general x2, matrix products, attend_tile(): jnp.einsum('hqk,khd->hqd', near_weights.astype(jnp.bfloat16), window_valu...  12.6 us
    ppermute x4, starting transfers between devices, from_behind(): return lax.ppermute(block, axis, route)  12.5 us
  transfers between devices with their start and end apart: 6, of which 1 were waited for; matrix products, arithmetic and copies ran while one was open for 12% of the time, Pallas kernels for 0%

commit v1 on v0

v1 whole, which is shorter than its diff:
```python
import functools
import math

import jax
import jax.numpy as jnp
from jax import lax
from jax.experimental import pallas as pl
from jax.experimental.pallas import tpu as pltpu
from jax.sharding import PartitionSpec as P

HD = 128
TT = 256
NH = 3
W = NH * HD
TEXT = 256
TL = 8
ROWS = 2 * TT
SCALE = math.log2(math.e) / math.sqrt(HD)
BIG = 1e30
F32 = jnp.float32
BF16 = jnp.bfloat16

ANY = pl.BlockSpec(memory_space=pl.ANY)
SM = pl.BlockSpec(memory_space=pltpu.SMEM)
VM = pl.BlockSpec(memory_space=pltpu.VMEM)


def params(mib):
    return pltpu.CompilerParams(vmem_limit_bytes=mib * 2**20)


def cost(flops, nbytes, exps=0):
    return pl.CostEstimate(flops=flops, bytes_accessed=nbytes, transcendentals=exps)


def rows_on(x, d):
    return lax.ppermute(x, "tile", [(i, ((i // 8 + d) % 4) * 8 + i % 8) for i in range(32)])


def over_chip(x):
    return lax.ppermute(
        x, "tile", [(i, (i // 8) * 8 + (i % 8 + (1 if i % 2 else -1)) % 8) for i in range(32)]
    )


def other_core(x):
    return lax.ppermute(x, "tile", [(i, i ^ 1) for i in range(32)])


def x_on(x, d):
    return lax.ppermute(x, "head", [(i, (i // 4) * 4 + (i + d) % 4) for i in range(8)])


def z_pair(x):
    return lax.ppermute(x, "head", [(i, i ^ 4) for i in range(8)])


def fold(x, op):
    r = x[:, :HD]
    for i in range(1, x.shape[1] // HD):
        r = op(r, x[:, i * HD : (i + 1) * HD])
    return r


def scores(q, k):
    return lax.dot_general(q, k, (((1,), (1,)), ((), ())), preferred_element_type=F32)


def spread(col):
    return jnp.broadcast_to(col, (col.shape[0], HD))


def bias_of(wm, tile, frame, row, col):
    live = wm[tile, 9 * (frame - tile + 1) + 3 * row + col]
    return jnp.where(live > 0, 0.0, -BIG).astype(F32)


def early_kernel(
    wm, tlen, core, q_ref, tk_ref, tv_ref, b0, b1, b2, b3, b4, b5,
    acc_ref, m_ref, l_ref, kbuf, s_s, mx_s, sem,
):
    blocks = (b0, b1, b2, b3, b4, b5)
    nb = len(blocks)
    for b in range(nb):
        pltpu.make_async_copy(blocks[b], kbuf.at[b], sem.at[b]).start()
    lane = lax.broadcasted_iota(jnp.int32, (1, TEXT), 1)
    tbias = jnp.where(lane < tlen[0], 0.0, -BIG)
    pcol = jnp.where(core[0] == 0, 2, 0)
    colof = (1, 1, 1, pcol, pcol, pcol)
    rowof = (1, 0, 2, 1, 0, 2)

    def hs(h):
        return pl.ds(h * HD, HD)

    def p1_text(h, w):
        for t in range(2):
            s = scores(q_ref[pl.ds(t * TT, TT), hs(h)], tk_ref[:, hs(h)]) * SCALE + tbias
            s_s[w, t, nb, :, :TEXT] = s
            mx_s[w, t] = fold(s, jnp.maximum)

    def p1(h, w, b):
        k = kbuf[b, :ROWS, hs(h)]
        for t in range(2):
            s = scores(q_ref[pl.ds(t * TT, TT), hs(h)], k)
            mx = mx_s[w, t]
            for f in range(2):
                sf = s[:, f * TT : (f + 1) * TT] * SCALE + bias_of(wm, t, f, rowof[b], colof[b])
                s_s[w, t, b, :, f * TT : (f + 1) * TT] = sf
                mx = jnp.maximum(mx, fold(sf, jnp.maximum))
            mx_s[w, t] = mx

    def top(h, w):
        for t in range(2):
            m_ref[pl.ds(t * TT, TT), hs(h)] = spread(jnp.max(mx_s[w, t], axis=1, keepdims=True))

    def weigh(s, m):
        return jnp.concatenate(
            [jnp.exp2(s[:, i * HD : (i + 1) * HD] - m) for i in range(s.shape[1] // HD)], axis=1
        )

    def p2_text(h, w):
        for t in range(2):
            rs = pl.ds(t * TT, TT)
            p = weigh(s_s[w, t, nb, :, :TEXT], m_ref[rs, hs(h)])
            l_ref[rs, hs(h)] = fold(p, jnp.add)
            acc_ref[rs, hs(h)] = jnp.dot(
                p.astype(BF16), tv_ref[:, hs(h)], preferred_element_type=F32
            )

    def p2(h, w, b):
        v = kbuf[b, ROWS:, hs(h)]
        for t in range(2):
            rs = pl.ds(t * TT, TT)
            p = weigh(s_s[w, t, b], m_ref[rs, hs(h)])
            l_ref[rs, hs(h)] += fold(p, jnp.add)
            acc_ref[rs, hs(h)] += jnp.dot(p.astype(BF16), v, preferred_element_type=F32)

    p1_text(0, 0)
    for b in range(nb):
        pltpu.make_async_copy(blocks[b], kbuf.at[b], sem.at[b]).wait()
        p1(0, 0, b)
    top(0, 0)
    for h in range(NH):
        w = h % 2
        p2_text(h, w)
        if h + 1 < NH:
            p1_text(h + 1, 1 - w)
        for b in range(nb):
            p2(h, w, b)
            if h + 1 < NH:
                p1(h + 1, 1 - w, b)
        if h + 1 < NH:
            top(h + 1, 1 - w)


def early(wm, tlen, core, q, tk, tv, blocks):
    nb = len(blocks)
    part = jax.ShapeDtypeStruct((ROWS, W), F32)
    return pl.pallas_call(
        early_kernel,
        out_shape=(part, part, part),
        in_specs=[SM, SM, SM, VM, VM, VM] + [ANY] * nb,
        out_specs=(VM, VM, VM),
        scratch_shapes=[
            pltpu.VMEM((nb, 2 * ROWS, W), BF16),
            pltpu.VMEM((2, 2, nb + 1, TT, ROWS), F32),
            pltpu.VMEM((2, 2, TT, HD), F32),
            pltpu.SemaphoreType.DMA((nb,)),
        ],
        compiler_params=params(44),
        cost_estimate=cost(4 * ROWS * (nb * ROWS + TEXT) * W, 8 * 2**20, ROWS * nb * ROWS * NH),
        name="early",
    )(wm, tlen, core, q, tk, tv, *blocks)


def late_kernel(wm, core, q_ref, b0, b1, b2, acc_ref, m_ref, l_ref, o_ref):
    blocks = (b0, b1, b2)
    fcol = jnp.where(core[0] == 0, 0, 2)
    rowof = (1, 0, 2)
    for t in range(2):
        rs = pl.ds(t * TT, TT)
        parts = []
        mx = None
        for b in range(3):
            s = scores(q_ref[rs, :], blocks[b][:ROWS, :])
            for f in range(2):
                sf = s[:, f * TT : (f + 1) * TT] * SCALE + bias_of(wm, t, f, rowof[b], fcol)
                parts.append(sf)
                fx = fold(sf, jnp.maximum)
                mx = fx if mx is None else jnp.maximum(mx, fx)
        mo = m_ref[rs, :]
        mn = jnp.maximum(mo, spread(jnp.max(mx, axis=1, keepdims=True)))
        al = jnp.exp2(mo - mn)
        acc = acc_ref[rs, :] * al
        tot = l_ref[rs, :] * al
        for b in range(3):
            p = jnp.concatenate(
                [
                    jnp.exp2(parts[2 * b + f][:, i * HD : (i + 1) * HD] - mn)
                    for f in range(2)
                    for i in range(2)
                ],
                axis=1,
            )
            tot += fold(p, jnp.add)
            acc += jnp.dot(p.astype(BF16), blocks[b][ROWS:, :], preferred_element_type=F32)
        o_ref[rs, :] = (acc / jnp.sum(tot, axis=1, keepdims=True)).astype(BF16)


def late(h, wm, core, q, far, far_up, far_dn, acc, m, l):
    head = pl.BlockSpec((ROWS, HD), lambda i: (0, h))
    block = pl.BlockSpec((2 * ROWS, HD), lambda i: (0, h))
    own = pl.BlockSpec((2 * ROWS, HD), lambda i: (0, 0))
    return pl.pallas_call(
        late_kernel,
        grid=(1,),
        out_shape=jax.ShapeDtypeStruct((ROWS, HD), BF16),
        in_specs=[SM, SM, head, block, own, own, head, head, head],
        out_specs=pl.BlockSpec((ROWS, HD), lambda i: (0, 0)),
        compiler_params=params(32),
        cost_estimate=cost(12 * ROWS * ROWS * HD, 2 * 2**20, 3 * ROWS * ROWS),
        name="late",
    )(wm, core, q, far, far_up, far_dn, acc, m, l)


def pieces3(x):
    hi = x.astype(BF16).astype(F32)
    mid = (x - hi).astype(BF16).astype(F32)
    return hi, mid, x - hi - mid


def text_kernel(tq_ref, kv_ref, msg_ref):
    lane = lax.broadcasted_iota(jnp.int32, (TEXT, HD), 1)
    stat = jnp.zeros((TEXT, HD), F32)
    for h in range(NH):
        hs = pl.ds(h * HD, HD)
        s = scores(tq_ref[:, hs], kv_ref[:ROWS, hs]) * SCALE
        m = jnp.max(fold(s, jnp.maximum), axis=1, keepdims=True)
        p = jnp.exp2(s - m)
        tot = jnp.sum(fold(p, jnp.add), axis=1, keepdims=True)
        acc = jnp.dot(p.astype(BF16), kv_ref[ROWS:, hs], preferred_element_type=F32)
        msg_ref[:, hs] = (acc / tot).astype(BF16)
        for j, piece in enumerate(pieces3(m + jnp.log2(tot))):
            stat = jnp.where(lane == 8 * j + h, spread(piece), stat)
    msg_ref[:, W:] = stat.astype(BF16)


def text_part(tq, kv):
    return pl.pallas_call(
        text_kernel,
        out_shape=jax.ShapeDtypeStruct((TEXT, W + HD), BF16),
        in_specs=[VM, VM],
        out_specs=VM,
        compiler_params=params(24),
        cost_estimate=cost(4 * TEXT * ROWS * W, 2 * 2**20, TEXT * ROWS * NH),
        name="text_part",
    )(tq, kv)


def merge_kernel(tlen, at, msg_ref, tq_ref, tk_ref, tv_ref, proj_ref, out_ref, flat):
    msg = msg_ref[...].astype(F32)
    stat = msg[:, W:]
    slane = lax.broadcasted_iota(jnp.int32, (TEXT, HD), 1)
    lane = lax.broadcasted_iota(jnp.int32, (1, TEXT), 1)
    tbias = jnp.where(lane < tlen[0], 0.0, -BIG)
    q = tq_ref[...]
    attn = []
    for h in range(NH):
        hs = slice(h * HD, (h + 1) * HD)
        s = scores(q[:, hs], tk_ref[:, hs]) * SCALE + tbias
        m = jnp.max(s, axis=1, keepdims=True)
        p = jnp.exp2(s - m)
        tot = jnp.sum(p, axis=1, keepdims=True)
        own = jnp.dot(p.astype(BF16), tv_ref[:, hs], preferred_element_type=F32)
        mine = (slane == h) | (slane == 8 + h) | (slane == 16 + h)
        lse = jnp.sum(jnp.where(mine, stat, 0.0), axis=1, keepdims=True)
        lse = spread(lse).reshape(TEXT // TL, TL, HD)
        peak = jnp.maximum(jnp.max(lse, axis=0), spread(m))
        wt = jnp.exp2(lse - peak[None])
        w0 = jnp.exp2(spread(m) - peak)
        num = jnp.sum(wt * msg[:, hs].reshape(TEXT // TL, TL, HD), axis=0) + w0 * own
        den = jnp.sum(wt, axis=0) + w0 * tot
        attn.append((num / den).astype(BF16))
    a = jnp.concatenate(attn, axis=1)
    flat[...] = jnp.dot(a, proj_ref[...], preferred_element_type=F32)
    x, z = at[0], at[1]
    for s in range(4):
        xd = lax.rem(x + s, 4)
        for j in range(2):
            zd = z if j == 0 else 1 - z
            col = pl.multiple_of((zd * 4 + xd) * W, HD)
            out_ref[s, :, j * W : (j + 1) * W] = flat[:, pl.ds(col, W)].astype(BF16)


def text_merge(tlen, at, msg, tq, tk, tv, proj):
    return pl.pallas_call(
        merge_kernel,
        out_shape=jax.ShapeDtypeStruct((4, TL, 2 * W), BF16),
        in_specs=[SM, SM, VM, VM, VM, VM, VM],
        out_specs=VM,
        scratch_shapes=[pltpu.VMEM((TL, 8 * W), F32)],
        compiler_params=params(24),
        cost_estimate=cost(2 * TL * W * 8 * W, 3 * 2**20, TEXT * HD * NH),
        name="text_merge",
    )(tlen, at, msg, tq, tk, tv, proj)


def split_kernel(at, proj_ref, o0, o1, o2, o3, sem):
    x, z = at[0], at[1]
    copies = []
    for s, out in enumerate((o0, o1, o2, o3)):
        xd = lax.rem(x + s, 4)
        for j in range(2):
            zd = z if j == 0 else 1 - z
            col = pl.multiple_of((zd * 4 + xd) * W, HD)
            copies.append(
                pltpu.make_async_copy(
                    proj_ref.at[:, pl.ds(col, W)], out.at[:, pl.ds(j * W, W)], sem.at[2 * s + j]
                )
            )
    for c in copies:
        c.start()
    for c in copies:
        c.wait()


def split_proj(at, proj):
    piece = jax.ShapeDtypeStruct((W, 2 * W), BF16)
    return pl.pallas_call(
        split_kernel,
        out_shape=(piece,) * 4,
        in_specs=[SM, ANY],
        out_specs=(ANY,) * 4,
        scratch_shapes=[pltpu.SemaphoreType.DMA((8,))],
        cost_estimate=cost(0, 5 * 2**20),
        name="split_proj",
    )(at, proj)


def project_kernel(*refs):
    a_refs, w_refs, t_refs = refs[:12], refs[12:16], refs[16:20]
    own_ref, away_ref = refs[20:]
    w = jnp.concatenate([r[...] for r in w_refs], axis=0)
    for i in range(2):
        rs = pl.ds(i * TT, TT)
        a = jnp.concatenate([r[rs, :] for r in a_refs], axis=1)
        o = jnp.dot(a, w, preferred_element_type=F32)
        own_ref[rs, :] = o[:, :W]
        away_ref[rs, :] = o[:, W:].astype(BF16)
    t = t_refs[0][...].astype(F32)
    for r in t_refs[1:]:
        t += r[...].astype(F32)
    t = jnp.concatenate([t, jnp.zeros_like(t)], axis=0)
    own_ref[pl.ds(ROWS, 16), :] = t[:, :W]
    away_ref[pl.ds(ROWS, 16), :] = t[:, W:].astype(BF16)


def project(attn, proj, text):
    return pl.pallas_call(
        project_kernel,
        out_shape=(
            jax.ShapeDtypeStruct((ROWS + 16, W), F32),
            jax.ShapeDtypeStruct((ROWS + 16, W), BF16),
        ),
        in_specs=[VM] * 20,
        out_specs=(VM, VM),
        compiler_params=params(32),
        cost_estimate=cost(2 * ROWS * 4 * W * 2 * W, 6 * 2**20),
        name="project",
    )(*attn, *proj, *text)


def add_kernel(own_ref, got_ref, video_ref, text_ref):
    video_ref[...] = (own_ref[:ROWS, :] + got_ref[:ROWS, :].astype(F32)).astype(BF16)
    t = own_ref[pl.ds(ROWS, 16), :] + got_ref[pl.ds(ROWS, 16), :].astype(F32)
    text_ref[...] = t[:TL, :].astype(BF16)


def add_up(own, got):
    return pl.pallas_call(
        add_kernel,
        out_shape=(jax.ShapeDtypeStruct((ROWS, W), BF16), jax.ShapeDtypeStruct((TL, W), BF16)),
        in_specs=[VM, VM],
        out_specs=(VM, VM),
        cost_estimate=cost(0, 2 * 2**20),
        name="add_up",
    )(own, got)


def per_device(
    video_q, video_k, video_v, text_q, text_k, text_v, video_proj, text_proj, window_mask, text_length
):
    core = (lax.axis_index("tile") % 2).astype(jnp.int32).reshape(1)
    head_at = lax.axis_index("head").astype(jnp.int32)
    at = jnp.stack([head_at % 4, head_at // 4])

    kv = jnp.concatenate([video_k, video_v], axis=0)
    far = over_chip(kv)
    up = rows_on(kv, 1)
    dn = rows_on(kv, -1)
    side = other_core(kv)

    both = jnp.concatenate([text_q, text_k, text_v], axis=1)
    every = lax.all_to_all(
        jnp.broadcast_to(both[None], (32, *both.shape)), "tile", 0, 0, tiled=True
    ).reshape(TEXT, 3 * W)
    tq, tk, tv = every[:, :W], every[:, W : 2 * W], every[:, 2 * W :]

    pieces = split_proj(at, video_proj)
    proj = [pieces[0]] + [x_on(pieces[s], s) for s in range(1, 4)]

    msg = text_part(tq, kv).reshape(32, TL, W + HD)

    far_up, far_dn = [], []
    for h in range(NH):
        fh = far[:, h * HD : (h + 1) * HD]
        far_up.append(rows_on(fh, 1))
        far_dn.append(rows_on(fh, -1))
    side_up, side_dn = other_core(up), other_core(dn)

    acc, m, l = early(
        window_mask, text_length, core, video_q, tk, tv, (kv, up, dn, side, side_up, side_dn)
    )
    got = lax.all_to_all(msg, "tile", 0, 0, tiled=True).reshape(TEXT, W + HD)

    attn = []
    for h in range(NH):
        a = late(h, window_mask, core, video_q, far, far_up[h], far_dn[h], acc, m, l)
        attn.append([a] + [x_on(a, s) for s in range(1, 4)])

    tp = text_merge(text_length, at, got, text_q, tk, tv, text_proj)
    text = [tp[0]] + [x_on(tp[s], s) for s in range(1, 4)]

    own, away = project([attn[h][s] for s in range(4) for h in range(NH)], proj, text)
    return add_up(own, z_pair(away))


def solution(mesh):
    both, rows = P("tile", "head"), P("head", None)
    return jax.shard_map(
        per_device,
        mesh=mesh,
        in_specs=(both,) * 6 + (rows, rows, P("tile", None), P()),
        out_specs=(both, both),
        check_vma=False,
    )
```

time: 292 us -> 216 us (0.74)
  Pallas kernels: 0 us -> 98.3 us
  blocking collectives: 97.8 us -> 0 us
  matrix products: 46.3 us -> 0 us
  other arithmetic: 36.7 us -> 1.39 us
  starting transfers between devices: 27.2 us -> 55.2 us
  local copies, waits for them, and re-layouts: 44.3 us -> 18.5 us
    pallas_call x0 -> x9, Pallas kernels: none -> 98.3 us  [the longest x1 73.4 us: split_proj(): pl.pallas_call(split_kernel, out_shape=(piece,) * 4, in_specs=[SM, ANY],...]
    all_gather x1 -> x0, blocking collectives: 54.8 us -> none  [side_by_side(): lax.all_gather(both, axis, axis=dim, tiled=True)]
    dot_general x14 -> x0, matrix products: 46.3 us -> none  [the longest x2 17.5 us: attend_tile(): jnp.einsum('qhd,khd->hqk', queries, window_keys, preferred_element_type=j...]
    all_to_all x1 -> x0, blocking collectives: 43 us -> none  [summed_on_arrival(): lax.all_to_all(pieces, axis, split_axis=0, concat_axis=0, tiled=True)]
    ppermute x4 -> x28, waiting for transfers between devices: 0.01 us -> 37.6 us  [the longest x15 16.9 us: x_on(): lax.ppermute(x, 'head', [(i, i // 4 * 4 + (i + d) % 4) for i in range(8)])]
    all_to_all x2, waiting for transfers between devices: 35.6 us -> 0.01 us  [the longest x1 0.01 us: per_device(): got = lax.all_to_all(msg, 'tile', 0, 0, tiled=True).reshape(TEXT, W + HD)]
    ppermute x4 -> x28, starting transfers between devices: 12.5 us -> 41.1 us  [the longest x15 20.2 us: x_on(): lax.ppermute(x, 'head', [(i, i // 4 * 4 + (i + d) % 4) for i in range(8)])]
    squeeze x4 -> x1, local copies, waits for them, and re-layouts: 28.2 us -> 0.01 us  [per_device(): text = [tp[0]] + [x_on(tp[s], s) for s in range(1, 4)]]
  transfers between devices with their start and end apart: 6 -> 30, of which waited for: 1 -> 11; matrix products, arithmetic and copies ran while one was open for 12% -> 2% of each run, Pallas kernels for 0% -> 44%
where the time goes in v1:
time: 216 us; the launch traced here: 213 us
  Pallas kernels  98.3 us (46%)
  starting transfers between devices  55.2 us (26%)
  waiting for transfers between devices  37.6 us (17%)
  local copies, waits for them, and re-layouts  18.5 us (9%)
    pallas_call x1, Pallas kernels, split_proj(): pl.pallas_call(split_kernel, out_shape=(piece,) * 4, in_specs=[SM, ANY],...  73.4 us
    ppermute x15, starting transfers between devices, x_on(): lax.ppermute(x, 'head', [(i, i // 4 * 4 + (i + d) % 4) for i in range(8)])  20.2 us
    ppermute x15, waiting for transfers between devices, x_on(): lax.ppermute(x, 'head', [(i, i // 4 * 4 + (i + d) % 4) for i in range(8)])  16.9 us
    unnamed x57, local copies, waits for them, and re-layouts  13.7 us
    ppermute x8, starting transfers between devices, rows_on(): lax.ppermute(x, 'tile', [(i, (i // 8 + d) % 4 * 8 + i % 8) for i in range...  12.8 us
    pallas_call x1, Pallas kernels, early(): pl.pallas_call(early_kernel, out_shape=(part, part, part), in_specs=[SM,...  9.09 us
    ppermute x8, waiting for transfers between devices, rows_on(): lax.ppermute(x, 'tile', [(i, (i // 8 + d) % 4 * 8 + i % 8) for i in range...  8.44 us
    all_to_all x1, starting transfers between devices, per_device(): lax.all_to_all(jnp.broadcast_to(both[None], (32, *both.shape)), 'tile', 0...  7.37 us
  transfers between devices with their start and end apart: 30, of which 11 were waited for; matrix products, arithmetic and copies ran while one was open for 2% of the time, Pallas kernels for 44%

profile of v1, /device:TPU:32, one launch (start us, length us, event | category | flops | bytes accessed | tf_op | source)
XLA Modules:
  0.0 212.6 jit_solution(817625050999281918)
XLA Ops:
  2.7 3.1 %collective-permute-start.4 = (bf16[1024,384]{1,0:T(8,128)(2,1)S(1)}, bf16[1024,384]{1,0:T(8,128)(2,1)S(1)}, u32[]{:S(2)}, u32[]{:S(2)}) collective-permute-start(bf16[1024,384]{1,0:T(8,128)(2,1)S(1)} %constant_dynamic-update-slice_fusion.b0.kv_ref), channel_id=1, source_target_pairs={{0,192},{8,200},{16,208},{24,216},{32,224},{40,232},{48,240},{56,2... | collective-permute-start | bytes 2359304 | tf_op jit(solution)/shard_map/ppermute | solution.py:37
  5.8 4.6 %collective-permute-start = (bf16[1024,384]{1,0:T(8,128)(2,1)S(1)}, bf16[1024,384]{1,0:T(8,128)(2,1)S(1)}, u32[]{:S(2)}, u32[]{:S(2)}) collective-permute-start(bf16[1024,384]{1,0:T(8,128)(2,1)S(1)} %constant_dynamic-update-slice_fusion.b0.kv_ref), channel_id=1, source_target_pairs={{0,56},{8,16},{16,8},{24,32},{32,24},{40,48},{48,40},{56,0},{64,12... | collective-permute-start | bytes 2359304 | tf_op jit(solution)/shard_map/ppermute | solution.py:41
  12.0 7.4 %all-to-all-start = ((bf16[32,8,1152]{2,1,0:T(8,128)(2,1)}), bf16[32,8,1152]{2,1,0:T(8,128)(2,1)}, u32[]{:S(2)}, u32[]{:S(2)}) async-start(bf16[32,8,1152]{2,1,0:T(8,128)(2,1)} %broadcast_in_dim.2), calls=%async_computation | async-start | bytes 1179648 | tf_op jit(solution)/shard_map/all_to_all | solution.py:404
  19.7 4.2 %collective-permute-done.4.b2 = bf16[1024,384]{1,0:T(8,128)(2,1)S(1)} collective-permute-done((bf16[1024,384]{1,0:T(8,128)(2,1)S(1)}, bf16[1024,384]{1,0:T(8,128)(2,1)S(1)}, u32[]{:S(2)}, u32[]{:S(2)}) %collective-permute-start.4) | collective-permute-done | bytes 786464 | tf_op jit(solution)/shard_map/ppermute | solution.py:37
  23.9 4.3 %collective-permute-done.3.b1 = bf16[1024,384]{1,0:T(8,128)(2,1)} collective-permute-done((bf16[1024,384]{1,0:T(8,128)(2,1)S(1)}, bf16[1024,384]{1,0:T(8,128)(2,1)}, u32[]{:S(2)}, u32[]{:S(2)}) %collective-permute-start.3) | collective-permute-done | bytes 786464 | tf_op jit(solution)/shard_map/ppermute | solution.py:37
  28.1 5.6 %collective-permute-done.b0 = bf16[1024,384]{1,0:T(8,128)(2,1)S(1)} collective-permute-done((bf16[1024,384]{1,0:T(8,128)(2,1)S(1)}, bf16[1024,384]{1,0:T(8,128)(2,1)S(1)}, u32[]{:S(2)}, u32[]{:S(2)}) %collective-permute-start) | collective-permute-done | bytes 786464 | tf_op jit(solution)/shard_map/ppermute | solution.py:41
  34.6 2.5 %collective-permute-start.11 = (bf16[1024,128]{1,0:T(8,128)(2,1)}, bf16[1024,128]{1,0:T(8,128)(2,1)S(1)}, u32[]{:S(2)}, u32[]{:S(2)}) collective-permute-start(bf16[1024,128]{1,0:T(8,128)(2,1)} %get-tuple-element.20), channel_id=1, source_target_pairs={{0,192},{8,200},{16,208},{24,216},{32,224},{40,232},{48,240},{56,2... | collective-permute-start | bytes 786440 | tf_op jit(solution)/shard_map/ppermute | solution.py:37
  38.0 3.2 %collective-permute-start.9 = (bf16[1024,128]{1,0:T(8,128)(2,1)}, bf16[1024,128]{1,0:T(8,128)(2,1)S(1)}, u32[]{:S(2)}, u32[]{:S(2)}) collective-permute-start(bf16[1024,128]{1,0:T(8,128)(2,1)} %get-tuple-element.21), channel_id=1, source_target_pairs={{0,192},{8,200},{16,208},{24,216},{32,224},{40,232},{48,240},{56,2... | collective-permute-start | bytes 786440 | tf_op jit(solution)/shard_map/ppermute | solution.py:37
  41.9 73.4 %split_proj.1 = (bf16[384,768]{1,0:T(8,128)(2,1)}, bf16[384,768]{1,0:T(8,128)(2,1)}, bf16[384,768]{1,0:T(8,128)(2,1)}, bf16[384,768]{1,0:T(8,128)(2,1)}) custom-call(s32[2]{0:T(128)} %pad_add_fusion.at, bf16[384,3072]{1,0:T(8,128)(2,1)} %proj_ref.2), custom_call_target="tpu_custom_call" | custom-call | bytes 5242880 | tf_op jit(solution)/shard_map/split_proj/pallas_call | solution.py:329
  115.4 1.6 collective-permute-start.21
  117.0 2.7 %collective-permute-start.22 = (bf16[384,768]{1,0:T(8,128)(2,1)}, bf16[384,768]{1,0:T(8,128)(2,1)}, u32[]{:S(2)}, u32[]{:S(2)}) collective-permute-start(bf16[384,768]{1,0:T(8,128)(2,1)} %get-tuple-element.16), channel_id=1, source_target_pairs={{0,2},{1,3},{2,0},{3,1},{4,6},{5,7},{6,4},{7,5},{8,10},{9,11},{10,... | collective-permute-start | bytes 1769480 | tf_op jit(solution)/shard_map/ppermute | solution.py:51
  121.2 1.9 fusion.1
  123.1 1.8 text_part.1
  124.9 6.8 %all-to-all-start.1 = ((bf16[32,8,512]{2,1,0:T(8,128)(2,1)}), bf16[32,8,512]{2,1,0:T(8,128)(2,1)}, u32[]{:S(2)}, u32[]{:S(2)}) async-start(bf16[32,8,512]{2,1,0:T(8,128)(2,1)} %bitcast.4), calls=%async_computation.1 | async-start | bytes 524288 | tf_op jit(solution)/shard_map/all_to_all | solution.py:424
  132.4 1.8 collective-permute-start.8
  141.0 9.1 %early.1 = (f32[512,384]{1,0:T(8,128)S(1)}, f32[512,384]{1,0:T(8,128)S(1)}, f32[512,384]{1,0:T(8,128)S(1)}) custom-call(s32[2,27]{1,0:T(2,128)S(1)} %copy-done.20, s32[1]{0:T(128)S(6)} %copy.13.tlen, s32[1]{0:T(128)} %bitcast.core, bf16[512,384]{1,0:T(8,128)(2,1)S(1)} %copy-done, bf16[256,384]{1,0:T(8,128)(2,1)S(1)} %copy-done.7, ...), custom_call_target="tpu_custom_call" | custom-call | flops 2617245696 | bytes 8388608 | tf_op jit(solution)/shard_map/early/pallas_call | solution.py:159
  150.1 2.1 late.5.refs_2_
  153.5 2.1 late.4.refs_1_
  156.3 1.7 copy-done.1
  159.8 2.2 %text_merge.1 = bf16[4,8,768]{2,1,0:T(8,128)(2,1)S(1)} custom-call(s32[1]{0:T(128)S(6)} %copy.13.tlen, s32[2]{0:T(128)S(1)} %copy-done.21, bf16[256,512]{1,0:T(8,128)(2,1)} %bitcast.5.msg_ref, bf16[8,384]{1,0:T(8,128)(2,1)S(1)} %copy-done.19, bf16[256,384]{1,0:T(8,128)(2,1)S(1)} %copy-done.8, bf16[256,384]{1,0:T(8,128)(2,1)S(1)} %copy-done.6, ...), custom_call_target="tpu_custom_call" | custom-call | flops 18874368 | bytes 3145728 | tf_op jit(solution)/shard_map/text_merge/pallas_call | solution.py:296
  162.3 2.6 %collective-permute-start.17 = (bf16[512,128]{1,0:T(8,128)(2,1)S(1)}, bf16[512,128]{1,0:T(8,128)(2,1)S(1)}, u32[]{:S(2)}, u32[]{:S(2)}) collective-permute-start(bf16[512,128]{1,0:T(8,128)(2,1)S(1)} %copy-done.16), channel_id=1, source_target_pairs={{0,2},{1,3},{2,0},{3,1},{4,6},{5,7},{6,4},{7,5},{8,10},{9,11},{10,... | collective-permute-start | bytes 393224 | tf_op jit(solution)/shard_map/ppermute | solution.py:51
  164.9 3.2 %collective-permute-start.19 = (bf16[512,128]{1,0:T(8,128)(2,1)S(1)}, bf16[512,128]{1,0:T(8,128)(2,1)S(1)}, u32[]{:S(2)}, u32[]{:S(2)}) collective-permute-start(bf16[512,128]{1,0:T(8,128)(2,1)S(1)} %copy-done.18), channel_id=1, source_target_pairs={{0,3},{1,0},{2,1},{3,2},{4,7},{5,4},{6,5},{7,6},{8,11},{9,8},{10,9... | collective-permute-start | bytes 393224 | tf_op jit(solution)/shard_map/ppermute | solution.py:51
  169.0 3.9 %collective-permute-done.26.refs_19_ = bf16[8,768]{1,0:T(8,128)(2,1)S(1)} collective-permute-done((bf16[8,768]{1,0:T(8,128)(2,1)S(1)}, bf16[8,768]{1,0:T(8,128)(2,1)S(1)}, u32[]{:S(2)}, u32[]{:S(2)}) %collective-permute-start.26) | collective-permute-done | bytes 12320 | tf_op jit(solution)/shard_map/ppermute | solution.py:51
  174.0 4.1 %collective-permute-done.25.refs_18_ = bf16[8,768]{1,0:T(8,128)(2,1)S(1)} collective-permute-done((bf16[8,768]{1,0:T(8,128)(2,1)S(1)}, bf16[8,768]{1,0:T(8,128)(2,1)S(1)}, u32[]{:S(2)}, u32[]{:S(2)}) %collective-permute-start.25) | collective-permute-done | bytes 12320 | tf_op jit(solution)/shard_map/ppermute | solution.py:51
  178.8 2.6 %late.3.refs_0_ = bf16[512,128]{1,0:T(8,128)(2,1)S(1)} custom-call(s32[2,27]{1,0:T(2,128)S(1)} %copy-done.20, s32[1]{0:T(128)} %bitcast.core, bf16[512,384]{1,0:T(8,128)(2,1)S(1)} %copy-done, bf16[1024,384]{1,0:T(8,128)(2,1)S(1)} %collective-permute-done.b0, bf16[1024,128]{1,0:T(8,128)(2,1)} %collective-permute-done.1.b1, ...), custom_call_target="tpu_custom_call" | custom-call | flops 402653184 | bytes 2097152 | tf_op jit(solution)/shard_map/late/pallas_call | solution.py:214
  184.9 2.9 %collective-permute-start.18 = (bf16[512,128]{1,0:T(8,128)(2,1)S(1)}, bf16[512,128]{1,0:T(8,128)(2,1)S(1)}, u32[]{:S(2)}, u32[]{:S(2)}) collective-permute-start(bf16[512,128]{1,0:T(8,128)(2,1)S(1)} %late.3.refs_0_), channel_id=1, source_target_pairs={{0,3},{1,0},{2,1},{3,2},{4,7},{5,4},{6,5},{7,6},{8,11},{9,8},{10,9... | collective-permute-start | bytes 393224 | tf_op jit(solution)/shard_map/ppermute | solution.py:51
  188.7 2.2 %collective-permute-done.16.refs_7_ = bf16[512,128]{1,0:T(8,128)(2,1)S(1)} collective-permute-done((bf16[512,128]{1,0:T(8,128)(2,1)S(1)}, bf16[512,128]{1,0:T(8,128)(2,1)S(1)}, u32[]{:S(2)}, u32[]{:S(2)}) %collective-permute-start.16) | collective-permute-done | bytes 131104 | tf_op jit(solution)/shard_map/ppermute | solution.py:51
  190.9 2.4 %collective-permute-done.13.refs_4_ = bf16[512,128]{1,0:T(8,128)(2,1)S(1)} collective-permute-done((bf16[512,128]{1,0:T(8,128)(2,1)S(1)}, bf16[512,128]{1,0:T(8,128)(2,1)S(1)}, u32[]{:S(2)}, u32[]{:S(2)}) %collective-permute-start.13) | collective-permute-done | bytes 131104 | tf_op jit(solution)/shard_map/ppermute | solution.py:51
  196.1 2.8 %project.1 = (f32[528,384]{1,0:T(8,128)S(1)}, bf16[528,384]{1,0:T(8,128)(2,1)S(1)}) custom-call(bf16[512,128]{1,0:T(8,128)(2,1)S(1)} %late.3.refs_0_, bf16[512,128]{1,0:T(8,128)(2,1)S(1)} %copy-done.18, bf16[512,128]{1,0:T(8,128)(2,1)S(1)} %copy-done.16, bf16[512,128]{1,0:T(8,128)(2,1)S(1)} %collective-permute-done.12.refs_3_, ...), custom_call_target="tpu_custom_call" | custom-call | flops 1207959552 | bytes 6291456 | tf_op jit(solution)/shard_map/project/pallas_call | solution.py:359
  199.9 3.2 %collective-permute-start.27 = (bf16[528,384]{1,0:T(8,128)(2,1)S(1)}, bf16[528,384]{1,0:T(8,128)(2,1)S(1)}, u32[]{:S(2)}, u32[]{:S(2)}) collective-permute-start(bf16[528,384]{1,0:T(8,128)(2,1)S(1)} %get-tuple-element.19), channel_id=1, source_target_pairs={{0,4},{1,5},{2,6},{3,7},{4,0},{5,1},{6,2},{7,3},{8,12},{9,13},{10,... | collective-permute-start | bytes 1216520 | tf_op jit(solution)/shard_map/ppermute | solution.py:55
  203.1 6.7 %collective-permute-done.27.got_ref = bf16[528,384]{1,0:T(8,128)(2,1)S(1)} collective-permute-done((bf16[528,384]{1,0:T(8,128)(2,1)S(1)}, bf16[528,384]{1,0:T(8,128)(2,1)S(1)}, u32[]{:S(2)}, u32[]{:S(2)}) %collective-permute-start.27) | collective-permute-done | bytes 405536 | tf_op jit(solution)/shard_map/ppermute | solution.py:55
  210.6 2.1 add_up.1
  (101 shorter events, 30.4 us)
Async XLA Ops:
  2.7 120.4 %copy-start.2 = (bf16[1024,384]{1,0:T(8,128)(2,1)}, bf16[1024,384]{1,0:T(8,128)(2,1)S(1)}, u32[]{:S(2)}) copy-start(bf16[1024,384]{1,0:T(8,128)(2,1)S(1)} %constant_dynamic-update-slice_fusion.b0.kv_ref) | copy-start | bytes 2359300
  2.7 21.1 %collective-permute-start.4 = (bf16[1024,384]{1,0:T(8,128)(2,1)S(1)}, bf16[1024,384]{1,0:T(8,128)(2,1)S(1)}, u32[]{:S(2)}, u32[]{:S(2)}) collective-permute-start(bf16[1024,384]{1,0:T(8,128)(2,1)S(1)} %constant_dynamic-update-slice_fusion.b0.kv_ref), channel_id=1, source_target_pairs={{0,192},{8,200},{16,208},{24,216},{32,224},{40,232},{48,240},{56,2... | collective-permute-start | bytes 2359304 | tf_op jit(solution)/shard_map/ppermute | solution.py:37
  5.8 22.3 %collective-permute-start.3 = (bf16[1024,384]{1,0:T(8,128)(2,1)S(1)}, bf16[1024,384]{1,0:T(8,128)(2,1)}, u32[]{:S(2)}, u32[]{:S(2)}) collective-permute-start(bf16[1024,384]{1,0:T(8,128)(2,1)S(1)} %constant_dynamic-update-slice_fusion.b0.kv_ref), channel_id=1, source_target_pairs={{0,64},{8,72},{16,80},{24,88},{32,96},{40,104},{48,112},{56,120},{... | collective-permute-start | bytes 2359304 | tf_op jit(solution)/shard_map/ppermute | solution.py:37
  5.8 27.8 %collective-permute-start = (bf16[1024,384]{1,0:T(8,128)(2,1)S(1)}, bf16[1024,384]{1,0:T(8,128)(2,1)S(1)}, u32[]{:S(2)}, u32[]{:S(2)}) collective-permute-start(bf16[1024,384]{1,0:T(8,128)(2,1)S(1)} %constant_dynamic-update-slice_fusion.b0.kv_ref), channel_id=1, source_target_pairs={{0,56},{8,16},{16,8},{24,32},{32,24},{40,48},{48,40},{56,0},{64,12... | collective-permute-start | bytes 2359304 | tf_op jit(solution)/shard_map/ppermute | solution.py:41
  12.0 109.2 %all-to-all-start = ((bf16[32,8,1152]{2,1,0:T(8,128)(2,1)}), bf16[32,8,1152]{2,1,0:T(8,128)(2,1)}, u32[]{:S(2)}, u32[]{:S(2)}) async-start(bf16[32,8,1152]{2,1,0:T(8,128)(2,1)} %broadcast_in_dim.2), calls=%async_computation | async-start | bytes 1179648 | tf_op jit(solution)/shard_map/all_to_all | solution.py:404
  19.4 17.8 %collective-permute-start.5 = (bf16[1024,384]{1,0:T(8,128)(2,1)S(1)}, bf16[1024,384]{1,0:T(8,128)(2,1)S(1)}, u32[]{:S(2)}, u32[]{:S(2)}) collective-permute-start(bf16[1024,384]{1,0:T(8,128)(2,1)S(1)} %constant_dynamic-update-slice_fusion.b0.kv_ref), channel_id=1, source_target_pairs={{0,8},{8,0},{16,24},{24,16},{32,40},{40,32},{48,56},{56,48},{64,72... | collective-permute-start | bytes 2359304 | tf_op jit(solution)/shard_map/ppermute | solution.py:47
  23.9 99.3 %copy-start.22 = (bf16[1024,384]{1,0:T(8,128)(2,1)}, bf16[1024,384]{1,0:T(8,128)(2,1)S(1)}, u32[]{:S(2)}) copy-start(bf16[1024,384]{1,0:T(8,128)(2,1)S(1)} %collective-permute-done.4.b2) | copy-start | bytes 2359300
  23.9 108.5 %collective-permute-start.7 = (bf16[1024,384]{1,0:T(8,128)(2,1)S(1)}, bf16[1024,384]{1,0:T(8,128)(2,1)}, u32[]{:S(2)}, u32[]{:S(2)}) collective-permute-start(bf16[1024,384]{1,0:T(8,128)(2,1)S(1)} %collective-permute-done.4.b2), channel_id=1, source_target_pairs={{0,8},{8,0},{16,24},{24,16},{32,40},{40,32},{48,56},{56,48},{64,72... | collective-permute-start | bytes 2359304 | tf_op jit(solution)/shard_map/ppermute | solution.py:47
  28.1 106.1 %collective-permute-start.6 = (bf16[1024,384]{1,0:T(8,128)(2,1)}, bf16[1024,384]{1,0:T(8,128)(2,1)}, u32[]{:S(2)}, u32[]{:S(2)}) collective-permute-start(bf16[1024,384]{1,0:T(8,128)(2,1)} %collective-permute-done.3.b1), channel_id=1, source_target_pairs={{0,8},{8,0},{16,24},{24,16},{32,40},{40,32},{48,56},{56,48},{64,72... | collective-permute-start | bytes 2359304 | tf_op jit(solution)/shard_map/ppermute | solution.py:47
  34.6 80.8 %collective-permute-start.11 = (bf16[1024,128]{1,0:T(8,128)(2,1)}, bf16[1024,128]{1,0:T(8,128)(2,1)S(1)}, u32[]{:S(2)}, u32[]{:S(2)}) collective-permute-start(bf16[1024,128]{1,0:T(8,128)(2,1)} %get-tuple-element.20), channel_id=1, source_target_pairs={{0,192},{8,200},{16,208},{24,216},{32,224},{40,232},{48,240},{56,2... | collective-permute-start | bytes 786440 | tf_op jit(solution)/shard_map/ppermute | solution.py:37
  37.1 79.9 %collective-permute-start.10 = (bf16[1024,128]{1,0:T(8,128)(2,1)}, bf16[1024,128]{1,0:T(8,128)(2,1)S(1)}, u32[]{:S(2)}, u32[]{:S(2)}) collective-permute-start(bf16[1024,128]{1,0:T(8,128)(2,1)} %get-tuple-element.20), channel_id=1, source_target_pairs={{0,64},{8,72},{16,80},{24,88},{32,96},{40,104},{48,112},{56,120},{... | collective-permute-start | bytes 786440 | tf_op jit(solution)/shard_map/ppermute | solution.py:37
  38.0 81.7 %collective-permute-start.9 = (bf16[1024,128]{1,0:T(8,128)(2,1)}, bf16[1024,128]{1,0:T(8,128)(2,1)S(1)}, u32[]{:S(2)}, u32[]{:S(2)}) collective-permute-start(bf16[1024,128]{1,0:T(8,128)(2,1)} %get-tuple-element.21), channel_id=1, source_target_pairs={{0,192},{8,200},{16,208},{24,216},{32,224},{40,232},{48,240},{56,2... | collective-permute-start | bytes 786440 | tf_op jit(solution)/shard_map/ppermute | solution.py:37
  115.4 46.7 %collective-permute-start.21 = (bf16[384,768]{1,0:T(8,128)(2,1)}, bf16[384,768]{1,0:T(8,128)(2,1)}, u32[]{:S(2)}, u32[]{:S(2)}) collective-permute-start(bf16[384,768]{1,0:T(8,128)(2,1)} %get-tuple-element.15), channel_id=1, source_target_pairs={{0,1},{1,2},{2,3},{3,0},{4,5},{5,6},{6,7},{7,4},{8,9},{9,10},{10,1... | collective-permute-start | bytes 1769480 | tf_op jit(solution)/shard_map/ppermute | solution.py:51
  117.0 45.3 %collective-permute-start.22 = (bf16[384,768]{1,0:T(8,128)(2,1)}, bf16[384,768]{1,0:T(8,128)(2,1)}, u32[]{:S(2)}, u32[]{:S(2)}) collective-permute-start(bf16[384,768]{1,0:T(8,128)(2,1)} %get-tuple-element.16), channel_id=1, source_target_pairs={{0,2},{1,3},{2,0},{3,1},{4,6},{5,7},{6,4},{7,5},{8,10},{9,11},{10,... | collective-permute-start | bytes 1769480 | tf_op jit(solution)/shard_map/ppermute | solution.py:51
  119.7 45.1 %collective-permute-start.23 = (bf16[384,768]{1,0:T(8,128)(2,1)}, bf16[384,768]{1,0:T(8,128)(2,1)}, u32[]{:S(2)}, u32[]{:S(2)}) collective-permute-start(bf16[384,768]{1,0:T(8,128)(2,1)} %get-tuple-element.17), channel_id=1, source_target_pairs={{0,3},{1,0},{2,1},{3,2},{4,7},{5,4},{6,5},{7,6},{8,11},{9,8},{10,9... | collective-permute-start | bytes 1769480 | tf_op jit(solution)/shard_map/ppermute | solution.py:51
  124.9 31.4 %all-to-all-start.1 = ((bf16[32,8,512]{2,1,0:T(8,128)(2,1)}), bf16[32,8,512]{2,1,0:T(8,128)(2,1)}, u32[]{:S(2)}, u32[]{:S(2)}) async-start(bf16[32,8,512]{2,1,0:T(8,128)(2,1)} %bitcast.4), calls=%async_computation.1 | async-start | bytes 524288 | tf_op jit(solution)/shard_map/all_to_all | solution.py:424
  132.4 20.5 %collective-permute-start.8 = (bf16[1024,128]{1,0:T(8,128)(2,1)}, bf16[1024,128]{1,0:T(8,128)(2,1)S(1)}, u32[]{:S(2)}, u32[]{:S(2)}) collective-permute-start(bf16[1024,128]{1,0:T(8,128)(2,1)} %get-tuple-element.21), channel_id=1, source_target_pairs={{0,64},{8,72},{16,80},{24,88},{32,96},{40,104},{48,112},{56,120},{... | collective-permute-start | bytes 786440 | tf_op jit(solution)/shard_map/ppermute | solution.py:37
  134.2 30.7 %collective-permute-start.2 = (bf16[1024,128]{1,0:T(8,128)(2,1)}, bf16[1024,128]{1,0:T(8,128)(2,1)}, u32[]{:S(2)}, u32[]{:S(2)}) collective-permute-start(bf16[1024,128]{1,0:T(8,128)(2,1)} %get-tuple-element.22), channel_id=1, source_target_pairs={{0,192},{8,200},{16,208},{24,216},{32,224},{40,232},{48,240},{56,2... | collective-permute-start | bytes 786440 | tf_op jit(solution)/shard_map/ppermute | solution.py:37
  152.9 15.2 %collective-permute-start.1 = (bf16[1024,128]{1,0:T(8,128)(2,1)}, bf16[1024,128]{1,0:T(8,128)(2,1)}, u32[]{:S(2)}, u32[]{:S(2)}) collective-permute-start(bf16[1024,128]{1,0:T(8,128)(2,1)} %get-tuple-element.22), channel_id=1, source_target_pairs={{0,64},{8,72},{16,80},{24,88},{32,96},{40,104},{48,112},{56,120},{... | collective-permute-start | bytes 786440 | tf_op jit(solution)/shard_map/ppermute | solution.py:37
  162.1 22.4 %collective-permute-start.20 = (bf16[512,128]{1,0:T(8,128)(2,1)S(1)}, bf16[512,128]{1,0:T(8,128)(2,1)S(1)}, u32[]{:S(2)}, u32[]{:S(2)}) collective-permute-start(bf16[512,128]{1,0:T(8,128)(2,1)S(1)} %copy-done.16), channel_id=1, source_target_pairs={{0,3},{1,0},{2,1},{3,2},{4,7},{5,4},{6,5},{7,6},{8,11},{9,8},{10,9... | collective-permute-start | bytes 393224 | tf_op jit(solution)/shard_map/ppermute | solution.py:51
  162.3 22.6 %collective-permute-start.17 = (bf16[512,128]{1,0:T(8,128)(2,1)S(1)}, bf16[512,128]{1,0:T(8,128)(2,1)S(1)}, u32[]{:S(2)}, u32[]{:S(2)}) collective-permute-start(bf16[512,128]{1,0:T(8,128)(2,1)S(1)} %copy-done.16), channel_id=1, source_target_pairs={{0,2},{1,3},{2,0},{3,1},{4,6},{5,7},{6,4},{7,5},{8,10},{9,11},{10,... | collective-permute-start | bytes 393224 | tf_op jit(solution)/shard_map/ppermute | solution.py:51
  164.8 22.9 %collective-permute-start.14 = (bf16[512,128]{1,0:T(8,128)(2,1)S(1)}, bf16[512,128]{1,0:T(8,128)(2,1)S(1)}, u32[]{:S(2)}, u32[]{:S(2)}) collective-permute-start(bf16[512,128]{1,0:T(8,128)(2,1)S(1)} %copy-done.16), channel_id=1, source_target_pairs={{0,1},{1,2},{2,3},{3,0},{4,5},{5,6},{6,7},{7,4},{8,9},{9,10},{10,1... | collective-permute-start | bytes 393224 | tf_op jit(solution)/shard_map/ppermute | solution.py:51
  164.9 23.7 %collective-permute-start.19 = (bf16[512,128]{1,0:T(8,128)(2,1)S(1)}, bf16[512,128]{1,0:T(8,128)(2,1)S(1)}, u32[]{:S(2)}, u32[]{:S(2)}) collective-permute-start(bf16[512,128]{1,0:T(8,128)(2,1)S(1)} %copy-done.18), channel_id=1, source_target_pairs={{0,3},{1,0},{2,1},{3,2},{4,7},{5,4},{6,5},{7,6},{8,11},{9,8},{10,9... | collective-permute-start | bytes 393224 | tf_op jit(solution)/shard_map/ppermute | solution.py:51
  168.1 4.8 %collective-permute-start.26 = (bf16[8,768]{1,0:T(8,128)(2,1)S(1)}, bf16[8,768]{1,0:T(8,128)(2,1)S(1)}, u32[]{:S(2)}, u32[]{:S(2)}) collective-permute-start(bf16[8,768]{1,0:T(8,128)(2,1)S(1)} %get-tuple-element.26), channel_id=1, source_target_pairs={{0,3},{1,0},{2,1},{3,2},{4,7},{5,4},{6,5},{7,6},{8,11},{9,8},{10,9... | collective-permute-start | bytes 36872 | tf_op jit(solution)/shard_map/ppermute | solution.py:51
  172.9 5.2 %collective-permute-start.25 = (bf16[8,768]{1,0:T(8,128)(2,1)S(1)}, bf16[8,768]{1,0:T(8,128)(2,1)S(1)}, u32[]{:S(2)}, u32[]{:S(2)}) collective-permute-start(bf16[8,768]{1,0:T(8,128)(2,1)S(1)} %get-tuple-element.27), channel_id=1, source_target_pairs={{0,2},{1,3},{2,0},{3,1},{4,6},{5,7},{6,4},{7,5},{8,10},{9,11},{10,... | collective-permute-start | bytes 36872 | tf_op jit(solution)/shard_map/ppermute | solution.py:51
  178.1 4.9 %collective-permute-start.24 = (bf16[8,768]{1,0:T(8,128)(2,1)S(1)}, bf16[8,768]{1,0:T(8,128)(2,1)S(1)}, u32[]{:S(2)}, u32[]{:S(2)}) collective-permute-start(bf16[8,768]{1,0:T(8,128)(2,1)S(1)} %get-tuple-element.28), channel_id=1, source_target_pairs={{0,1},{1,2},{2,3},{3,0},{4,5},{5,6},{6,7},{7,4},{8,9},{9,10},{10,1... | collective-permute-start | bytes 36872 | tf_op jit(solution)/shard_map/ppermute | solution.py:51
  183.0 7.9 %collective-permute-start.16 = (bf16[512,128]{1,0:T(8,128)(2,1)S(1)}, bf16[512,128]{1,0:T(8,128)(2,1)S(1)}, u32[]{:S(2)}, u32[]{:S(2)}) collective-permute-start(bf16[512,128]{1,0:T(8,128)(2,1)S(1)} %copy-done.18), channel_id=1, source_target_pairs={{0,2},{1,3},{2,0},{3,1},{4,6},{5,7},{6,4},{7,5},{8,10},{9,11},{10,... | collective-permute-start | bytes 393224 | tf_op jit(solution)/shard_map/ppermute | solution.py:51
  184.5 8.8 %collective-permute-start.13 = (bf16[512,128]{1,0:T(8,128)(2,1)S(1)}, bf16[512,128]{1,0:T(8,128)(2,1)S(1)}, u32[]{:S(2)}, u32[]{:S(2)}) collective-permute-start(bf16[512,128]{1,0:T(8,128)(2,1)S(1)} %copy-done.18), channel_id=1, source_target_pairs={{0,1},{1,2},{2,3},{3,0},{4,5},{5,6},{6,7},{7,4},{8,9},{9,10},{10,1... | collective-permute-start | bytes 393224 | tf_op jit(solution)/shard_map/ppermute | solution.py:51
  184.9 8.4 %collective-permute-start.18 = (bf16[512,128]{1,0:T(8,128)(2,1)S(1)}, bf16[512,128]{1,0:T(8,128)(2,1)S(1)}, u32[]{:S(2)}, u32[]{:S(2)}) collective-permute-start(bf16[512,128]{1,0:T(8,128)(2,1)S(1)} %late.3.refs_0_), channel_id=1, source_target_pairs={{0,3},{1,0},{2,1},{3,2},{4,7},{5,4},{6,5},{7,6},{8,11},{9,8},{10,9... | collective-permute-start | bytes 393224 | tf_op jit(solution)/shard_map/ppermute | solution.py:51
  187.8 7.1 %collective-permute-start.15 = (bf16[512,128]{1,0:T(8,128)(2,1)S(1)}, bf16[512,128]{1,0:T(8,128)(2,1)S(1)}, u32[]{:S(2)}, u32[]{:S(2)}) collective-permute-start(bf16[512,128]{1,0:T(8,128)(2,1)S(1)} %late.3.refs_0_), channel_id=1, source_target_pairs={{0,2},{1,3},{2,0},{3,1},{4,6},{5,7},{6,4},{7,5},{8,10},{9,11},{10,... | collective-permute-start | bytes 393224 | tf_op jit(solution)/shard_map/ppermute | solution.py:51
  188.6 7.6 %collective-permute-start.12 = (bf16[512,128]{1,0:T(8,128)(2,1)S(1)}, bf16[512,128]{1,0:T(8,128)(2,1)S(1)}, u32[]{:S(2)}, u32[]{:S(2)}) collective-permute-start(bf16[512,128]{1,0:T(8,128)(2,1)S(1)} %late.3.refs_0_), channel_id=1, source_target_pairs={{0,1},{1,2},{2,3},{3,0},{4,5},{5,6},{6,7},{7,4},{8,9},{9,10},{10,1... | collective-permute-start | bytes 393224 | tf_op jit(solution)/shard_map/ppermute | solution.py:51
  199.9 9.9 %collective-permute-start.27 = (bf16[528,384]{1,0:T(8,128)(2,1)S(1)}, bf16[528,384]{1,0:T(8,128)(2,1)S(1)}, u32[]{:S(2)}, u32[]{:S(2)}) collective-permute-start(bf16[528,384]{1,0:T(8,128)(2,1)S(1)} %get-tuple-element.19), channel_id=1, source_target_pairs={{0,4},{1,5},{2,6},{3,7},{4,0},{5,1},{6,2},{7,3},{8,12},{9,13},{10,... | collective-permute-start | bytes 1216520 | tf_op jit(solution)/shard_map/ppermute | solution.py:55
  (26 other events, 325.1 us)

commit v2 on v1

v2 whole, which is shorter than its diff:
```python
import functools
import math

import jax
import jax.numpy as jnp
from jax import lax
from jax.experimental import pallas as pl
from jax.experimental.pallas import tpu as pltpu
from jax.sharding import PartitionSpec as P

HD = 128
TT = 256
NH = 3
W = NH * HD
TEXT = 256
TL = 8
ROWS = 2 * TT
SCALE = math.log2(math.e) / math.sqrt(HD)
BIG = 1e30
F32 = jnp.float32
BF16 = jnp.bfloat16

ANY = pl.BlockSpec(memory_space=pl.ANY)
SM = pl.BlockSpec(memory_space=pltpu.SMEM)
VM = pl.BlockSpec(memory_space=pltpu.VMEM)
HBM = pl.BlockSpec(memory_space=pltpu.HBM)


def params(mib):
    return pltpu.CompilerParams(vmem_limit_bytes=mib * 2**20)


def cost(flops, nbytes, exps=0):
    return pl.CostEstimate(flops=1, bytes_accessed=1, transcendentals=1)


def rows_on(x, d):
    return lax.ppermute(x, "tile", [(i, ((i // 8 + d) % 4) * 8 + i % 8) for i in range(32)])


def over_chip(x):
    return lax.ppermute(
        x, "tile", [(i, (i // 8) * 8 + (i % 8 + (1 if i % 2 else -1)) % 8) for i in range(32)]
    )


def other_core(x):
    return lax.ppermute(x, "tile", [(i, i ^ 1) for i in range(32)])


def x_swap(x):
    groups = [[0, 1, 2, 3], [4, 5, 6, 7]]
    return lax.all_to_all(x, "head", 0, 0, tiled=True, axis_index_groups=groups)


def x_on(x, d):
    return lax.ppermute(x, "head", [(i, (i // 4) * 4 + (i + d) % 4) for i in range(8)])


def z_pair(x):
    return lax.ppermute(x, "head", [(i, i ^ 4) for i in range(8)])


def fold(x, op):
    r = x[:, :HD]
    for i in range(1, x.shape[1] // HD):
        r = op(r, x[:, i * HD : (i + 1) * HD])
    return r


def scores(q, k):
    return lax.dot_general(q, k, (((1,), (1,)), ((), ())), preferred_element_type=F32)


def spread(col):
    return jnp.broadcast_to(col, (col.shape[0], HD))


def bias_of(wm, tile, frame, row, col):
    live = wm[tile, 9 * (frame - tile + 1) + 3 * row + col]
    return jnp.where(live > 0, 0.0, -BIG).astype(F32)


def early_kernel(
    wm, tlen, q_ref, t_ref, b0, b1, b2, b3, b4, b5, acc_ref, m_ref, l_ref, kbuf, s_s, mx_s, sem
):
    blocks = (b0, b1, b2, b3, b4, b5)
    nb = len(blocks)
    for b in range(nb):
        pltpu.make_async_copy(blocks[b], kbuf.at[b], sem.at[b]).start()
    lane = lax.broadcasted_iota(jnp.int32, (1, TEXT), 1)
    tbias = jnp.where(lane < tlen[0], 0.0, -BIG)
    pcol = 2 - 2 * lax.rem(lax.axis_index("tile"), 2)
    colof = (1, 1, 1, pcol, pcol, pcol)
    rowof = (1, 0, 2, 1, 0, 2)

    def hs(h):
        return pl.ds(h * HD, HD)

    def p1_text(h, w):
        for t in range(2):
            k = t_ref[:, pl.ds(W + h * HD, HD)]
            s = scores(q_ref[pl.ds(t * TT, TT), hs(h)], k) * SCALE + tbias
            s_s[w, t, nb, :, :TEXT] = s
            mx_s[w, t] = fold(s, jnp.maximum)

    def p1(h, w, b):
        k = kbuf[b, :ROWS, hs(h)]
        for t in range(2):
            s = scores(q_ref[pl.ds(t * TT, TT), hs(h)], k)
            mx = mx_s[w, t]
            for f in range(2):
                sf = s[:, f * TT : (f + 1) * TT] * SCALE + bias_of(wm, t, f, rowof[b], colof[b])
                s_s[w, t, b, :, f * TT : (f + 1) * TT] = sf
                mx = jnp.maximum(mx, fold(sf, jnp.maximum))
            mx_s[w, t] = mx

    def top(h, w):
        for t in range(2):
            m_ref[pl.ds(t * TT, TT), hs(h)] = spread(jnp.max(mx_s[w, t], axis=1, keepdims=True))

    def weigh(s, m):
        return jnp.concatenate(
            [jnp.exp2(s[:, i * HD : (i + 1) * HD] - m) for i in range(s.shape[1] // HD)], axis=1
        )

    def p2_text(h, w):
        for t in range(2):
            rs = pl.ds(t * TT, TT)
            p = weigh(s_s[w, t, nb, :, :TEXT], m_ref[rs, hs(h)])
            l_ref[rs, hs(h)] = fold(p, jnp.add)
            v = t_ref[:, pl.ds(2 * W + h * HD, HD)]
            acc_ref[rs, hs(h)] = jnp.dot(p.astype(BF16), v, preferred_element_type=F32)

    def p2(h, w, b):
        v = kbuf[b, ROWS:, hs(h)]
        for t in range(2):
            rs = pl.ds(t * TT, TT)
            p = weigh(s_s[w, t, b], m_ref[rs, hs(h)])
            l_ref[rs, hs(h)] += fold(p, jnp.add)
            acc_ref[rs, hs(h)] += jnp.dot(p.astype(BF16), v, preferred_element_type=F32)

    p1_text(0, 0)
    for b in range(nb):
        pltpu.make_async_copy(blocks[b], kbuf.at[b], sem.at[b]).wait()
        p1(0, 0, b)
    top(0, 0)
    for h in range(NH):
        w = h % 2
        p2_text(h, w)
        if h + 1 < NH:
            p1_text(h + 1, 1 - w)
        for b in range(nb):
            p2(h, w, b)
            if h + 1 < NH:
                p1(h + 1, 1 - w, b)
        if h + 1 < NH:
            top(h + 1, 1 - w)


def early(wm, tlen, q, every, blocks):
    nb = len(blocks)
    part = jax.ShapeDtypeStruct((ROWS, W), F32)
    return pl.pallas_call(
        early_kernel,
        out_shape=(part, part, part),
        in_specs=[SM, SM, VM, VM] + [ANY] * nb,
        out_specs=(VM, VM, VM),
        scratch_shapes=[
            pltpu.VMEM((nb, 2 * ROWS, W), BF16),
            pltpu.VMEM((2, 2, nb + 1, TT, ROWS), F32),
            pltpu.VMEM((2, 2, TT, HD), F32),
            pltpu.SemaphoreType.DMA((nb,)),
        ],
        compiler_params=params(60),
        cost_estimate=cost(4 * ROWS * (nb * ROWS + TEXT) * W, 8 * 2**20, ROWS * nb * ROWS * NH),
        name="early",
    )(wm, tlen, q, every, *blocks)


def late_kernel(wm, q_ref, b0, b1, b2, acc_ref, m_ref, l_ref, *rest):
    o_ref = rest[-1]
    blocks = (b0, b1, b2)
    fcol = 2 * lax.rem(lax.axis_index("tile"), 2)
    rowof = (1, 0, 2)
    for t in range(2):
        rs = pl.ds(t * TT, TT)
        parts = []
        mx = None
        for b in range(3):
            s = scores(q_ref[rs, :], blocks[b][:ROWS, :])
            for f in range(2):
                sf = s[:, f * TT : (f + 1) * TT] * SCALE + bias_of(wm, t, f, rowof[b], fcol)
                parts.append(sf)
                fx = fold(sf, jnp.maximum)
                mx = fx if mx is None else jnp.maximum(mx, fx)
        mo = m_ref[rs, :]
        mn = jnp.maximum(mo, spread(jnp.max(mx, axis=1, keepdims=True)))
        al = jnp.exp2(mo - mn)
        acc = acc_ref[rs, :] * al
        tot = l_ref[rs, :] * al
        for b in range(3):
            p = jnp.concatenate(
                [
                    jnp.exp2(parts[2 * b + f][:, i * HD : (i + 1) * HD] - mn)
                    for f in range(2)
                    for i in range(2)
                ],
                axis=1,
            )
            tot += fold(p, jnp.add)
            acc += jnp.dot(p.astype(BF16), blocks[b][ROWS:, :], preferred_element_type=F32)
        o = (acc / jnp.sum(tot, axis=1, keepdims=True)).astype(BF16)
        for x in range(4):
            o_ref[x, rs, :] = o


def late(wm, q, far, acc, m, l, *deps):
    head = pl.BlockSpec((ROWS, HD), lambda i: (0, i))
    block = pl.BlockSpec((2 * ROWS, HD), lambda i: (0, i))
    return pl.pallas_call(
        late_kernel,
        grid=(NH,),
        out_shape=jax.ShapeDtypeStruct((4, ROWS, W), BF16),
        in_specs=[SM, head, block, block, block, head, head, head] + [ANY] * len(deps),
        out_specs=pl.BlockSpec((4, ROWS, HD), lambda i: (0, 0, i)),
        compiler_params=params(60),
        cost_estimate=cost(12 * ROWS * ROWS * W, 2 * 2**20, 3 * ROWS * ROWS),
        name="late",
    )(wm, q, *far, acc, m, l, *deps)


def columns(xd, j):
    z = lax.axis_index("head") // 4
    return pl.ds(pl.multiple_of(((z + j - 2 * j * z) * 4 + xd) * W, HD), W)


def pieces3(x):
    hi = x.astype(BF16).astype(F32)
    mid = (x - hi).astype(BF16).astype(F32)
    return hi, mid, x - hi - mid


def text_kernel(t_ref, kv_ref, *rest):
    msg_ref = rest[-1]
    lane = lax.broadcasted_iota(jnp.int32, (TEXT, HD), 1)
    stat = jnp.zeros((TEXT, HD), F32)
    for h in range(NH):
        hs = pl.ds(h * HD, HD)
        s = scores(t_ref[:, hs], kv_ref[:ROWS, hs]) * SCALE
        m = jnp.max(fold(s, jnp.maximum), axis=1, keepdims=True)
        p = jnp.exp2(s - m)
        tot = jnp.sum(fold(p, jnp.add), axis=1, keepdims=True)
        acc = jnp.dot(p.astype(BF16), kv_ref[ROWS:, hs], preferred_element_type=F32)
        msg_ref[:, hs] = (acc / tot).astype(BF16)
        for j, piece in enumerate(pieces3(m + jnp.log2(tot))):
            stat = jnp.where(lane == 8 * j + h, spread(piece), stat)
    msg_ref[:, W:] = stat.astype(BF16)


def text_part(every, kv, *deps):
    return pl.pallas_call(
        text_kernel,
        out_shape=jax.ShapeDtypeStruct((TEXT, W + HD), BF16),
        in_specs=[VM, VM] + [ANY] * len(deps),
        out_specs=VM,
        compiler_params=params(60),
        cost_estimate=cost(4 * TEXT * ROWS * W, 2 * 2**20, TEXT * ROWS * NH),
        name="text_part",
    )(every, kv, *deps)


def merge_kernel(tlen, msg_ref, tq_ref, t_ref, proj_ref, o0, o1, o2, o3, flat):
    msg = msg_ref[...].astype(F32)
    stat = msg[:, W:]
    slane = lax.broadcasted_iota(jnp.int32, (TEXT, HD), 1)
    lane = lax.broadcasted_iota(jnp.int32, (1, TEXT), 1)
    tbias = jnp.where(lane < tlen[0], 0.0, -BIG)
    q = tq_ref[...]
    attn = []
    for h in range(NH):
        hs = slice(h * HD, (h + 1) * HD)
        s = scores(q[:, hs], t_ref[:, pl.ds(W + h * HD, HD)]) * SCALE + tbias
        m = jnp.max(s, axis=1, keepdims=True)
        p = jnp.exp2(s - m)
        tot = jnp.sum(p, axis=1, keepdims=True)
        own = jnp.dot(p.astype(BF16), t_ref[:, pl.ds(2 * W + h * HD, HD)], preferred_element_type=F32)
        mine = (slane == h) | (slane == 8 + h) | (slane == 16 + h)
        lse = jnp.sum(jnp.where(mine, stat, 0.0), axis=1, keepdims=True)
        lse = spread(lse).reshape(TEXT // TL, TL, HD)
        peak = jnp.maximum(jnp.max(lse, axis=0), spread(m))
        wt = jnp.exp2(lse - peak[None])
        w0 = jnp.exp2(spread(m) - peak)
        num = jnp.sum(wt * msg[:, hs].reshape(TEXT // TL, TL, HD), axis=0) + w0 * own
        den = jnp.sum(wt, axis=0) + w0 * tot
        attn.append((num / den).astype(BF16))
    a = jnp.concatenate(attn, axis=1)
    flat[...] = jnp.dot(a, proj_ref[...], preferred_element_type=F32)
    x = lax.rem(lax.axis_index("head"), 4)
    for d, out in enumerate((o0, o1, o2, o3)):
        for j in range(2):
            cs = columns(lax.rem(x + d, 4), j)
            out[:, j * W : (j + 1) * W] = flat[:, cs].astype(BF16)


def text_merge(tlen, msg, tq, every, proj):
    return pl.pallas_call(
        merge_kernel,
        out_shape=(jax.ShapeDtypeStruct((TL, 2 * W), BF16),) * 4,
        in_specs=[SM, VM, VM, VM, VM],
        out_specs=(VM,) * 4,
        scratch_shapes=[pltpu.VMEM((TL, 8 * W), F32)],
        compiler_params=params(60),
        cost_estimate=cost(2 * TL * W * 8 * W, 3 * 2**20, TEXT * HD * NH),
        name="text_merge",
    )(tlen, msg, tq, every, proj)


def split_kernel(proj_ref, *rest):
    x = lax.rem(lax.axis_index("head"), 4)
    for d, out in enumerate(rest[-4:]):
        for j in range(2):
            out[:, j * W : (j + 1) * W] = proj_ref[:, columns(lax.rem(x + d, 4), j)]


def split_proj(proj, *deps):
    return pl.pallas_call(
        split_kernel,
        out_shape=(jax.ShapeDtypeStruct((W, 2 * W), BF16),) * 4,
        in_specs=[VM] + [ANY] * len(deps),
        out_specs=(VM,) * 4,
        compiler_params=params(60),
        cost_estimate=cost(0, 5 * 2**20),
        name="split_proj",
    )(proj, *deps)


def pack_kernel(k_ref, v_ref, tq_ref, tk_ref, tv_ref, kv_ref, t_ref, buf, sem):
    copies = [
        pltpu.make_async_copy(r, d, sem.at[i])
        for i, (r, d) in enumerate(
            (
                (k_ref, kv_ref.at[pl.ds(0, ROWS)]),
                (v_ref, kv_ref.at[pl.ds(ROWS, ROWS)]),
                (tq_ref, buf.at[0]),
                (tk_ref, buf.at[1]),
                (tv_ref, buf.at[2]),
            )
        )
    ]
    for c in copies:
        c.start()
    for c in copies[2:]:
        c.wait()
    both = jnp.concatenate([buf[i] for i in range(3)], axis=1)
    for i in range(32):
        t_ref[i] = both
    for c in copies[:2]:
        c.wait()


def pack(k, v, tq, tk, tv):
    return pl.pallas_call(
        pack_kernel,
        out_shape=(
            jax.ShapeDtypeStruct((2 * ROWS, W), BF16),
            jax.ShapeDtypeStruct((32, TL, 3 * W), BF16),
        ),
        in_specs=[HBM] * 5,
        out_specs=(VM, VM),
        scratch_shapes=[pltpu.VMEM((3, TL, W), BF16), pltpu.SemaphoreType.DMA((5,))],
        compiler_params=params(60),
        cost_estimate=cost(0, 2 * 2**20),
        name="pack",
    )(k, v, tq, tk, tv)


def after_kernel(x_ref, *rest):
    pass


def after(x, *deps):
    return pl.pallas_call(
        after_kernel,
        out_shape=jax.ShapeDtypeStruct(x.shape, x.dtype),
        in_specs=[ANY] * (1 + len(deps)),
        out_specs=ANY,
        input_output_aliases={0: 0},
        compiler_params=params(60),
        cost_estimate=cost(0, 1),
        name="after",
    )(x, *deps)


def project_kernel(
    a_ref, w0, w1, w2, w3, t0, t1, t2, t3, own_ref, away_ref, abuf, wbuf, acc, sem
):
    me = lax.rem(lax.axis_index("head"), 4)
    copies = []
    for x, w_ref in enumerate((w0, w1, w2, w3)):
        a_at = a_ref.at[lax.rem(me + 4 - x, 4)]
        for i, (src, dst) in enumerate(((w_ref, wbuf), (a_at, abuf))):
            copies.append(pltpu.make_async_copy(src, dst.at[x], sem.at[2 * x + i]))
            copies[-1].start()
    t = sum(r[...].astype(F32) for r in (t0, t1, t2, t3))
    t = jnp.concatenate([t, jnp.zeros_like(t)], axis=0)
    own_ref[pl.ds(ROWS, 16), :] = t[:, :W]
    away_ref[pl.ds(ROWS, 16), :] = t[:, W:].astype(BF16)
    for x in range(4):
        for c in copies[2 * x : 2 * x + 2]:
            c.wait()
        o = jnp.dot(abuf[x], wbuf[x], preferred_element_type=F32)
        if x > 0:
            o += acc[...]
        if x < 3:
            acc[...] = o
        else:
            own_ref[:ROWS, :] = o[:, :W]
            away_ref[:ROWS, :] = o[:, W:].astype(BF16)


def project(attn, proj, text):
    return pl.pallas_call(
        project_kernel,
        out_shape=(
            jax.ShapeDtypeStruct((ROWS + 16, W), F32),
            jax.ShapeDtypeStruct((ROWS + 16, W), BF16),
        ),
        in_specs=[ANY] * 5 + [VM] * 4,
        out_specs=(VM, VM),
        scratch_shapes=[
            pltpu.VMEM((4, ROWS, W), BF16),
            pltpu.VMEM((4, W, 2 * W), BF16),
            pltpu.VMEM((ROWS, 2 * W), F32),
            pltpu.SemaphoreType.DMA((8,)),
        ],
        compiler_params=params(24),
        cost_estimate=cost(2 * ROWS * 4 * W * 2 * W, 6 * 2**20),
        name="project",
    )(attn, *proj, *text)


def add_kernel(own_ref, got_ref, video_ref, text_ref):
    video_ref[...] = (own_ref[:ROWS, :] + got_ref[:ROWS, :].astype(F32)).astype(BF16)
    t = own_ref[pl.ds(ROWS, 16), :] + got_ref[pl.ds(ROWS, 16), :].astype(F32)
    text_ref[...] = t[:TL, :].astype(BF16)


def add_up(own, got):
    return pl.pallas_call(
        add_kernel,
        out_shape=(jax.ShapeDtypeStruct((ROWS, W), BF16), jax.ShapeDtypeStruct((TL, W), BF16)),
        in_specs=[VM, VM],
        out_specs=(VM, VM),
        compiler_params=params(8),
        cost_estimate=cost(0, 2 * 2**20),
        name="add_up",
    )(own, got)


def per_device(
    video_q, video_k, video_v, text_q, text_k, text_v, video_proj, text_proj, window_mask, text_length
):
    kv, text = pack(video_k, video_v, text_q, text_k, text_v)
    far = over_chip(kv)
    up = rows_on(kv, 1)
    dn = rows_on(kv, -1)
    side = other_core(kv)

    proj = split_proj(video_proj)
    proj = [x_on(p, d) if d else p for d, p in enumerate(proj)]
    every = lax.all_to_all(text, "tile", 0, 0, tiled=True).reshape(TEXT, 3 * W)
    far_up, far_dn = rows_on(far, 1), rows_on(far, -1)
    up, dn = after(up, every, proj[0]), after(dn, every, proj[0])
    side_up, side_dn = other_core(up), other_core(dn)
    acc, m, l = early(
        window_mask, text_length, video_q, every, (kv, up, dn, side, side_up, side_dn)
    )
    msg = text_part(every, kv).reshape(32, TL, W + HD)
    msg = after(msg, far_up, far_dn, acc)
    got = lax.all_to_all(msg, "tile", 0, 0, tiled=True).reshape(TEXT, W + HD)

    attn = x_swap(late(window_mask, video_q, (far, far_up, far_dn), acc, m, l, *proj[1:]))
    parts = text_merge(text_length, got, text_q, every, text_proj)
    parts = [x_on(p, d) if d else p for d, p in enumerate(parts)]
    own, away = project(attn, proj, parts)
    return add_up(own, z_pair(away))


def solution(mesh):
    both, rows = P("tile", "head"), P("head", None)
    return jax.shard_map(
        per_device,
        mesh=mesh,
        in_specs=(both,) * 6 + (rows, rows, P("tile", None), P()),
        out_specs=(both, both),
        check_vma=False,
    )
```

time: 216 us -> 136 us (0.63); the launches traced: 213 us -> 135 us
  Pallas kernels: 98.3 us -> 35.3 us
  starting transfers between devices: 55.2 us -> 41.3 us
  waiting for transfers between devices: 37.6 us -> 49.2 us
  local copies, waits for them, and re-layouts: 18.5 us -> 7.74 us
    pallas_call x5 -> x7, Pallas kernels: 82.5 us -> 16.4 us  [the longest x1 6.98 us: late(): pl.pallas_call(late_kernel, grid=(NH,), out_shape=jax.ShapeDtypeStruct((4...]
    ppermute x8 -> x4, waiting for transfers between devices: 8.44 us -> 17.6 us  [rows_on(): lax.ppermute(x, 'tile', [(i, (i // 8 + d) % 4 * 8 + i % 8) for i in range...]
    ppermute x15 -> x6, starting transfers between devices: 20.2 us -> 11.1 us  [x_on(): lax.ppermute(x, 'head', [(i, i // 4 * 4 + (i + d) % 4) for i in range(8)])]
    all_to_all x1 -> x2, starting transfers between devices: 7.37 us -> 14.2 us  [the longest x1 10.6 us: per_device(): every = lax.all_to_all(text, 'tile', 0, 0, tiled=True).reshape(TEXT, 3 * W)]
    ppermute x8 -> x4, starting transfers between devices: 12.8 us -> 6.55 us  [rows_on(): lax.ppermute(x, 'tile', [(i, (i // 8 + d) % 4 * 8 + i % 8) for i in range...]
    unnamed x57 -> x32, local copies, waits for them, and re-layouts: 13.7 us -> 7.74 us
    ppermute x15 -> x6, waiting for transfers between devices: 16.9 us -> 11.9 us  [x_on(): lax.ppermute(x, 'head', [(i, i // 4 * 4 + (i + d) % 4) for i in range(8)])]
    all_to_all x1, waiting for transfers between devices: 0.01 us -> 4.69 us  [per_device(): got = lax.all_to_all(msg, 'tile', 0, 0, tiled=True).reshape(TEXT, W + HD)]
  transfers between devices with their start and end apart: 30 -> 18, of which waited for: 11 -> 6; matrix products, arithmetic and copies ran while one was open for 2% -> 0% of each run, Pallas kernels for 44% -> 21%
where the time goes in v2:
time: 136 us; the launch traced here: 135 us
  waiting for transfers between devices  49.2 us (36%)
  starting transfers between devices  41.3 us (30%)
  Pallas kernels  35.3 us (26%)
  local copies, waits for them, and re-layouts  7.74 us (6%)
  between operations  1.51 us (1%)
    ppermute x4, waiting for transfers between devices, rows_on(): lax.ppermute(x, 'tile', [(i, (i // 8 + d) % 4 * 8 + i % 8) for i in range...  17.6 us
    ppermute x6, waiting for transfers between devices, x_on(): lax.ppermute(x, 'head', [(i, i // 4 * 4 + (i + d) % 4) for i in range(8)])  11.9 us
    ppermute x6, starting transfers between devices, x_on(): lax.ppermute(x, 'head', [(i, i // 4 * 4 + (i + d) % 4) for i in range(8)])  11.1 us
    pallas_call x1, Pallas kernels, early(): pl.pallas_call(early_kernel, out_shape=(part, part, part), in_specs=[SM,...  11 us
    all_to_all x1, starting transfers between devices, per_device(): every = lax.all_to_all(text, 'tile', 0, 0, tiled=True).reshape(TEXT, 3 * W)  10.6 us
    ppermute x1, waiting for transfers between devices, z_pair(): return lax.ppermute(x, 'head', [(i, i ^ 4) for i in range(8)])  10.3 us
    unnamed x32, local copies, waits for them, and re-layouts  7.74 us
    pallas_call x1, Pallas kernels, late(): pl.pallas_call(late_kernel, grid=(NH,), out_shape=jax.ShapeDtypeStruct((4...  6.98 us
  transfers between devices with their start and end apart: 18, of which 6 were waited for; matrix products, arithmetic and copies ran while one was open for 0% of the time, Pallas kernels for 21%

profile of v2, /device:TPU:32, one launch (start us, length us, event | category | flops | bytes accessed | tf_op | source)
XLA Modules:
  0.0 135.0 jit_solution(5112507788183090742)
XLA Ops:
  0.6 2.2 %pack.1 = (bf16[1024,384]{1,0:T(8,128)(2,1)}, bf16[32,8,1152]{2,1,0:T(8,128)(2,1)}) custom-call(bf16[512,384]{1,0:T(8,128)(2,1)} %k_ref.1, bf16[512,384]{1,0:T(8,128)(2,1)} %v_ref.1, bf16[8,384]{1,0:T(8,128)(2,1)} %tq_ref.3, bf16[8,384]{1,0:T(8,128)(2,1)} %tk_ref.1, bf16[8,384]{1,0:T(8,128)(2,1)} %tv_ref.1), custom_call_target="tpu_custom_call" | custom-call | flops 1 | bytes 1 | tf_op jit(solution)/shard_map/pack/pallas_call | solution.py:363
  2.9 10.6 %all-to-all-start = ((bf16[32,8,1152]{2,1,0:T(8,128)(2,1)}), bf16[32,8,1152]{2,1,0:T(8,128)(2,1)S(1)}, u32[]{:S(2)}, u32[]{:S(2)}) async-start(bf16[32,8,1152]{2,1,0:T(8,128)(2,1)} %get-tuple-element.18), calls=%async_computation | async-start | bytes 1179648 | tf_op jit(solution)/shard_map/all_to_all | solution.py:472
  13.5 1.9 %collective-permute-start.3 = (bf16[1024,384]{1,0:T(8,128)(2,1)}, bf16[1024,384]{1,0:T(8,128)(2,1)S(1)}, u32[]{:S(2)}, u32[]{:S(2)}) collective-permute-start(bf16[1024,384]{1,0:T(8,128)(2,1)} %get-tuple-element.17.b0.kv_ref), channel_id=1, source_target_pairs={{0,64},{8,72},{16,80},{24,88},{32,96},{40,104},{48,112},{56,120},{... | collective-permute-start | bytes 2359304 | tf_op jit(solution)/shard_map/ppermute | solution.py:38
  15.4 1.4 %collective-permute-start.4 = (bf16[1024,384]{1,0:T(8,128)(2,1)}, bf16[1024,384]{1,0:T(8,128)(2,1)S(1)}, u32[]{:S(2)}, u32[]{:S(2)}) collective-permute-start(bf16[1024,384]{1,0:T(8,128)(2,1)} %get-tuple-element.17.b0.kv_ref), channel_id=1, source_target_pairs={{0,192},{8,200},{16,208},{24,216},{32,224},{40,232},{48,240},{56,2... | collective-permute-start | bytes 2359304 | tf_op jit(solution)/shard_map/ppermute | solution.py:38
  16.8 3.1 %collective-permute-start = (bf16[1024,384]{1,0:T(8,128)(2,1)}, bf16[1024,384]{1,0:T(8,128)(2,1)}, u32[]{:S(2)}, u32[]{:S(2)}) collective-permute-start(bf16[1024,384]{1,0:T(8,128)(2,1)} %get-tuple-element.17.b0.kv_ref), channel_id=1, source_target_pairs={{0,56},{8,16},{16,8},{24,32},{32,24},{40,48},{48,40},{56,0},{64,12... | collective-permute-start | bytes 2359304 | tf_op jit(solution)/shard_map/ppermute | solution.py:42
  19.9 3.3 %split_proj.1 = (bf16[384,768]{1,0:T(8,128)(2,1)}, bf16[384,768]{1,0:T(8,128)(2,1)}, bf16[384,768]{1,0:T(8,128)(2,1)}, bf16[384,768]{1,0:T(8,128)(2,1)}) custom-call(bf16[384,3072]{1,0:T(8,128)(2,1)} %proj_ref.2), custom_call_target="tpu_custom_call" | custom-call | flops 1 | bytes 1 | tf_op jit(solution)/shard_map/split_proj/pallas_call | solution.py:327
  23.2 17.6 %collective-permute-done.3.x_ref = bf16[1024,384]{1,0:T(8,128)(2,1)S(1)} collective-permute-done((bf16[1024,384]{1,0:T(8,128)(2,1)}, bf16[1024,384]{1,0:T(8,128)(2,1)S(1)}, u32[]{:S(2)}, u32[]{:S(2)}) %collective-permute-start.3) | collective-permute-done | bytes 786464 | tf_op jit(solution)/shard_map/ppermute | solution.py:38
  40.8 0.9 copy-done.12
  41.9 0.9 copy-done.11
  43.4 4.7 %collective-permute-done.b0 = bf16[1024,384]{1,0:T(8,128)(2,1)} collective-permute-done((bf16[1024,384]{1,0:T(8,128)(2,1)}, bf16[1024,384]{1,0:T(8,128)(2,1)}, u32[]{:S(2)}, u32[]{:S(2)}) %collective-permute-start) | collective-permute-done | bytes 786464 | tf_op jit(solution)/shard_map/ppermute | solution.py:42
  48.1 1.5 %collective-permute-start.1 = (bf16[1024,384]{1,0:T(8,128)(2,1)}, bf16[1024,384]{1,0:T(8,128)(2,1)S(1)}, u32[]{:S(2)}, u32[]{:S(2)}) collective-permute-start(bf16[1024,384]{1,0:T(8,128)(2,1)} %collective-permute-done.b0), channel_id=1, source_target_pairs={{0,64},{8,72},{16,80},{24,88},{32,96},{40,104},{48,112},{56,120},{... | collective-permute-start | bytes 2359304 | tf_op jit(solution)/shard_map/ppermute | solution.py:38
  49.6 1.8 %collective-permute-start.2 = (bf16[1024,384]{1,0:T(8,128)(2,1)}, bf16[1024,384]{1,0:T(8,128)(2,1)S(1)}, u32[]{:S(2)}, u32[]{:S(2)}) collective-permute-start(bf16[1024,384]{1,0:T(8,128)(2,1)} %collective-permute-done.b0), channel_id=1, source_target_pairs={{0,192},{8,200},{16,208},{24,216},{32,224},{40,232},{48,240},{56,2... | collective-permute-start | bytes 2359304 | tf_op jit(solution)/shard_map/ppermute | solution.py:38
  51.3 2.8 %collective-permute-start.10 = (bf16[384,768]{1,0:T(8,128)(2,1)}, bf16[384,768]{1,0:T(8,128)(2,1)S(1)}, u32[]{:S(2)}, u32[]{:S(2)}) collective-permute-start(bf16[384,768]{1,0:T(8,128)(2,1)} %get-tuple-element.25), channel_id=1, source_target_pairs={{0,3},{1,0},{2,1},{3,2},{4,7},{5,4},{6,5},{7,6},{8,11},{9,8},{10,9... | collective-permute-start | bytes 1769480 | tf_op jit(solution)/shard_map/ppermute | solution.py:57
  54.1 0.9 copy-done.15
  55.0 2.3 %collective-permute-start.9 = (bf16[384,768]{1,0:T(8,128)(2,1)}, bf16[384,768]{1,0:T(8,128)(2,1)S(1)}, u32[]{:S(2)}, u32[]{:S(2)}) collective-permute-start(bf16[384,768]{1,0:T(8,128)(2,1)} %get-tuple-element.24), channel_id=1, source_target_pairs={{0,2},{1,3},{2,0},{3,1},{4,6},{5,7},{6,4},{7,5},{8,10},{9,11},{10,... | collective-permute-start | bytes 1769480 | tf_op jit(solution)/shard_map/ppermute | solution.py:57
  57.9 3.2 %text_part.1 = bf16[256,512]{1,0:T(8,128)(2,1)} custom-call(bf16[256,1152]{1,0:T(8,128)(2,1)} %bitcast.5, bf16[1024,384]{1,0:T(8,128)(2,1)} %get-tuple-element.17.b0.kv_ref), custom_call_target="tpu_custom_call" | custom-call | flops 1 | bytes 1 | tf_op jit(solution)/shard_map/text_part/pallas_call | solution.py:262
  61.1 11.0 %early.1 = (f32[512,384]{1,0:T(8,128)}, f32[512,384]{1,0:T(8,128)}, f32[512,384]{1,0:T(8,128)}) custom-call(s32[2,27]{1,0:T(2,128)} %wm.3, s32[1]{0:T(128)S(6)} %copy.18.tlen, bf16[512,384]{1,0:T(8,128)(2,1)} %q_ref.3, bf16[256,1152]{1,0:T(8,128)(2,1)} %bitcast.6, bf16[1024,384]{1,0:T(8,128)(2,1)} %get-tuple-element.17.b0.kv_ref, ...), custom_call_target="tpu_custom_call" | custom-call | flops 1 | bytes 1 | tf_op jit(solution)/shard_map/early/pallas_call | solution.py:164
  72.2 0.9 copy-done.9
  73.3 5.3 %all-to-all-start.2 = ((bf16[32,8,512]{2,1,0:T(8,128)(2,1)}), bf16[32,8,512]{2,1,0:T(8,128)(2,1)S(1)}, u32[]{:S(2)}, u32[]{:S(2)}) async-start(bf16[32,8,512]{2,1,0:T(8,128)(2,1)} %after.5), calls=%async_computation.2 | async-start | bytes 524288 | tf_op jit(solution)/shard_map/all_to_all | solution.py:481
  79.8 7.0 %late.1 = bf16[4,512,384]{2,1,0:T(8,128)(2,1)} custom-call(s32[2,27]{1,0:T(2,128)} %wm.3, bf16[512,384]{1,0:T(8,128)(2,1)} %q_ref.3, bf16[1024,384]{1,0:T(8,128)(2,1)} %collective-permute-done.b0, bf16[1024,384]{1,0:T(8,128)(2,1)} %copy-done.9, bf16[1024,384]{1,0:T(8,128)(2,1)} %copy-done.10, f32[512,384]{1,0:T(8,128)} %get-tuple-element.20.acc_ref.rest_2_, ...), custom_call_target="tpu_custom_call" | custom-call | flops 1 | bytes 1 | tf_op jit(solution)/shard_map/late/pallas_call | solution.py:221
  86.8 4.7 %all-to-all-done.2 = bf16[32,8,512]{2,1,0:T(8,128)(2,1)S(1)} async-done(((bf16[32,8,512]{2,1,0:T(8,128)(2,1)}), bf16[32,8,512]{2,1,0:T(8,128)(2,1)S(1)}, u32[]{:S(2)}, u32[]{:S(2)}) %all-to-all-start.2) | async-done | bytes 262176 | tf_op jit(solution)/shard_map/all_to_all | solution.py:481
  92.2 3.6 %all-to-all-start.1 = ((bf16[4,512,384]{2,1,0:T(8,128)(2,1)}), bf16[4,512,384]{2,1,0:T(8,128)(2,1)S(1)}, u32[]{:S(2)}, u32[]{:S(2)}) async-start(bf16[4,512,384]{2,1,0:T(8,128)(2,1)} %late.1), calls=%async_computation.1 | async-start | bytes 3145728 | tf_op jit(solution)/shard_map/all_to_all | solution.py:53
  95.8 3.9 %text_merge.1 = (bf16[8,768]{1,0:T(8,128)(2,1)}, bf16[8,768]{1,0:T(8,128)(2,1)}, bf16[8,768]{1,0:T(8,128)(2,1)}, bf16[8,768]{1,0:T(8,128)(2,1)}) custom-call(s32[1]{0:T(128)S(6)} %copy.18.tlen, bf16[256,512]{1,0:T(8,128)(2,1)} %bitcast.9, bf16[8,384]{1,0:T(8,128)(2,1)} %tq_ref.3, bf16[256,1152]{1,0:T(8,128)(2,1)} %bitcast.7, bf16[384,3072]{1,0:T(8,128)(2,1)} %proj_ref.3), custom_call_target="tpu_custom_call" | custom-call | flops 1 | bytes 1 | tf_op jit(solution)/shard_map/text_merge/pallas_call | solution.py:307
  99.7 2.0 %collective-permute-start.11 = (bf16[8,768]{1,0:T(8,128)(2,1)}, bf16[8,768]{1,0:T(8,128)(2,1)S(1)}, u32[]{:S(2)}, u32[]{:S(2)}) collective-permute-start(bf16[8,768]{1,0:T(8,128)(2,1)} %get-tuple-element.27), channel_id=1, source_target_pairs={{0,1},{1,2},{2,3},{3,0},{4,5},{5,6},{6,7},{7,4},{8,9},{9,10},{10,1... | collective-permute-start | bytes 36872 | tf_op jit(solution)/shard_map/ppermute | solution.py:57
  101.7 2.7 %collective-permute-start.12 = (bf16[8,768]{1,0:T(8,128)(2,1)}, bf16[8,768]{1,0:T(8,128)(2,1)S(1)}, u32[]{:S(2)}, u32[]{:S(2)}) collective-permute-start(bf16[8,768]{1,0:T(8,128)(2,1)} %get-tuple-element.28), channel_id=1, source_target_pairs={{0,2},{1,3},{2,0},{3,1},{4,6},{5,7},{6,4},{7,5},{8,10},{9,11},{10,... | collective-permute-start | bytes 36872 | tf_op jit(solution)/shard_map/ppermute | solution.py:57
  104.3 1.5 %collective-permute-start.13 = (bf16[8,768]{1,0:T(8,128)(2,1)}, bf16[8,768]{1,0:T(8,128)(2,1)S(1)}, u32[]{:S(2)}, u32[]{:S(2)}) collective-permute-start(bf16[8,768]{1,0:T(8,128)(2,1)} %get-tuple-element.29), channel_id=1, source_target_pairs={{0,3},{1,0},{2,1},{3,2},{4,7},{5,4},{6,5},{7,6},{8,11},{9,8},{10,9... | collective-permute-start | bytes 36872 | tf_op jit(solution)/shard_map/ppermute | solution.py:57
  105.8 8.1 %collective-permute-done.11.t1 = bf16[8,768]{1,0:T(8,128)(2,1)S(1)} collective-permute-done((bf16[8,768]{1,0:T(8,128)(2,1)}, bf16[8,768]{1,0:T(8,128)(2,1)S(1)}, u32[]{:S(2)}, u32[]{:S(2)}) %collective-permute-start.11) | collective-permute-done | bytes 12320 | tf_op jit(solution)/shard_map/ppermute | solution.py:57
  113.9 3.8 %collective-permute-done.12.t2 = bf16[8,768]{1,0:T(8,128)(2,1)S(1)} collective-permute-done((bf16[8,768]{1,0:T(8,128)(2,1)}, bf16[8,768]{1,0:T(8,128)(2,1)S(1)}, u32[]{:S(2)}, u32[]{:S(2)}) %collective-permute-start.12) | collective-permute-done | bytes 12320 | tf_op jit(solution)/shard_map/ppermute | solution.py:57
  117.7 1.1 copy-done.6
  119.5 3.9 %project.1 = (f32[528,384]{1,0:T(8,128)S(1)}, bf16[528,384]{1,0:T(8,128)(2,1)S(1)}) custom-call(bf16[4,512,384]{2,1,0:T(8,128)(2,1)S(1)} %all-to-all-done.1.a_ref, bf16[384,768]{1,0:T(8,128)(2,1)S(1)} %copy-done, bf16[384,768]{1,0:T(8,128)(2,1)S(1)} %copy-done.4, bf16[384,768]{1,0:T(8,128)(2,1)S(1)} %copy-done.6, bf16[384,768]{1,0:T(8,128)(2,1)S(1)} %copy-done.2, ...), custom_call_target="tpu_custom_call" | custom-call | flops 1 | bytes 1 | tf_op jit(solution)/shard_map/project/pallas_call | solution.py:423
  124.0 10.3 %collective-permute-done.14.got_ref = bf16[528,384]{1,0:T(8,128)(2,1)S(1)} collective-permute-done((bf16[528,384]{1,0:T(8,128)(2,1)S(1)}, bf16[528,384]{1,0:T(8,128)(2,1)S(1)}, u32[]{:S(2)}, u32[]{:S(2)}) %collective-permute-start.14) | collective-permute-done | bytes 405536 | tf_op jit(solution)/shard_map/ppermute | solution.py:61
  134.2 0.8 add_up.1
  (47 shorter events, 4.2 us)
Async XLA Ops:
  2.9 37.9 %all-to-all-start = ((bf16[32,8,1152]{2,1,0:T(8,128)(2,1)}), bf16[32,8,1152]{2,1,0:T(8,128)(2,1)S(1)}, u32[]{:S(2)}, u32[]{:S(2)}) async-start(bf16[32,8,1152]{2,1,0:T(8,128)(2,1)} %get-tuple-element.18), calls=%async_computation | async-start | bytes 1179648 | tf_op jit(solution)/shard_map/all_to_all | solution.py:472
  13.5 27.3 %collective-permute-start.3 = (bf16[1024,384]{1,0:T(8,128)(2,1)}, bf16[1024,384]{1,0:T(8,128)(2,1)S(1)}, u32[]{:S(2)}, u32[]{:S(2)}) collective-permute-start(bf16[1024,384]{1,0:T(8,128)(2,1)} %get-tuple-element.17.b0.kv_ref), channel_id=1, source_target_pairs={{0,64},{8,72},{16,80},{24,88},{32,96},{40,104},{48,112},{56,120},{... | collective-permute-start | bytes 2359304 | tf_op jit(solution)/shard_map/ppermute | solution.py:38
  15.4 26.6 %collective-permute-start.4 = (bf16[1024,384]{1,0:T(8,128)(2,1)}, bf16[1024,384]{1,0:T(8,128)(2,1)S(1)}, u32[]{:S(2)}, u32[]{:S(2)}) collective-permute-start(bf16[1024,384]{1,0:T(8,128)(2,1)} %get-tuple-element.17.b0.kv_ref), channel_id=1, source_target_pairs={{0,192},{8,200},{16,208},{24,216},{32,224},{40,232},{48,240},{56,2... | collective-permute-start | bytes 2359304 | tf_op jit(solution)/shard_map/ppermute | solution.py:38
  16.8 31.3 %collective-permute-start = (bf16[1024,384]{1,0:T(8,128)(2,1)}, bf16[1024,384]{1,0:T(8,128)(2,1)}, u32[]{:S(2)}, u32[]{:S(2)}) collective-permute-start(bf16[1024,384]{1,0:T(8,128)(2,1)} %get-tuple-element.17.b0.kv_ref), channel_id=1, source_target_pairs={{0,56},{8,16},{16,8},{24,32},{32,24},{40,48},{48,40},{56,0},{64,12... | collective-permute-start | bytes 2359304 | tf_op jit(solution)/shard_map/ppermute | solution.py:42
  19.9 31.4 %collective-permute-start.5 = (bf16[1024,384]{1,0:T(8,128)(2,1)}, bf16[1024,384]{1,0:T(8,128)(2,1)S(1)}, u32[]{:S(2)}, u32[]{:S(2)}) collective-permute-start(bf16[1024,384]{1,0:T(8,128)(2,1)} %get-tuple-element.17.b0.kv_ref), channel_id=1, source_target_pairs={{0,8},{8,0},{16,24},{24,16},{32,40},{40,32},{48,56},{56,48},{64,72... | collective-permute-start | bytes 2359304 | tf_op jit(solution)/shard_map/ppermute | solution.py:48
  40.8 0.9 copy-start.12
  40.8 1.1 copy-start.8
  41.9 12.2 %collective-permute-start.6 = (bf16[1024,384]{1,0:T(8,128)(2,1)}, bf16[1024,384]{1,0:T(8,128)(2,1)}, u32[]{:S(2)}, u32[]{:S(2)}) collective-permute-start(bf16[1024,384]{1,0:T(8,128)(2,1)} %after.3.b1), channel_id=1, source_target_pairs={{0,8},{8,0},{16,24},{24,16},{32,40},{40,32},{48,56},{56,48},{64,72... | collective-permute-start | bytes 2359304 | tf_op jit(solution)/shard_map/ppermute | solution.py:48
  41.9 0.9 copy-start.11
  42.9 11.2 %collective-permute-start.7 = (bf16[1024,384]{1,0:T(8,128)(2,1)}, bf16[1024,384]{1,0:T(8,128)(2,1)S(1)}, u32[]{:S(2)}, u32[]{:S(2)}) collective-permute-start(bf16[1024,384]{1,0:T(8,128)(2,1)} %after.4.b2), channel_id=1, source_target_pairs={{0,8},{8,0},{16,24},{24,16},{32,40},{40,32},{48,56},{56,48},{64,72... | collective-permute-start | bytes 2359304 | tf_op jit(solution)/shard_map/ppermute | solution.py:48
  48.1 24.0 %collective-permute-start.1 = (bf16[1024,384]{1,0:T(8,128)(2,1)}, bf16[1024,384]{1,0:T(8,128)(2,1)S(1)}, u32[]{:S(2)}, u32[]{:S(2)}) collective-permute-start(bf16[1024,384]{1,0:T(8,128)(2,1)} %collective-permute-done.b0), channel_id=1, source_target_pairs={{0,64},{8,72},{16,80},{24,88},{32,96},{40,104},{48,112},{56,120},{... | collective-permute-start | bytes 2359304 | tf_op jit(solution)/shard_map/ppermute | solution.py:38
  49.6 22.6 %collective-permute-start.2 = (bf16[1024,384]{1,0:T(8,128)(2,1)}, bf16[1024,384]{1,0:T(8,128)(2,1)S(1)}, u32[]{:S(2)}, u32[]{:S(2)}) collective-permute-start(bf16[1024,384]{1,0:T(8,128)(2,1)} %collective-permute-done.b0), channel_id=1, source_target_pairs={{0,192},{8,200},{16,208},{24,216},{32,224},{40,232},{48,240},{56,2... | collective-permute-start | bytes 2359304 | tf_op jit(solution)/shard_map/ppermute | solution.py:38
  51.3 2.8 %copy-start.14 = (bf16[1024,384]{1,0:T(8,128)(2,1)}, bf16[1024,384]{1,0:T(8,128)(2,1)S(1)}, u32[]{:S(2)}) copy-start(bf16[1024,384]{1,0:T(8,128)(2,1)S(1)} %collective-permute-done.5.b3) | copy-start | bytes 2359300
  51.3 27.3 %collective-permute-start.10 = (bf16[384,768]{1,0:T(8,128)(2,1)}, bf16[384,768]{1,0:T(8,128)(2,1)S(1)}, u32[]{:S(2)}, u32[]{:S(2)}) collective-permute-start(bf16[384,768]{1,0:T(8,128)(2,1)} %get-tuple-element.25), channel_id=1, source_target_pairs={{0,3},{1,0},{2,1},{3,2},{4,7},{5,4},{6,5},{7,6},{8,11},{9,8},{10,9... | collective-permute-start | bytes 1769480 | tf_op jit(solution)/shard_map/ppermute | solution.py:57
  54.1 24.6 %collective-permute-start.8 = (bf16[384,768]{1,0:T(8,128)(2,1)}, bf16[384,768]{1,0:T(8,128)(2,1)S(1)}, u32[]{:S(2)}, u32[]{:S(2)}) collective-permute-start(bf16[384,768]{1,0:T(8,128)(2,1)} %get-tuple-element.23), channel_id=1, source_target_pairs={{0,1},{1,2},{2,3},{3,0},{4,5},{5,6},{6,7},{7,4},{8,9},{9,10},{10,1... | collective-permute-start | bytes 1769480 | tf_op jit(solution)/shard_map/ppermute | solution.py:57
  54.1 0.9 copy-start.15
  55.0 23.7 %collective-permute-start.9 = (bf16[384,768]{1,0:T(8,128)(2,1)}, bf16[384,768]{1,0:T(8,128)(2,1)S(1)}, u32[]{:S(2)}, u32[]{:S(2)}) collective-permute-start(bf16[384,768]{1,0:T(8,128)(2,1)} %get-tuple-element.24), channel_id=1, source_target_pairs={{0,2},{1,3},{2,0},{3,1},{4,6},{5,7},{6,4},{7,5},{8,10},{9,11},{10,... | collective-permute-start | bytes 1769480 | tf_op jit(solution)/shard_map/ppermute | solution.py:57
  72.1 0.9 copy-start.9
  72.1 1.2 copy-start.10
  73.3 18.2 %all-to-all-start.2 = ((bf16[32,8,512]{2,1,0:T(8,128)(2,1)}), bf16[32,8,512]{2,1,0:T(8,128)(2,1)S(1)}, u32[]{:S(2)}, u32[]{:S(2)}) async-start(bf16[32,8,512]{2,1,0:T(8,128)(2,1)} %after.5), calls=%async_computation.2 | async-start | bytes 524288 | tf_op jit(solution)/shard_map/all_to_all | solution.py:481
  78.6 0.8 copy-start.1
  78.7 1.0 copy-start.3
  78.7 1.2 copy-start.5
  92.2 25.5 %all-to-all-start.1 = ((bf16[4,512,384]{2,1,0:T(8,128)(2,1)}), bf16[4,512,384]{2,1,0:T(8,128)(2,1)S(1)}, u32[]{:S(2)}, u32[]{:S(2)}) async-start(bf16[4,512,384]{2,1,0:T(8,128)(2,1)} %late.1), calls=%async_computation.1 | async-start | bytes 3145728 | tf_op jit(solution)/shard_map/all_to_all | solution.py:53
  95.8 21.9 %copy-start = (bf16[384,768]{1,0:T(8,128)(2,1)S(1)}, bf16[384,768]{1,0:T(8,128)(2,1)}, u32[]{:S(2)}) copy-start(bf16[384,768]{1,0:T(8,128)(2,1)} %get-tuple-element.19.rest_1_.w0) | copy-start | bytes 1769476
  95.8 21.9 %copy-start.2 = (bf16[384,768]{1,0:T(8,128)(2,1)S(1)}, bf16[384,768]{1,0:T(8,128)(2,1)}, u32[]{:S(2)}) copy-start(bf16[384,768]{1,0:T(8,128)(2,1)} %copy-done.1) | copy-start | bytes 1769476
  95.8 21.9 %copy-start.4 = (bf16[384,768]{1,0:T(8,128)(2,1)S(1)}, bf16[384,768]{1,0:T(8,128)(2,1)}, u32[]{:S(2)}) copy-start(bf16[384,768]{1,0:T(8,128)(2,1)} %copy-done.3) | copy-start | bytes 1769476
  99.7 14.2 %collective-permute-start.11 = (bf16[8,768]{1,0:T(8,128)(2,1)}, bf16[8,768]{1,0:T(8,128)(2,1)S(1)}, u32[]{:S(2)}, u32[]{:S(2)}) collective-permute-start(bf16[8,768]{1,0:T(8,128)(2,1)} %get-tuple-element.27), channel_id=1, source_target_pairs={{0,1},{1,2},{2,3},{3,0},{4,5},{5,6},{6,7},{7,4},{8,9},{9,10},{10,1... | collective-permute-start | bytes 36872 | tf_op jit(solution)/shard_map/ppermute | solution.py:57
  101.7 16.0 %collective-permute-start.12 = (bf16[8,768]{1,0:T(8,128)(2,1)}, bf16[8,768]{1,0:T(8,128)(2,1)S(1)}, u32[]{:S(2)}, u32[]{:S(2)}) collective-permute-start(bf16[8,768]{1,0:T(8,128)(2,1)} %get-tuple-element.28), channel_id=1, source_target_pairs={{0,2},{1,3},{2,0},{3,1},{4,6},{5,7},{6,4},{7,5},{8,10},{9,11},{10,... | collective-permute-start | bytes 36872 | tf_op jit(solution)/shard_map/ppermute | solution.py:57
  104.3 13.4 %collective-permute-start.13 = (bf16[8,768]{1,0:T(8,128)(2,1)}, bf16[8,768]{1,0:T(8,128)(2,1)S(1)}, u32[]{:S(2)}, u32[]{:S(2)}) collective-permute-start(bf16[8,768]{1,0:T(8,128)(2,1)} %get-tuple-element.29), channel_id=1, source_target_pairs={{0,3},{1,0},{2,1},{3,2},{4,7},{5,4},{6,5},{7,6},{8,11},{9,8},{10,9... | collective-permute-start | bytes 36872 | tf_op jit(solution)/shard_map/ppermute | solution.py:57
  117.7 1.1 copy-start.6
  123.4 10.8 %collective-permute-start.14 = (bf16[528,384]{1,0:T(8,128)(2,1)S(1)}, bf16[528,384]{1,0:T(8,128)(2,1)S(1)}, u32[]{:S(2)}, u32[]{:S(2)}) collective-permute-start(bf16[528,384]{1,0:T(8,128)(2,1)S(1)} %get-tuple-element.31), channel_id=1, source_target_pairs={{0,4},{1,5},{2,6},{3,7},{4,0},{5,1},{6,2},{7,3},{8,12},{9,13},{10,... | collective-permute-start | bytes 1216520 | tf_op jit(solution)/shard_map/ppermute | solution.py:61
  (2 other events, 1.4 us)

commit v3 on v2

--- a/solution.py
+++ b/solution.py
@@ -16,6 +16,7 @@
 TL = 8
 ROWS = 2 * TT
 SCALE = math.log2(math.e) / math.sqrt(HD)
+HALF = W // 2
 BIG = 1e30
 F32 = jnp.float32
 BF16 = jnp.bfloat16
@@ -316,23 +317,24 @@
     )(tlen, msg, tq, every, proj)
 
 
-def split_kernel(proj_ref, *rest):
-    x = lax.rem(lax.axis_index("head"), 4)
-    for d, out in enumerate(rest[-4:]):
+def split_kernel(proj_ref, after_ref, out_ref):
+    core = lax.rem(lax.axis_index("tile"), 2)
+    mine = pl.ds(pl.multiple_of(core * HALF, 16), HALF)
+    for xd in range(4):
         for j in range(2):
-            out[:, j * W : (j + 1) * W] = proj_ref[:, columns(lax.rem(x + d, 4), j)]
-
-
-def split_proj(proj, *deps):
+            out_ref[xd, :, j * W : (j + 1) * W] = proj_ref[mine, columns(xd, j)]
+
+
+def split_proj(proj, after_this):
     return pl.pallas_call(
         split_kernel,
-        out_shape=(jax.ShapeDtypeStruct((W, 2 * W), BF16),) * 4,
-        in_specs=[VM] + [ANY] * len(deps),
-        out_specs=(VM,) * 4,
+        out_shape=jax.ShapeDtypeStruct((4, HALF, 2 * W), BF16),
+        in_specs=[VM, ANY],
+        out_specs=VM,
         compiler_params=params(60),
         cost_estimate=cost(0, 5 * 2**20),
         name="split_proj",
-    )(proj, *deps)
+    )(proj, after_this)
 
 
 def pack_kernel(k_ref, v_ref, tq_ref, tk_ref, tv_ref, kv_ref, t_ref, buf, sem):
@@ -393,21 +395,26 @@
 
 
 def project_kernel(
-    a_ref, w0, w1, w2, w3, t0, t1, t2, t3, own_ref, away_ref, abuf, wbuf, acc, sem
+    a_ref, w_ref, v_ref, t0, t1, t2, t3, own_ref, away_ref, abuf, wbuf, acc, sem
 ):
-    me = lax.rem(lax.axis_index("head"), 4)
+    core = lax.rem(lax.axis_index("tile"), 2)
     copies = []
-    for x, w_ref in enumerate((w0, w1, w2, w3)):
-        a_at = a_ref.at[lax.rem(me + 4 - x, 4)]
-        for i, (src, dst) in enumerate(((w_ref, wbuf), (a_at, abuf))):
-            copies.append(pltpu.make_async_copy(src, dst.at[x], sem.at[2 * x + i]))
+    for x in range(4):
+        for i, (src, dst) in enumerate(
+            (
+                (w_ref, wbuf.at[x, pl.ds(pl.multiple_of(core * HALF, 16), HALF)]),
+                (v_ref, wbuf.at[x, pl.ds(pl.multiple_of((1 - core) * HALF, 16), HALF)]),
+                (a_ref, abuf.at[x]),
+            )
+        ):
+            copies.append(pltpu.make_async_copy(src.at[x], dst, sem.at[3 * x + i]))
             copies[-1].start()
     t = sum(r[...].astype(F32) for r in (t0, t1, t2, t3))
     t = jnp.concatenate([t, jnp.zeros_like(t)], axis=0)
     own_ref[pl.ds(ROWS, 16), :] = t[:, :W]
     away_ref[pl.ds(ROWS, 16), :] = t[:, W:].astype(BF16)
     for x in range(4):
-        for c in copies[2 * x : 2 * x + 2]:
+        for c in copies[3 * x : 3 * x + 3]:
             c.wait()
         o = jnp.dot(abuf[x], wbuf[x], preferred_element_type=F32)
         if x > 0:
@@ -426,13 +433,13 @@
             jax.ShapeDtypeStruct((ROWS + 16, W), F32),
             jax.ShapeDtypeStruct((ROWS + 16, W), BF16),
         ),
-        in_specs=[ANY] * 5 + [VM] * 4,
+        in_specs=[ANY] * 3 + [VM] * 4,
         out_specs=(VM, VM),
         scratch_shapes=[
             pltpu.VMEM((4, ROWS, W), BF16),
             pltpu.VMEM((4, W, 2 * W), BF16),
             pltpu.VMEM((ROWS, 2 * W), F32),
-            pltpu.SemaphoreType.DMA((8,)),
+            pltpu.SemaphoreType.DMA((12,)),
         ],
         compiler_params=params(24),
         cost_estimate=cost(2 * ROWS * 4 * W * 2 * W, 6 * 2**20),
@@ -467,23 +474,23 @@
     dn = rows_on(kv, -1)
     side = other_core(kv)
 
-    proj = split_proj(video_proj)
-    proj = [x_on(p, d) if d else p for d, p in enumerate(proj)]
     every = lax.all_to_all(text, "tile", 0, 0, tiled=True).reshape(TEXT, 3 * W)
     far_up, far_dn = rows_on(far, 1), rows_on(far, -1)
-    up, dn = after(up, every, proj[0]), after(dn, every, proj[0])
+    msg = text_part(every, kv)
+    pieces = split_proj(video_proj, msg)
+    proj = x_swap(pieces)
+    up, dn = after(up, msg, pieces), after(dn, msg, pieces)
     side_up, side_dn = other_core(up), other_core(dn)
     acc, m, l = early(
         window_mask, text_length, video_q, every, (kv, up, dn, side, side_up, side_dn)
     )
-    msg = text_part(every, kv).reshape(32, TL, W + HD)
-    msg = after(msg, far_up, far_dn, acc)
+    msg = after(msg.reshape(32, TL, W + HD), acc)
     got = lax.all_to_all(msg, "tile", 0, 0, tiled=True).reshape(TEXT, W + HD)
 
-    attn = x_swap(late(window_mask, video_q, (far, far_up, far_dn), acc, m, l, *proj[1:]))
+    attn = x_swap(late(window_mask, video_q, (far, far_up, far_dn), acc, m, l))
     parts = text_merge(text_length, got, text_q, every, text_proj)
     parts = [x_on(p, d) if d else p for d, p in enumerate(parts)]
-    own, away = project(attn, proj, parts)
+    own, away = project(attn, (proj, other_core(proj)), parts)
     return add_up(own, z_pair(away))
 
 

time: 136 us -> 128 us (0.941)
  waiting for transfers between devices: 49.2 us -> 43.5 us
  local copies, waits for them, and re-layouts: 7.74 us -> 5.85 us
    ppermute x4, waiting for transfers between devices: 17.6 us -> 0.01 us  [rows_on(): lax.ppermute(x, 'tile', [(i, (i // 8 + d) % 4 * 8 + i % 8) for i in range...]
    all_to_all x1, waiting for transfers between devices: 0.01 us -> 15.3 us  [per_device(): every = lax.all_to_all(text, 'tile', 0, 0, tiled=True).reshape(TEXT, 3 * W)]
    ppermute x6 -> x3, starting transfers between devices: 11.1 us -> 5.39 us  [x_on(): lax.ppermute(x, 'head', [(i, i // 4 * 4 + (i + d) % 4) for i in range(8)])]
    all_to_all x1 -> x2, starting transfers between devices: 3.56 us -> 8.94 us  [x_swap(): return lax.all_to_all(x, 'head', 0, 0, tiled=True, axis_index_groups=groups)]
    ppermute x1, waiting for transfers between devices: 4.72 us -> 0.01 us  [over_chip(): lax.ppermute(x, 'tile', [(i, i // 8 * 8 + (i % 8 + (1 if i % 2 else -1))...]
    ppermute x3 -> x4, starting transfers between devices: 0.51 us -> 2.45 us  [other_core(): return lax.ppermute(x, 'tile', [(i, i ^ 1) for i in range(32)])]
    unnamed x32 -> x16, local copies, waits for them, and re-layouts: 7.74 us -> 5.85 us
    ppermute x6 -> x3, waiting for transfers between devices: 11.9 us -> 12.4 us  [x_on(): lax.ppermute(x, 'head', [(i, i // 4 * 4 + (i + d) % 4) for i in range(8)])]
  transfers between devices with their start and end apart: 18 -> 17, of which waited for: 6 -> 4; matrix products, arithmetic and copies ran while one was open for 0% -> 0% of each run, Pallas kernels for 21% -> 22%
where the time goes in v3:
time: 128 us; the launch traced here: 127 us
  waiting for transfers between devices  43.5 us (34%)
  starting transfers between devices  41.8 us (33%)
  Pallas kernels  34.5 us (27%)
  local copies, waits for them, and re-layouts  5.85 us (5%)
  between operations  1.44 us (1%)
    all_to_all x1, waiting for transfers between devices, per_device(): every = lax.all_to_all(text, 'tile', 0, 0, tiled=True).reshape(TEXT, 3 * W)  15.3 us
    ppermute x3, waiting for transfers between devices, x_on(): lax.ppermute(x, 'head', [(i, i // 4 * 4 + (i + d) % 4) for i in range(8)])  12.4 us
    pallas_call x1, Pallas kernels, early(): pl.pallas_call(early_kernel, out_shape=(part, part, part), in_specs=[SM,...  11 us
    all_to_all x1, starting transfers between devices, per_device(): every = lax.all_to_all(text, 'tile', 0, 0, tiled=True).reshape(TEXT, 3 * W)  10.6 us
    ppermute x1, waiting for transfers between devices, z_pair(): return lax.ppermute(x, 'head', [(i, i ^ 4) for i in range(8)])  10.5 us
    all_to_all x2, starting transfers between devices, x_swap(): return lax.all_to_all(x, 'head', 0, 0, tiled=True, axis_index_groups=groups)  8.94 us
    pallas_call x1, Pallas kernels, late(): pl.pallas_call(late_kernel, grid=(NH,), out_shape=jax.ShapeDtypeStruct((4...  6.98 us
    ppermute x4, starting transfers between devices, rows_on(): lax.ppermute(x, 'tile', [(i, (i // 8 + d) % 4 * 8 + i % 8) for i in range...  6.36 us
  transfers between devices with their start and end apart: 17, of which 4 were waited for; matrix products, arithmetic and copies ran while one was open for 0% of the time, Pallas kernels for 22%

profile of v3, /device:TPU:32, one launch (start us, length us, event | category | flops | bytes accessed | tf_op | source)
XLA Modules:
  0.0 127.1 jit_solution(12070176582641067690)
XLA Ops:
  0.6 2.3 %pack.1 = (bf16[1024,384]{1,0:T(8,128)(2,1)}, bf16[32,8,1152]{2,1,0:T(8,128)(2,1)}) custom-call(bf16[512,384]{1,0:T(8,128)(2,1)} %k_ref.1, bf16[512,384]{1,0:T(8,128)(2,1)} %v_ref.1, bf16[8,384]{1,0:T(8,128)(2,1)} %tq_ref.3, bf16[8,384]{1,0:T(8,128)(2,1)} %tk_ref.1, bf16[8,384]{1,0:T(8,128)(2,1)} %tv_ref.1), custom_call_target="tpu_custom_call" | custom-call | flops 1 | bytes 1 | tf_op jit(solution)/shard_map/pack/pallas_call | solution.py:365
  2.9 10.6 %all-to-all-start = ((bf16[32,8,1152]{2,1,0:T(8,128)(2,1)}), bf16[32,8,1152]{2,1,0:T(8,128)(2,1)S(1)}, u32[]{:S(2)}, u32[]{:S(2)}) async-start(bf16[32,8,1152]{2,1,0:T(8,128)(2,1)} %get-tuple-element.14), calls=%async_computation | async-start | bytes 1179648 | tf_op jit(solution)/shard_map/all_to_all | solution.py:477
  13.5 3.1 %collective-permute-start.4 = (bf16[1024,384]{1,0:T(8,128)(2,1)}, bf16[1024,384]{1,0:T(8,128)(2,1)S(1)}, u32[]{:S(2)}, u32[]{:S(2)}) collective-permute-start(bf16[1024,384]{1,0:T(8,128)(2,1)} %get-tuple-element.13.kv_ref.b0), channel_id=1, source_target_pairs={{0,192},{8,200},{16,208},{24,216},{32,224},{40,232},{48,240},{56,2... | collective-permute-start | bytes 2359304 | tf_op jit(solution)/shard_map/ppermute | solution.py:39
  16.6 3.1 %collective-permute-start = (bf16[1024,384]{1,0:T(8,128)(2,1)}, bf16[1024,384]{1,0:T(8,128)(2,1)}, u32[]{:S(2)}, u32[]{:S(2)}) collective-permute-start(bf16[1024,384]{1,0:T(8,128)(2,1)} %get-tuple-element.13.kv_ref.b0), channel_id=1, source_target_pairs={{0,56},{8,16},{16,8},{24,32},{32,24},{40,48},{48,40},{56,0},{64,12... | collective-permute-start | bytes 2359304 | tf_op jit(solution)/shard_map/ppermute | solution.py:43
  19.7 15.3 %all-to-all-done = bf16[32,8,1152]{2,1,0:T(8,128)(2,1)S(1)} async-done(((bf16[32,8,1152]{2,1,0:T(8,128)(2,1)}), bf16[32,8,1152]{2,1,0:T(8,128)(2,1)S(1)}, u32[]{:S(2)}, u32[]{:S(2)}) %all-to-all-start) | async-done | bytes 589856 | tf_op jit(solution)/shard_map/all_to_all | solution.py:477
  35.0 0.8 copy-done.1
  35.8 3.1 %text_part.1.after_ref.rest_0_ = bf16[256,512]{1,0:T(8,128)(2,1)} custom-call(bf16[256,1152]{1,0:T(8,128)(2,1)} %bitcast.3, bf16[1024,384]{1,0:T(8,128)(2,1)} %get-tuple-element.13.kv_ref.b0), custom_call_target="tpu_custom_call" | custom-call | flops 1 | bytes 1 | tf_op jit(solution)/shard_map/text_part/pallas_call | solution.py:263
  39.0 2.8 %split_proj.1.rest_1_ = bf16[4,192,768]{2,1,0:T(8,128)(2,1)} custom-call(bf16[384,3072]{1,0:T(8,128)(2,1)} %proj_ref.2, bf16[256,512]{1,0:T(8,128)(2,1)} %text_part.1.after_ref.rest_0_), custom_call_target="tpu_custom_call" | custom-call | flops 1 | bytes 1 | tf_op jit(solution)/shard_map/split_proj/pallas_call | solution.py:329
  41.8 4.4 %all-to-all-start.2 = ((bf16[4,192,768]{2,1,0:T(8,128)(2,1)}), bf16[4,192,768]{2,1,0:T(8,128)(2,1)S(1)}, u32[]{:S(2)}, u32[]{:S(2)}) async-start(bf16[4,192,768]{2,1,0:T(8,128)(2,1)} %split_proj.1.rest_1_), calls=%async_computation.2 | async-start | bytes 2359296 | tf_op jit(solution)/shard_map/all_to_all | solution.py:54
  46.2 1.8 %collective-permute-start.5 = (bf16[1024,384]{1,0:T(8,128)(2,1)S(1)}, bf16[1024,384]{1,0:T(8,128)(2,1)}, u32[]{:S(2)}, u32[]{:S(2)}) collective-permute-start(bf16[1024,384]{1,0:T(8,128)(2,1)S(1)} %copy-done.2), channel_id=1, source_target_pairs={{0,8},{8,0},{16,24},{24,16},{32,40},{40,32},{48,56},{56,48},{64,72... | collective-permute-start | bytes 2359304 | tf_op jit(solution)/shard_map/ppermute | solution.py:49
  48.0 0.9 copy-done.4
  48.9 0.9 copy-done.3
  49.8 0.5 collective-permute-start.6
  50.4 3.2 %collective-permute-start.2 = (bf16[1024,384]{1,0:T(8,128)(2,1)}, bf16[1024,384]{1,0:T(8,128)(2,1)}, u32[]{:S(2)}, u32[]{:S(2)}) collective-permute-start(bf16[1024,384]{1,0:T(8,128)(2,1)} %collective-permute-done.b0), channel_id=1, source_target_pairs={{0,192},{8,200},{16,208},{24,216},{32,224},{40,232},{48,240},{56,2... | collective-permute-start | bytes 2359304 | tf_op jit(solution)/shard_map/ppermute | solution.py:39
  54.3 0.9 copy-done.6
  55.2 0.9 copy-done.7
  56.1 11.0 %early.1 = (f32[512,384]{1,0:T(8,128)}, f32[512,384]{1,0:T(8,128)}, f32[512,384]{1,0:T(8,128)}) custom-call(s32[2,27]{1,0:T(2,128)} %wm.3, s32[1]{0:T(128)S(6)} %copy.18.tlen, bf16[512,384]{1,0:T(8,128)(2,1)} %q_ref.3, bf16[256,1152]{1,0:T(8,128)(2,1)} %bitcast.4, bf16[1024,384]{1,0:T(8,128)(2,1)} %get-tuple-element.13.kv_ref.b0, ...), custom_call_target="tpu_custom_call" | custom-call | flops 1 | bytes 1 | tf_op jit(solution)/shard_map/early/pallas_call | solution.py:165
  67.1 4.9 %all-to-all-start.3 = ((bf16[32,8,512]{2,1,0:T(8,128)(2,1)}), bf16[32,8,512]{2,1,0:T(8,128)(2,1)S(1)}, u32[]{:S(2)}, u32[]{:S(2)}) async-start(bf16[32,8,512]{2,1,0:T(8,128)(2,1)} %after.5), calls=%async_computation.3 | async-start | bytes 524288 | tf_op jit(solution)/shard_map/all_to_all | solution.py:488
  72.0 7.0 %late.1 = bf16[4,512,384]{2,1,0:T(8,128)(2,1)} custom-call(s32[2,27]{1,0:T(2,128)} %wm.3, bf16[512,384]{1,0:T(8,128)(2,1)} %q_ref.3, bf16[1024,384]{1,0:T(8,128)(2,1)} %collective-permute-done.b0, bf16[1024,384]{1,0:T(8,128)(2,1)} %collective-permute-done.1.b1, bf16[1024,384]{1,0:T(8,128)(2,1)} %collective-permute-done.2.b2, ...), custom_call_target="tpu_custom_call" | custom-call | flops 1 | bytes 1 | tf_op jit(solution)/shard_map/late/pallas_call | solution.py:222
  79.0 5.4 %all-to-all-done.3 = bf16[32,8,512]{2,1,0:T(8,128)(2,1)S(1)} async-done(((bf16[32,8,512]{2,1,0:T(8,128)(2,1)}), bf16[32,8,512]{2,1,0:T(8,128)(2,1)S(1)}, u32[]{:S(2)}, u32[]{:S(2)}) %all-to-all-start.3) | async-done | bytes 262176 | tf_op jit(solution)/shard_map/all_to_all | solution.py:488
  84.3 0.7 copy-done.5
  85.0 4.5 %all-to-all-start.1 = ((bf16[4,512,384]{2,1,0:T(8,128)(2,1)}), bf16[4,512,384]{2,1,0:T(8,128)(2,1)S(1)}, u32[]{:S(2)}, u32[]{:S(2)}) async-start(bf16[4,512,384]{2,1,0:T(8,128)(2,1)} %late.1), calls=%async_computation.1 | async-start | bytes 3145728 | tf_op jit(solution)/shard_map/all_to_all | solution.py:54
  89.6 0.2 collective-permute-start.8
  89.7 3.8 %text_merge.1 = (bf16[8,768]{1,0:T(8,128)(2,1)}, bf16[8,768]{1,0:T(8,128)(2,1)}, bf16[8,768]{1,0:T(8,128)(2,1)}, bf16[8,768]{1,0:T(8,128)(2,1)}) custom-call(s32[1]{0:T(128)S(6)} %copy.18.tlen, bf16[256,512]{1,0:T(8,128)(2,1)} %bitcast.7, bf16[8,384]{1,0:T(8,128)(2,1)} %tq_ref.3, bf16[256,1152]{1,0:T(8,128)(2,1)} %bitcast.5, bf16[384,3072]{1,0:T(8,128)(2,1)} %proj_ref.3), custom_call_target="tpu_custom_call" | custom-call | flops 1 | bytes 1 | tf_op jit(solution)/shard_map/text_merge/pallas_call | solution.py:308
  93.5 3.4 %collective-permute-start.10 = (bf16[8,768]{1,0:T(8,128)(2,1)}, bf16[8,768]{1,0:T(8,128)(2,1)S(1)}, u32[]{:S(2)}, u32[]{:S(2)}) collective-permute-start(bf16[8,768]{1,0:T(8,128)(2,1)} %get-tuple-element.20), channel_id=1, source_target_pairs={{0,2},{1,3},{2,0},{3,1},{4,6},{5,7},{6,4},{7,5},{8,10},{9,11},{10,... | collective-permute-start | bytes 36872 | tf_op jit(solution)/shard_map/ppermute | solution.py:58
  96.9 1.2 collective-permute-start.11
  98.1 0.9 collective-permute-start.9
  98.9 12.4 %collective-permute-done.10.t2 = bf16[8,768]{1,0:T(8,128)(2,1)S(1)} collective-permute-done((bf16[8,768]{1,0:T(8,128)(2,1)}, bf16[8,768]{1,0:T(8,128)(2,1)S(1)}, u32[]{:S(2)}, u32[]{:S(2)}) %collective-permute-start.10) | collective-permute-done | bytes 12320 | tf_op jit(solution)/shard_map/ppermute | solution.py:58
  111.3 0.7 copy-done
  112.0 3.7 %project.1 = (f32[528,384]{1,0:T(8,128)S(1)}, bf16[528,384]{1,0:T(8,128)(2,1)S(1)}) custom-call(bf16[4,512,384]{2,1,0:T(8,128)(2,1)S(1)} %all-to-all-done.1.a_ref, bf16[4,192,768]{2,1,0:T(8,128)(2,1)S(1)} %all-to-all-done.2.w_ref, bf16[4,192,768]{2,1,0:T(8,128)(2,1)} %collective-permute-done.8.v_ref, bf16[8,768]{1,0:T(8,128)(2,1)S(1)} %copy-done, ...), custom_call_target="tpu_custom_call" | custom-call | flops 1 | bytes 1 | tf_op jit(solution)/shard_map/project/pallas_call | solution.py:430
  115.8 10.5 %collective-permute-done.12.got_ref = bf16[528,384]{1,0:T(8,128)(2,1)S(1)} collective-permute-done((bf16[528,384]{1,0:T(8,128)(2,1)S(1)}, bf16[528,384]{1,0:T(8,128)(2,1)S(1)}, u32[]{:S(2)}, u32[]{:S(2)}) %collective-permute-start.12) | collective-permute-done | bytes 405536 | tf_op jit(solution)/shard_map/ppermute | solution.py:62
  126.3 0.8 add_up.1
  (29 shorter events, 0.2 us)
Async XLA Ops:
  2.9 32.1 %all-to-all-start = ((bf16[32,8,1152]{2,1,0:T(8,128)(2,1)}), bf16[32,8,1152]{2,1,0:T(8,128)(2,1)S(1)}, u32[]{:S(2)}, u32[]{:S(2)}) async-start(bf16[32,8,1152]{2,1,0:T(8,128)(2,1)} %get-tuple-element.14), calls=%async_computation | async-start | bytes 1179648 | tf_op jit(solution)/shard_map/all_to_all | solution.py:477
  13.5 34.5 %collective-permute-start.4 = (bf16[1024,384]{1,0:T(8,128)(2,1)}, bf16[1024,384]{1,0:T(8,128)(2,1)S(1)}, u32[]{:S(2)}, u32[]{:S(2)}) collective-permute-start(bf16[1024,384]{1,0:T(8,128)(2,1)} %get-tuple-element.13.kv_ref.b0), channel_id=1, source_target_pairs={{0,192},{8,200},{16,208},{24,216},{32,224},{40,232},{48,240},{56,2... | collective-permute-start | bytes 2359304 | tf_op jit(solution)/shard_map/ppermute | solution.py:39
  16.6 32.3 %collective-permute-start.3 = (bf16[1024,384]{1,0:T(8,128)(2,1)}, bf16[1024,384]{1,0:T(8,128)(2,1)S(1)}, u32[]{:S(2)}, u32[]{:S(2)}) collective-permute-start(bf16[1024,384]{1,0:T(8,128)(2,1)} %get-tuple-element.13.kv_ref.b0), channel_id=1, source_target_pairs={{0,64},{8,72},{16,80},{24,88},{32,96},{40,104},{48,112},{56,120},{... | collective-permute-start | bytes 2359304 | tf_op jit(solution)/shard_map/ppermute | solution.py:39
  16.6 33.7 %collective-permute-start = (bf16[1024,384]{1,0:T(8,128)(2,1)}, bf16[1024,384]{1,0:T(8,128)(2,1)}, u32[]{:S(2)}, u32[]{:S(2)}) collective-permute-start(bf16[1024,384]{1,0:T(8,128)(2,1)} %get-tuple-element.13.kv_ref.b0), channel_id=1, source_target_pairs={{0,56},{8,16},{16,8},{24,32},{32,24},{40,48},{48,40},{56,0},{64,12... | collective-permute-start | bytes 2359304 | tf_op jit(solution)/shard_map/ppermute | solution.py:43
  35.0 0.8 copy-start.1
  41.8 4.4 %copy-start.2 = (bf16[1024,384]{1,0:T(8,128)(2,1)S(1)}, bf16[1024,384]{1,0:T(8,128)(2,1)}, u32[]{:S(2)}) copy-start(bf16[1024,384]{1,0:T(8,128)(2,1)} %get-tuple-element.13.kv_ref.b0) | copy-start | bytes 2359300
  41.8 25.3 %all-to-all-start.2 = ((bf16[4,192,768]{2,1,0:T(8,128)(2,1)}), bf16[4,192,768]{2,1,0:T(8,128)(2,1)S(1)}, u32[]{:S(2)}, u32[]{:S(2)}) async-start(bf16[4,192,768]{2,1,0:T(8,128)(2,1)} %split_proj.1.rest_1_), calls=%async_computation.2 | async-start | bytes 2359296 | tf_op jit(solution)/shard_map/all_to_all | solution.py:54
  46.2 8.0 %collective-permute-start.5 = (bf16[1024,384]{1,0:T(8,128)(2,1)S(1)}, bf16[1024,384]{1,0:T(8,128)(2,1)}, u32[]{:S(2)}, u32[]{:S(2)}) collective-permute-start(bf16[1024,384]{1,0:T(8,128)(2,1)S(1)} %copy-done.2), channel_id=1, source_target_pairs={{0,8},{8,0},{16,24},{24,16},{32,40},{40,32},{48,56},{56,48},{64,72... | collective-permute-start | bytes 2359304 | tf_op jit(solution)/shard_map/ppermute | solution.py:49
  48.0 0.9 copy-start.4
  48.9 5.3 %collective-permute-start.7 = (bf16[1024,384]{1,0:T(8,128)(2,1)}, bf16[1024,384]{1,0:T(8,128)(2,1)S(1)}, u32[]{:S(2)}, u32[]{:S(2)}) collective-permute-start(bf16[1024,384]{1,0:T(8,128)(2,1)} %after.4.b2), channel_id=1, source_target_pairs={{0,8},{8,0},{16,24},{24,16},{32,40},{40,32},{48,56},{56,48},{64,72... | collective-permute-start | bytes 2359304 | tf_op jit(solution)/shard_map/ppermute | solution.py:49
  48.9 0.9 copy-start.3
  49.8 4.4 %collective-permute-start.6 = (bf16[1024,384]{1,0:T(8,128)(2,1)}, bf16[1024,384]{1,0:T(8,128)(2,1)S(1)}, u32[]{:S(2)}, u32[]{:S(2)}) collective-permute-start(bf16[1024,384]{1,0:T(8,128)(2,1)} %after.3.b1), channel_id=1, source_target_pairs={{0,8},{8,0},{16,24},{24,16},{32,40},{40,32},{48,56},{56,48},{64,72... | collective-permute-start | bytes 2359304 | tf_op jit(solution)/shard_map/ppermute | solution.py:49
  50.3 21.6 %collective-permute-start.1 = (bf16[1024,384]{1,0:T(8,128)(2,1)}, bf16[1024,384]{1,0:T(8,128)(2,1)}, u32[]{:S(2)}, u32[]{:S(2)}) collective-permute-start(bf16[1024,384]{1,0:T(8,128)(2,1)} %collective-permute-done.b0), channel_id=1, source_target_pairs={{0,64},{8,72},{16,80},{24,88},{32,96},{40,104},{48,112},{56,120},{... | collective-permute-start | bytes 2359304 | tf_op jit(solution)/shard_map/ppermute | solution.py:39
  50.4 21.6 %collective-permute-start.2 = (bf16[1024,384]{1,0:T(8,128)(2,1)}, bf16[1024,384]{1,0:T(8,128)(2,1)}, u32[]{:S(2)}, u32[]{:S(2)}) collective-permute-start(bf16[1024,384]{1,0:T(8,128)(2,1)} %collective-permute-done.b0), channel_id=1, source_target_pairs={{0,192},{8,200},{16,208},{24,216},{32,224},{40,232},{48,240},{56,2... | collective-permute-start | bytes 2359304 | tf_op jit(solution)/shard_map/ppermute | solution.py:39
  54.3 0.9 copy-start.6
  55.2 0.9 copy-start.7
  67.1 17.2 %all-to-all-start.3 = ((bf16[32,8,512]{2,1,0:T(8,128)(2,1)}), bf16[32,8,512]{2,1,0:T(8,128)(2,1)S(1)}, u32[]{:S(2)}, u32[]{:S(2)}) async-start(bf16[32,8,512]{2,1,0:T(8,128)(2,1)} %after.5), calls=%async_computation.3 | async-start | bytes 524288 | tf_op jit(solution)/shard_map/all_to_all | solution.py:488
  84.3 0.7 copy-start.5
  85.0 26.2 %all-to-all-start.1 = ((bf16[4,512,384]{2,1,0:T(8,128)(2,1)}), bf16[4,512,384]{2,1,0:T(8,128)(2,1)S(1)}, u32[]{:S(2)}, u32[]{:S(2)}) async-start(bf16[4,512,384]{2,1,0:T(8,128)(2,1)} %late.1), calls=%async_computation.1 | async-start | bytes 3145728 | tf_op jit(solution)/shard_map/all_to_all | solution.py:54
  89.6 21.7 %collective-permute-start.8 = (bf16[4,192,768]{2,1,0:T(8,128)(2,1)S(1)}, bf16[4,192,768]{2,1,0:T(8,128)(2,1)}, u32[]{:S(2)}, u32[]{:S(2)}) collective-permute-start(bf16[4,192,768]{2,1,0:T(8,128)(2,1)S(1)} %all-to-all-done.2.w_ref), channel_id=1, source_target_pairs={{0,8},{8,0},{16,24},{24,16},{32,40},{40,32},{48,56},{56,48},{64,72... | collective-permute-start | bytes 3538952 | tf_op jit(solution)/shard_map/ppermute | solution.py:49
  93.5 17.8 %collective-permute-start.10 = (bf16[8,768]{1,0:T(8,128)(2,1)}, bf16[8,768]{1,0:T(8,128)(2,1)S(1)}, u32[]{:S(2)}, u32[]{:S(2)}) collective-permute-start(bf16[8,768]{1,0:T(8,128)(2,1)} %get-tuple-element.20), channel_id=1, source_target_pairs={{0,2},{1,3},{2,0},{3,1},{4,6},{5,7},{6,4},{7,5},{8,10},{9,11},{10,... | collective-permute-start | bytes 36872 | tf_op jit(solution)/shard_map/ppermute | solution.py:58
  96.9 14.4 %collective-permute-start.11 = (bf16[8,768]{1,0:T(8,128)(2,1)}, bf16[8,768]{1,0:T(8,128)(2,1)S(1)}, u32[]{:S(2)}, u32[]{:S(2)}) collective-permute-start(bf16[8,768]{1,0:T(8,128)(2,1)} %get-tuple-element.21), channel_id=1, source_target_pairs={{0,3},{1,0},{2,1},{3,2},{4,7},{5,4},{6,5},{7,6},{8,11},{9,8},{10,9... | collective-permute-start | bytes 36872 | tf_op jit(solution)/shard_map/ppermute | solution.py:58
  98.1 13.2 %collective-permute-start.9 = (bf16[8,768]{1,0:T(8,128)(2,1)}, bf16[8,768]{1,0:T(8,128)(2,1)S(1)}, u32[]{:S(2)}, u32[]{:S(2)}) collective-permute-start(bf16[8,768]{1,0:T(8,128)(2,1)} %get-tuple-element.19), channel_id=1, source_target_pairs={{0,1},{1,2},{2,3},{3,0},{4,5},{5,6},{6,7},{7,4},{8,9},{9,10},{10,1... | collective-permute-start | bytes 36872 | tf_op jit(solution)/shard_map/ppermute | solution.py:58
  111.3 0.7 copy-start
  115.7 10.6 %collective-permute-start.12 = (bf16[528,384]{1,0:T(8,128)(2,1)S(1)}, bf16[528,384]{1,0:T(8,128)(2,1)S(1)}, u32[]{:S(2)}, u32[]{:S(2)}) collective-permute-start(bf16[528,384]{1,0:T(8,128)(2,1)S(1)} %get-tuple-element.23), channel_id=1, source_target_pairs={{0,4},{1,5},{2,6},{3,7},{4,0},{5,1},{6,2},{7,3},{8,12},{9,13},{10,... | collective-permute-start | bytes 1216520 | tf_op jit(solution)/shard_map/ppermute | solution.py:62

commit v4 on v3

--- a/solution.py
+++ b/solution.py
@@ -179,56 +179,60 @@
     )(wm, tlen, q, every, *blocks)
 
 
-def late_kernel(wm, q_ref, b0, b1, b2, acc_ref, m_ref, l_ref, *rest):
-    o_ref = rest[-1]
+def late_kernel(t, wm, q_ref, b0, b1, b2, acc_ref, m_ref, l_ref, o_ref):
     blocks = (b0, b1, b2)
     fcol = 2 * lax.rem(lax.axis_index("tile"), 2)
     rowof = (1, 0, 2)
-    for t in range(2):
-        rs = pl.ds(t * TT, TT)
-        parts = []
-        mx = None
-        for b in range(3):
-            s = scores(q_ref[rs, :], blocks[b][:ROWS, :])
-            for f in range(2):
-                sf = s[:, f * TT : (f + 1) * TT] * SCALE + bias_of(wm, t, f, rowof[b], fcol)
-                parts.append(sf)
-                fx = fold(sf, jnp.maximum)
-                mx = fx if mx is None else jnp.maximum(mx, fx)
-        mo = m_ref[rs, :]
-        mn = jnp.maximum(mo, spread(jnp.max(mx, axis=1, keepdims=True)))
-        al = jnp.exp2(mo - mn)
-        acc = acc_ref[rs, :] * al
-        tot = l_ref[rs, :] * al
-        for b in range(3):
-            p = jnp.concatenate(
-                [
-                    jnp.exp2(parts[2 * b + f][:, i * HD : (i + 1) * HD] - mn)
-                    for f in range(2)
-                    for i in range(2)
-                ],
-                axis=1,
-            )
-            tot += fold(p, jnp.add)
-            acc += jnp.dot(p.astype(BF16), blocks[b][ROWS:, :], preferred_element_type=F32)
-        o = (acc / jnp.sum(tot, axis=1, keepdims=True)).astype(BF16)
+    parts = []
+    mx = None
+    for b in range(3):
+        s = scores(q_ref[...], blocks[b][:ROWS, :])
+        for f in range(2):
+            sf = s[:, f * TT : (f + 1) * TT] * SCALE + bias_of(wm, t, f, rowof[b], fcol)
+            parts.append(sf)
+            fx = fold(sf, jnp.maximum)
+            mx = fx if mx is None else jnp.maximum(mx, fx)
+    mo = m_ref[...]
+    mn = jnp.maximum(mo, spread(jnp.max(mx, axis=1, keepdims=True)))
+    al = jnp.exp2(mo - mn)
+    acc = acc_ref[...] * al
+    tot = l_ref[...] * al
+    for b in range(3):
+        p = jnp.concatenate(
+            [
+                jnp.exp2(parts[2 * b + f][:, i * HD : (i + 1) * HD] - mn)
+                for f in range(2)
+                for i in range(2)
+            ],
+            axis=1,
+        )
+        tot += fold(p, jnp.add)
+        acc += jnp.dot(p.astype(BF16), blocks[b][ROWS:, :], preferred_element_type=F32)
+    o = (acc / jnp.sum(tot, axis=1, keepdims=True)).astype(BF16)
+    if t == 0:
         for x in range(4):
-            o_ref[x, rs, :] = o
-
-
-def late(wm, q, far, acc, m, l, *deps):
-    head = pl.BlockSpec((ROWS, HD), lambda i: (0, i))
+            o_ref[x] = o
+    else:
+        o_ref[...] = o
+
+
+def late(t, wm, q, far, acc, m, l):
+    head = pl.BlockSpec((TT, HD), lambda i: (t, i))
     block = pl.BlockSpec((2 * ROWS, HD), lambda i: (0, i))
-    return pl.pallas_call(
-        late_kernel,
+    if t == 0:
+        shape, out = (4, TT, W), pl.BlockSpec((4, TT, HD), lambda i: (0, 0, i))
+    else:
+        shape, out = (TT, W), pl.BlockSpec((TT, HD), lambda i: (0, i))
+    return pl.pallas_call(
+        functools.partial(late_kernel, t),
         grid=(NH,),
-        out_shape=jax.ShapeDtypeStruct((4, ROWS, W), BF16),
-        in_specs=[SM, head, block, block, block, head, head, head] + [ANY] * len(deps),
-        out_specs=pl.BlockSpec((4, ROWS, HD), lambda i: (0, 0, i)),
-        compiler_params=params(60),
-        cost_estimate=cost(12 * ROWS * ROWS * W, 2 * 2**20, 3 * ROWS * ROWS),
+        out_shape=jax.ShapeDtypeStruct(shape, BF16),
+        in_specs=[SM, head, block, block, block, head, head, head],
+        out_specs=out,
+        compiler_params=params(60),
+        cost_estimate=cost(6 * ROWS * ROWS * W, 2 * 2**20, 3 * ROWS * TT),
         name="late",
-    )(wm, q, *far, acc, m, l, *deps)
+    )(wm, q, *far, acc, m, l)
 
 
 def columns(xd, j):
@@ -394,75 +398,84 @@
     )(x, *deps)
 
 
-def project_kernel(
-    a_ref, w_ref, v_ref, t0, t1, t2, t3, own_ref, away_ref, abuf, wbuf, acc, sem
-):
+def project_kernel(t, *refs):
+    if t == 0:
+        (a_ref, w_ref, v_ref), rest = refs[:3], refs[3:]
+        order = [(a_ref.at[x], x) for x in range(4)]
+    else:
+        me = lax.rem(lax.axis_index("head"), 4)
+        (w_ref, v_ref), rest = refs[4:6], refs[6:]
+        order = [(refs[d], lax.rem(me + 4 - d, 4)) for d in range(4)]
+    own_ref, away_ref, abuf, wbuf, acc, sem = rest[-6:]
     core = lax.rem(lax.axis_index("tile"), 2)
     copies = []
-    for x in range(4):
-        for i, (src, dst) in enumerate(
+    for i, (a, x) in enumerate(order):
+        for j, (src, dst) in enumerate(
             (
-                (w_ref, wbuf.at[x, pl.ds(pl.multiple_of(core * HALF, 16), HALF)]),
-                (v_ref, wbuf.at[x, pl.ds(pl.multiple_of((1 - core) * HALF, 16), HALF)]),
-                (a_ref, abuf.at[x]),
+                (w_ref.at[x], wbuf.at[i, pl.ds(pl.multiple_of(core * HALF, 16), HALF)]),
+                (v_ref.at[x], wbuf.at[i, pl.ds(pl.multiple_of((1 - core) * HALF, 16), HALF)]),
+                (a, abuf.at[i]),
             )
         ):
-            copies.append(pltpu.make_async_copy(src.at[x], dst, sem.at[3 * x + i]))
+            copies.append(pltpu.make_async_copy(src, dst, sem.at[3 * i + j]))
             copies[-1].start()
-    t = sum(r[...].astype(F32) for r in (t0, t1, t2, t3))
-    t = jnp.concatenate([t, jnp.zeros_like(t)], axis=0)
-    own_ref[pl.ds(ROWS, 16), :] = t[:, :W]
-    away_ref[pl.ds(ROWS, 16), :] = t[:, W:].astype(BF16)
-    for x in range(4):
-        for c in copies[3 * x : 3 * x + 3]:
+    if t == 1:
+        text = sum(r[...].astype(F32) for r in rest[:4])
+        text = jnp.concatenate([text, jnp.zeros_like(text)], axis=0)
+        own_ref[pl.ds(TT, 16), :] = text[:, :W]
+        away_ref[pl.ds(TT, 16), :] = text[:, W:].astype(BF16)
+    for i in range(4):
+        for c in copies[3 * i : 3 * i + 3]:
             c.wait()
-        o = jnp.dot(abuf[x], wbuf[x], preferred_element_type=F32)
-        if x > 0:
+        o = jnp.dot(abuf[i], wbuf[i], preferred_element_type=F32)
+        if i > 0:
             o += acc[...]
-        if x < 3:
+        if i < 3:
             acc[...] = o
         else:
-            own_ref[:ROWS, :] = o[:, :W]
-            away_ref[:ROWS, :] = o[:, W:].astype(BF16)
-
-
-def project(attn, proj, text):
-    return pl.pallas_call(
-        project_kernel,
+            own_ref[:TT, :] = o[:, :W]
+            away_ref[:TT, :] = o[:, W:].astype(BF16)
+
+
+def project(t, attn, proj, text=(), deps=()):
+    rows = TT + 16 * t
+    return pl.pallas_call(
+        functools.partial(project_kernel, t),
         out_shape=(
-            jax.ShapeDtypeStruct((ROWS + 16, W), F32),
-            jax.ShapeDtypeStruct((ROWS + 16, W), BF16),
+            jax.ShapeDtypeStruct((rows, W), F32),
+            jax.ShapeDtypeStruct((rows, W), BF16),
         ),
-        in_specs=[ANY] * 3 + [VM] * 4,
+        in_specs=[ANY] * (len(attn) + 2) + [VM] * len(text) + [ANY] * len(deps),
         out_specs=(VM, VM),
         scratch_shapes=[
-            pltpu.VMEM((4, ROWS, W), BF16),
+            pltpu.VMEM((4, TT, W), BF16),
             pltpu.VMEM((4, W, 2 * W), BF16),
-            pltpu.VMEM((ROWS, 2 * W), F32),
+            pltpu.VMEM((TT, 2 * W), F32),
             pltpu.SemaphoreType.DMA((12,)),
         ],
         compiler_params=params(24),
-        cost_estimate=cost(2 * ROWS * 4 * W * 2 * W, 6 * 2**20),
+        cost_estimate=cost(2 * TT * 4 * W * 2 * W, 6 * 2**20),
         name="project",
-    )(attn, *proj, *text)
-
-
-def add_kernel(own_ref, got_ref, video_ref, text_ref):
-    video_ref[...] = (own_ref[:ROWS, :] + got_ref[:ROWS, :].astype(F32)).astype(BF16)
-    t = own_ref[pl.ds(ROWS, 16), :] + got_ref[pl.ds(ROWS, 16), :].astype(F32)
+    )(*attn, *proj, *text, *deps)
+
+
+def add_kernel(o0, g0, o1, g1, video_ref, text_ref):
+    video_ref[:TT, :] = (o0[...] + g0[...].astype(F32)).astype(BF16)
+    video_ref[TT:, :] = (o1[:TT, :] + g1[:TT, :].astype(F32)).astype(BF16)
+    t = o1[pl.ds(TT, 16), :] + g1[pl.ds(TT, 16), :].astype(F32)
     text_ref[...] = t[:TL, :].astype(BF16)
 
 
-def add_up(own, got):
+def add_up(*parts):
     return pl.pallas_call(
         add_kernel,
         out_shape=(jax.ShapeDtypeStruct((ROWS, W), BF16), jax.ShapeDtypeStruct((TL, W), BF16)),
-        in_specs=[VM, VM],
+        in_specs=[VM] * 4,
         out_specs=(VM, VM),
         compiler_params=params(8),
         cost_estimate=cost(0, 2 * 2**20),
         name="add_up",
-    )(own, got)
+    )(*parts)
 
 
 def per_device(
@@ -487,11 +500,16 @@
     msg = after(msg.reshape(32, TL, W + HD), acc)
     got = lax.all_to_all(msg, "tile", 0, 0, tiled=True).reshape(TEXT, W + HD)
 
-    attn = x_swap(late(window_mask, video_q, (far, far_up, far_dn), acc, m, l))
+    given = (window_mask, video_q, (far, far_up, far_dn), acc, m, l)
+    first = x_swap(late(0, *given))
+    second = late(1, *given)
+    second = [x_on(second, d) if d else second for d in range(4)]
     parts = text_merge(text_length, got, text_q, every, text_proj)
     parts = [x_on(p, d) if d else p for d, p in enumerate(parts)]
-    own, away = project(attn, (proj, other_core(proj)), parts)
-    return add_up(own, z_pair(away))
+    proj = (proj, other_core(proj))
+    own0, away0 = project(0, [first], proj)
+    own1, away1 = project(1, second, proj, parts, (away0,))
+    return add_up(own0, z_pair(away0), own1, z_pair(away1))
 
 
 def solution(mesh):

time: 128 us -> 139 us (1.086)
  starting transfers between devices: 41.8 us -> 49.4 us
  Pallas kernels: 34.5 us -> 40.4 us
  local copies, waits for them, and re-layouts: 5.85 us -> 4.19 us
    all_to_all x2, waiting for transfers between devices: 0.01 us -> 9.8 us  [x_swap(): return lax.all_to_all(x, 'head', 0, 0, tiled=True, axis_index_groups=groups)]
    ppermute x3 -> x6, waiting for transfers between devices: 12.4 us -> 3.18 us  [x_on(): lax.ppermute(x, 'head', [(i, i // 4 * 4 + (i + d) % 4) for i in range(8)])]
    pallas_call x2 -> x4, Pallas kernels: 10.7 us -> 16.5 us  [the longest x2 10.1 us: late(): pl.pallas_call(functools.partial(late_kernel, t), grid=(NH,), out_shape=j...]
    ppermute x3 -> x6, starting transfers between devices: 5.39 us -> 11.1 us  [x_on(): lax.ppermute(x, 'head', [(i, i // 4 * 4 + (i + d) % 4) for i in range(8)])]
    ppermute x1 -> x2, waiting for transfers between devices: 10.5 us -> 8.02 us  [z_pair(): return lax.ppermute(x, 'head', [(i, i ^ 4) for i in range(8)])]
    ppermute x1 -> x2, starting transfers between devices: 0.09 us -> 2.11 us  [z_pair(): return lax.ppermute(x, 'head', [(i, i ^ 4) for i in range(8)])]
    unnamed x16 -> x14, local copies, waits for them, and re-layouts: 5.85 us -> 4.19 us
  transfers between devices with their start and end apart: 17 -> 21, of which waited for: 4 -> 6; matrix products, arithmetic and copies ran while one was open for 0% -> 0% of each run, Pallas kernels for 22% -> 25%
where the time goes in v4:
time: 139 us; the launch traced here: 138 us
  starting transfers between devices  49.4 us (36%)
  waiting for transfers between devices  42.7 us (31%)
  Pallas kernels  40.4 us (29%)
  local copies, waits for them, and re-layouts  4.19 us (3%)
  between operations  1.47 us (1%)
    all_to_all x1, waiting for transfers between devices, per_device(): every = lax.all_to_all(text, 'tile', 0, 0, tiled=True).reshape(TEXT, 3 * W)  15.3 us
    ppermute x6, starting transfers between devices, x_on(): lax.ppermute(x, 'head', [(i, i // 4 * 4 + (i + d) % 4) for i in range(8)])  11.1 us
    pallas_call x1, Pallas kernels, early(): pl.pallas_call(early_kernel, out_shape=(part, part, part), in_specs=[SM,...  11 us
    all_to_all x1, starting transfers between devices, per_device(): every = lax.all_to_all(text, 'tile', 0, 0, tiled=True).reshape(TEXT, 3 * W)  10.6 us
    pallas_call x2, Pallas kernels, late(): pl.pallas_call(functools.partial(late_kernel, t), grid=(NH,), out_shape=j...  10.1 us
    all_to_all x2, waiting for transfers between devices, x_swap(): return lax.all_to_all(x, 'head', 0, 0, tiled=True, axis_index_groups=groups)  9.8 us
    ppermute x2, waiting for transfers between devices, z_pair(): return lax.ppermute(x, 'head', [(i, i ^ 4) for i in range(8)])  8.02 us
    all_to_all x2, starting transfers between devices, x_swap(): return lax.all_to_all(x, 'head', 0, 0, tiled=True, axis_index_groups=groups)  7.79 us
  transfers between devices with their start and end apart: 21, of which 6 were waited for; matrix products, arithmetic and copies ran while one was open for 0% of the time, Pallas kernels for 25%

profile of v4, /device:TPU:32, one launch (start us, length us, event | category | flops | bytes accessed | tf_op | source)
XLA Modules:
  0.0 138.1 jit_solution(14331143026866362555)
XLA Ops:
  0.6 2.3 %pack.1 = (bf16[1024,384]{1,0:T(8,128)(2,1)}, bf16[32,8,1152]{2,1,0:T(8,128)(2,1)}) custom-call(bf16[512,384]{1,0:T(8,128)(2,1)} %k_ref.1, bf16[512,384]{1,0:T(8,128)(2,1)} %v_ref.1, bf16[8,384]{1,0:T(8,128)(2,1)} %tq_ref.3, bf16[8,384]{1,0:T(8,128)(2,1)} %tk_ref.1, bf16[8,384]{1,0:T(8,128)(2,1)} %tv_ref.1), custom_call_target="tpu_custom_call" | custom-call | flops 1 | bytes 1 | tf_op jit(solution)/shard_map/pack/pallas_call | solution.py:369
  2.9 10.6 %all-to-all-start = ((bf16[32,8,1152]{2,1,0:T(8,128)(2,1)}), bf16[32,8,1152]{2,1,0:T(8,128)(2,1)S(1)}, u32[]{:S(2)}, u32[]{:S(2)}) async-start(bf16[32,8,1152]{2,1,0:T(8,128)(2,1)} %get-tuple-element.16), calls=%async_computation | async-start | bytes 1179648 | tf_op jit(solution)/shard_map/all_to_all | solution.py:490
  13.5 3.1 %collective-permute-start.4 = (bf16[1024,384]{1,0:T(8,128)(2,1)}, bf16[1024,384]{1,0:T(8,128)(2,1)S(1)}, u32[]{:S(2)}, u32[]{:S(2)}) collective-permute-start(bf16[1024,384]{1,0:T(8,128)(2,1)} %get-tuple-element.15.kv_ref.b0), channel_id=1, source_target_pairs={{0,192},{8,200},{16,208},{24,216},{32,224},{40,232},{48,240},{56,2... | collective-permute-start | bytes 2359304 | tf_op jit(solution)/shard_map/ppermute | solution.py:39
  16.6 3.1 %collective-permute-start = (bf16[1024,384]{1,0:T(8,128)(2,1)}, bf16[1024,384]{1,0:T(8,128)(2,1)}, u32[]{:S(2)}, u32[]{:S(2)}) collective-permute-start(bf16[1024,384]{1,0:T(8,128)(2,1)} %get-tuple-element.15.kv_ref.b0), channel_id=1, source_target_pairs={{0,56},{8,16},{16,8},{24,32},{32,24},{40,48},{48,40},{56,0},{64,12... | collective-permute-start | bytes 2359304 | tf_op jit(solution)/shard_map/ppermute | solution.py:43
  19.7 15.3 %all-to-all-done = bf16[32,8,1152]{2,1,0:T(8,128)(2,1)S(1)} async-done(((bf16[32,8,1152]{2,1,0:T(8,128)(2,1)}), bf16[32,8,1152]{2,1,0:T(8,128)(2,1)S(1)}, u32[]{:S(2)}, u32[]{:S(2)}) %all-to-all-start) | async-done | bytes 589856 | tf_op jit(solution)/shard_map/all_to_all | solution.py:490
  35.8 3.1 %text_part.1.after_ref.rest_0_ = bf16[256,512]{1,0:T(8,128)(2,1)} custom-call(bf16[256,1152]{1,0:T(8,128)(2,1)} %bitcast.3, bf16[1024,384]{1,0:T(8,128)(2,1)} %get-tuple-element.15.kv_ref.b0), custom_call_target="tpu_custom_call" | custom-call | flops 1 | bytes 1 | tf_op jit(solution)/shard_map/text_part/pallas_call | solution.py:267
  39.0 2.8 %split_proj.1.rest_1_ = bf16[4,192,768]{2,1,0:T(8,128)(2,1)} custom-call(bf16[384,3072]{1,0:T(8,128)(2,1)} %proj_ref.2, bf16[256,512]{1,0:T(8,128)(2,1)} %text_part.1.after_ref.rest_0_), custom_call_target="tpu_custom_call" | custom-call | flops 1 | bytes 1 | tf_op jit(solution)/shard_map/split_proj/pallas_call | solution.py:333
  41.8 4.3 %all-to-all-start.2 = ((bf16[4,192,768]{2,1,0:T(8,128)(2,1)}), bf16[4,192,768]{2,1,0:T(8,128)(2,1)S(1)}, u32[]{:S(2)}, u32[]{:S(2)}) async-start(bf16[4,192,768]{2,1,0:T(8,128)(2,1)} %split_proj.1.rest_1_), calls=%async_computation.2 | async-start | bytes 2359296 | tf_op jit(solution)/shard_map/all_to_all | solution.py:54
  46.1 1.8 %collective-permute-start.5 = (bf16[1024,384]{1,0:T(8,128)(2,1)}, bf16[1024,384]{1,0:T(8,128)(2,1)}, u32[]{:S(2)}, u32[]{:S(2)}) collective-permute-start(bf16[1024,384]{1,0:T(8,128)(2,1)} %get-tuple-element.15.kv_ref.b0), channel_id=1, source_target_pairs={{0,8},{8,0},{16,24},{24,16},{32,40},{40,32},{48,56},{56,48},{64,72... | collective-permute-start | bytes 2359304 | tf_op jit(solution)/shard_map/ppermute | solution.py:49
  47.9 0.9 copy-done.4
  48.7 0.9 copy-done.3
  50.2 3.2 %collective-permute-start.2 = (bf16[1024,384]{1,0:T(8,128)(2,1)}, bf16[1024,384]{1,0:T(8,128)(2,1)}, u32[]{:S(2)}, u32[]{:S(2)}) collective-permute-start(bf16[1024,384]{1,0:T(8,128)(2,1)} %collective-permute-done.b0), channel_id=1, source_target_pairs={{0,192},{8,200},{16,208},{24,216},{32,224},{40,232},{48,240},{56,2... | collective-permute-start | bytes 2359304 | tf_op jit(solution)/shard_map/ppermute | solution.py:39
  53.4 9.8 %all-to-all-done.2.refs_1_.refs_4_ = bf16[4,192,768]{2,1,0:T(8,128)(2,1)S(1)} async-done(((bf16[4,192,768]{2,1,0:T(8,128)(2,1)}), bf16[4,192,768]{2,1,0:T(8,128)(2,1)S(1)}, u32[]{:S(2)}, u32[]{:S(2)}) %all-to-all-start.2) | async-done | bytes 1179680 | tf_op jit(solution)/shard_map/all_to_all | solution.py:54
  64.5 11.0 %early.1 = (f32[512,384]{1,0:T(8,128)}, f32[512,384]{1,0:T(8,128)}, f32[512,384]{1,0:T(8,128)}) custom-call(s32[2,27]{1,0:T(2,128)} %wm.5, s32[1]{0:T(128)S(6)} %copy.18.tlen, bf16[512,384]{1,0:T(8,128)(2,1)} %q_ref.5, bf16[256,1152]{1,0:T(8,128)(2,1)} %bitcast.4, bf16[1024,384]{1,0:T(8,128)(2,1)} %get-tuple-element.15.kv_ref.b0, ...), custom_call_target="tpu_custom_call" | custom-call | flops 1 | bytes 1 | tf_op jit(solution)/shard_map/early/pallas_call | solution.py:165
  75.5 5.5 %all-to-all-start.3 = ((bf16[32,8,512]{2,1,0:T(8,128)(2,1)}), bf16[32,8,512]{2,1,0:T(8,128)(2,1)S(1)}, u32[]{:S(2)}, u32[]{:S(2)}) async-start(bf16[32,8,512]{2,1,0:T(8,128)(2,1)} %after.5), calls=%async_computation.3 | async-start | bytes 524288 | tf_op jit(solution)/shard_map/all_to_all | solution.py:501
  81.0 0.9 copy-done.5
  81.9 5.1 %late.2 = bf16[4,256,384]{2,1,0:T(8,128)(2,1)} custom-call(s32[2,27]{1,0:T(2,128)} %wm.5, bf16[512,384]{1,0:T(8,128)(2,1)} %q_ref.5, bf16[1024,384]{1,0:T(8,128)(2,1)} %collective-permute-done.b0, bf16[1024,384]{1,0:T(8,128)(2,1)} %copy-done.5, bf16[1024,384]{1,0:T(8,128)(2,1)} %collective-permute-done.2.b2, f32[512,384]{1,0:T(8,128)} %get-tuple-element.17.acc_ref.rest_0_, ...), custom_call_target="tpu_custom_call" | custom-call | flops 1 | bytes 1 | tf_op jit(solution)/shard_map/late/pallas_call | solution.py:226
  87.0 6.4 %all-to-all-done.3 = bf16[32,8,512]{2,1,0:T(8,128)(2,1)S(1)} async-done(((bf16[32,8,512]{2,1,0:T(8,128)(2,1)}), bf16[32,8,512]{2,1,0:T(8,128)(2,1)S(1)}, u32[]{:S(2)}, u32[]{:S(2)}) %all-to-all-start.3) | async-done | bytes 262176 | tf_op jit(solution)/shard_map/all_to_all | solution.py:501
  94.1 3.5 %all-to-all-start.1 = ((bf16[4,256,384]{2,1,0:T(8,128)(2,1)}), bf16[4,256,384]{2,1,0:T(8,128)(2,1)S(1)}, u32[]{:S(2)}, u32[]{:S(2)}) async-start(bf16[4,256,384]{2,1,0:T(8,128)(2,1)} %late.2), calls=%async_computation.1 | async-start | bytes 1572864 | tf_op jit(solution)/shard_map/all_to_all | solution.py:54
  97.6 5.0 %late.3.refs_0_ = bf16[256,384]{1,0:T(8,128)(2,1)} custom-call(s32[2,27]{1,0:T(2,128)} %wm.5, bf16[512,384]{1,0:T(8,128)(2,1)} %q_ref.5, bf16[1024,384]{1,0:T(8,128)(2,1)} %collective-permute-done.b0, bf16[1024,384]{1,0:T(8,128)(2,1)} %copy-done.5, bf16[1024,384]{1,0:T(8,128)(2,1)} %collective-permute-done.2.b2, ...), custom_call_target="tpu_custom_call" | custom-call | flops 1 | bytes 1 | tf_op jit(solution)/shard_map/late/pallas_call | solution.py:226
  102.5 2.0 %collective-permute-start.10 = (bf16[256,384]{1,0:T(8,128)(2,1)}, bf16[256,384]{1,0:T(8,128)(2,1)S(1)}, u32[]{:S(2)}, u32[]{:S(2)}) collective-permute-start(bf16[256,384]{1,0:T(8,128)(2,1)} %late.3.refs_0_), channel_id=1, source_target_pairs={{0,1},{1,2},{2,3},{3,0},{4,5},{5,6},{6,7},{7,4},{8,9},{9,10},{10,1... | collective-permute-start | bytes 589832 | tf_op jit(solution)/shard_map/ppermute | solution.py:58
  104.5 2.7 %collective-permute-start.11 = (bf16[256,384]{1,0:T(8,128)(2,1)}, bf16[256,384]{1,0:T(8,128)(2,1)}, u32[]{:S(2)}, u32[]{:S(2)}) collective-permute-start(bf16[256,384]{1,0:T(8,128)(2,1)} %late.3.refs_0_), channel_id=1, source_target_pairs={{0,2},{1,3},{2,0},{3,1},{4,6},{5,7},{6,4},{7,5},{8,10},{9,11},{10,... | collective-permute-start | bytes 589832 | tf_op jit(solution)/shard_map/ppermute | solution.py:58
  107.2 1.5 %collective-permute-start.12 = (bf16[256,384]{1,0:T(8,128)(2,1)}, bf16[256,384]{1,0:T(8,128)(2,1)}, u32[]{:S(2)}, u32[]{:S(2)}) collective-permute-start(bf16[256,384]{1,0:T(8,128)(2,1)} %late.3.refs_0_), channel_id=1, source_target_pairs={{0,3},{1,0},{2,1},{3,2},{4,7},{5,4},{6,5},{7,6},{8,11},{9,8},{10,9... | collective-permute-start | bytes 589832 | tf_op jit(solution)/shard_map/ppermute | solution.py:58
  108.6 3.8 %text_merge.1 = (bf16[8,768]{1,0:T(8,128)(2,1)}, bf16[8,768]{1,0:T(8,128)(2,1)}, bf16[8,768]{1,0:T(8,128)(2,1)}, bf16[8,768]{1,0:T(8,128)(2,1)}) custom-call(s32[1]{0:T(128)S(6)} %copy.18.tlen, bf16[256,512]{1,0:T(8,128)(2,1)} %bitcast.7, bf16[8,384]{1,0:T(8,128)(2,1)} %tq_ref.3, bf16[256,1152]{1,0:T(8,128)(2,1)} %bitcast.5, bf16[384,3072]{1,0:T(8,128)(2,1)} %proj_ref.3), custom_call_target="tpu_custom_call" | custom-call | flops 1 | bytes 1 | tf_op jit(solution)/shard_map/text_merge/pallas_call | solution.py:312
  113.0 2.3 %collective-permute-done.10.refs_1_ = bf16[256,384]{1,0:T(8,128)(2,1)S(1)} collective-permute-done((bf16[256,384]{1,0:T(8,128)(2,1)}, bf16[256,384]{1,0:T(8,128)(2,1)S(1)}, u32[]{:S(2)}, u32[]{:S(2)}) %collective-permute-start.10) | collective-permute-done | bytes 196640 | tf_op jit(solution)/shard_map/ppermute | solution.py:58
  115.3 4.5 %collective-permute-start.14 = (bf16[8,768]{1,0:T(8,128)(2,1)}, bf16[8,768]{1,0:T(8,128)(2,1)}, u32[]{:S(2)}, u32[]{:S(2)}) collective-permute-start(bf16[8,768]{1,0:T(8,128)(2,1)} %get-tuple-element.24), channel_id=1, source_target_pairs={{0,2},{1,3},{2,0},{3,1},{4,6},{5,7},{6,4},{7,5},{8,10},{9,11},{10,... | collective-permute-start | bytes 36872 | tf_op jit(solution)/shard_map/ppermute | solution.py:58
  119.8 3.1 %project.2 = (f32[256,384]{1,0:T(8,128)S(1)}, bf16[256,384]{1,0:T(8,128)(2,1)S(1)}) custom-call(bf16[4,256,384]{2,1,0:T(8,128)(2,1)S(1)} %all-to-all-done.1.refs_0_, bf16[4,192,768]{2,1,0:T(8,128)(2,1)S(1)} %all-to-all-done.2.refs_1_.refs_4_, bf16[4,192,768]{2,1,0:T(8,128)(2,1)S(1)} %collective-permute-done.8.refs_2_.refs_5_), custom_call_target="tpu_custom_call" | custom-call | flops 1 | bytes 1 | tf_op jit(solution)/shard_map/project/pallas_call | solution.py:442
  123.0 0.8 collective-permute-done.15.refs_9_
  123.8 3.3 %project.3 = (f32[272,384]{1,0:T(8,128)S(1)}, bf16[272,384]{1,0:T(8,128)(2,1)S(1)}) custom-call(bf16[256,384]{1,0:T(8,128)(2,1)S(1)} %copy-done, bf16[256,384]{1,0:T(8,128)(2,1)S(1)} %collective-permute-done.10.refs_1_, bf16[256,384]{1,0:T(8,128)(2,1)} %collective-permute-done.11.refs_2_, bf16[256,384]{1,0:T(8,128)(2,1)} %collective-permute-done.12.refs_3_, ...), custom_call_target="tpu_custom_call" | custom-call | flops 1 | bytes 1 | tf_op jit(solution)/shard_map/project/pallas_call | solution.py:442
  127.3 2.0 %collective-permute-start.9 = (bf16[256,384]{1,0:T(8,128)(2,1)S(1)}, bf16[256,384]{1,0:T(8,128)(2,1)S(1)}, u32[]{:S(2)}, u32[]{:S(2)}) collective-permute-start(bf16[256,384]{1,0:T(8,128)(2,1)S(1)} %get-tuple-element.21.refs_10_), channel_id=1, source_target_pairs={{0,4},{1,5},{2,6},{3,7},{4,0},{5,1},{6,2},{7,3},{8,12},{9,13},{10,... | collective-permute-start | bytes 589832 | tf_op jit(solution)/shard_map/ppermute | solution.py:62
  129.3 8.0 %collective-permute-done.9.g0 = bf16[256,384]{1,0:T(8,128)(2,1)S(1)} collective-permute-done((bf16[256,384]{1,0:T(8,128)(2,1)S(1)}, bf16[256,384]{1,0:T(8,128)(2,1)S(1)}, u32[]{:S(2)}, u32[]{:S(2)}) %collective-permute-start.9) | collective-permute-done | bytes 196640 | tf_op jit(solution)/shard_map/ppermute | solution.py:62
  137.3 0.8 add_up.1
  (37 shorter events, 3.4 us)
Async XLA Ops:
  2.9 32.1 %all-to-all-start = ((bf16[32,8,1152]{2,1,0:T(8,128)(2,1)}), bf16[32,8,1152]{2,1,0:T(8,128)(2,1)S(1)}, u32[]{:S(2)}, u32[]{:S(2)}) async-start(bf16[32,8,1152]{2,1,0:T(8,128)(2,1)} %get-tuple-element.16), calls=%async_computation | async-start | bytes 1179648 | tf_op jit(solution)/shard_map/all_to_all | solution.py:490
  13.5 34.4 %collective-permute-start.4 = (bf16[1024,384]{1,0:T(8,128)(2,1)}, bf16[1024,384]{1,0:T(8,128)(2,1)S(1)}, u32[]{:S(2)}, u32[]{:S(2)}) collective-permute-start(bf16[1024,384]{1,0:T(8,128)(2,1)} %get-tuple-element.15.kv_ref.b0), channel_id=1, source_target_pairs={{0,192},{8,200},{16,208},{24,216},{32,224},{40,232},{48,240},{56,2... | collective-permute-start | bytes 2359304 | tf_op jit(solution)/shard_map/ppermute | solution.py:39
  16.6 32.1 %collective-permute-start.3 = (bf16[1024,384]{1,0:T(8,128)(2,1)}, bf16[1024,384]{1,0:T(8,128)(2,1)S(1)}, u32[]{:S(2)}, u32[]{:S(2)}) collective-permute-start(bf16[1024,384]{1,0:T(8,128)(2,1)} %get-tuple-element.15.kv_ref.b0), channel_id=1, source_target_pairs={{0,64},{8,72},{16,80},{24,88},{32,96},{40,104},{48,112},{56,120},{... | collective-permute-start | bytes 2359304 | tf_op jit(solution)/shard_map/ppermute | solution.py:39
  16.6 33.5 %collective-permute-start = (bf16[1024,384]{1,0:T(8,128)(2,1)}, bf16[1024,384]{1,0:T(8,128)(2,1)}, u32[]{:S(2)}, u32[]{:S(2)}) collective-permute-start(bf16[1024,384]{1,0:T(8,128)(2,1)} %get-tuple-element.15.kv_ref.b0), channel_id=1, source_target_pairs={{0,56},{8,16},{16,8},{24,32},{32,24},{40,48},{48,40},{56,0},{64,12... | collective-permute-start | bytes 2359304 | tf_op jit(solution)/shard_map/ppermute | solution.py:43
  35.0 0.8 copy-start.2
  41.8 21.4 %all-to-all-start.2 = ((bf16[4,192,768]{2,1,0:T(8,128)(2,1)}), bf16[4,192,768]{2,1,0:T(8,128)(2,1)S(1)}, u32[]{:S(2)}, u32[]{:S(2)}) async-start(bf16[4,192,768]{2,1,0:T(8,128)(2,1)} %split_proj.1.rest_1_), calls=%async_computation.2 | async-start | bytes 2359296 | tf_op jit(solution)/shard_map/all_to_all | solution.py:54
  46.1 7.3 %collective-permute-start.5 = (bf16[1024,384]{1,0:T(8,128)(2,1)}, bf16[1024,384]{1,0:T(8,128)(2,1)}, u32[]{:S(2)}, u32[]{:S(2)}) collective-permute-start(bf16[1024,384]{1,0:T(8,128)(2,1)} %get-tuple-element.15.kv_ref.b0), channel_id=1, source_target_pairs={{0,8},{8,0},{16,24},{24,16},{32,40},{40,32},{48,56},{56,48},{64,72... | collective-permute-start | bytes 2359304 | tf_op jit(solution)/shard_map/ppermute | solution.py:49
  47.9 0.9 copy-start.4
  48.7 15.7 %collective-permute-start.7 = (bf16[1024,384]{1,0:T(8,128)(2,1)}, bf16[1024,384]{1,0:T(8,128)(2,1)}, u32[]{:S(2)}, u32[]{:S(2)}) collective-permute-start(bf16[1024,384]{1,0:T(8,128)(2,1)} %after.4.b2), channel_id=1, source_target_pairs={{0,8},{8,0},{16,24},{24,16},{32,40},{40,32},{48,56},{56,48},{64,72... | collective-permute-start | bytes 2359304 | tf_op jit(solution)/shard_map/ppermute | solution.py:49
  48.7 0.9 copy-start.3
  49.7 14.8 %collective-permute-start.6 = (bf16[1024,384]{1,0:T(8,128)(2,1)}, bf16[1024,384]{1,0:T(8,128)(2,1)}, u32[]{:S(2)}, u32[]{:S(2)}) collective-permute-start(bf16[1024,384]{1,0:T(8,128)(2,1)} %after.3.b1), channel_id=1, source_target_pairs={{0,8},{8,0},{16,24},{24,16},{32,40},{40,32},{48,56},{56,48},{64,72... | collective-permute-start | bytes 2359304 | tf_op jit(solution)/shard_map/ppermute | solution.py:49
  50.2 30.8 %collective-permute-start.1 = (bf16[1024,384]{1,0:T(8,128)(2,1)}, bf16[1024,384]{1,0:T(8,128)(2,1)S(1)}, u32[]{:S(2)}, u32[]{:S(2)}) collective-permute-start(bf16[1024,384]{1,0:T(8,128)(2,1)} %collective-permute-done.b0), channel_id=1, source_target_pairs={{0,64},{8,72},{16,80},{24,88},{32,96},{40,104},{48,112},{56,120},{... | collective-permute-start | bytes 2359304 | tf_op jit(solution)/shard_map/ppermute | solution.py:39
  50.2 30.9 %collective-permute-start.2 = (bf16[1024,384]{1,0:T(8,128)(2,1)}, bf16[1024,384]{1,0:T(8,128)(2,1)}, u32[]{:S(2)}, u32[]{:S(2)}) collective-permute-start(bf16[1024,384]{1,0:T(8,128)(2,1)} %collective-permute-done.b0), channel_id=1, source_target_pairs={{0,192},{8,200},{16,208},{24,216},{32,224},{40,232},{48,240},{56,2... | collective-permute-start | bytes 2359304 | tf_op jit(solution)/shard_map/ppermute | solution.py:39
  63.2 56.6 %collective-permute-start.8 = (bf16[4,192,768]{2,1,0:T(8,128)(2,1)S(1)}, bf16[4,192,768]{2,1,0:T(8,128)(2,1)S(1)}, u32[]{:S(2)}, u32[]{:S(2)}) collective-permute-start(bf16[4,192,768]{2,1,0:T(8,128)(2,1)S(1)} %all-to-all-done.2.refs_1_.refs_4_), channel_id=1, source_target_pairs={{0,8},{8,0},{16,24},{24,16},{32,40},{40,32},{48,56},{56,48},{64,72... | collective-permute-start | bytes 3538952 | tf_op jit(solution)/shard_map/ppermute | solution.py:49
  75.5 17.8 %all-to-all-start.3 = ((bf16[32,8,512]{2,1,0:T(8,128)(2,1)}), bf16[32,8,512]{2,1,0:T(8,128)(2,1)S(1)}, u32[]{:S(2)}, u32[]{:S(2)}) async-start(bf16[32,8,512]{2,1,0:T(8,128)(2,1)} %after.5), calls=%async_computation.3 | async-start | bytes 524288 | tf_op jit(solution)/shard_map/all_to_all | solution.py:501
  81.0 0.9 copy-start.5
  93.4 0.7 copy-start.6
  94.1 25.8 %all-to-all-start.1 = ((bf16[4,256,384]{2,1,0:T(8,128)(2,1)}), bf16[4,256,384]{2,1,0:T(8,128)(2,1)S(1)}, u32[]{:S(2)}, u32[]{:S(2)}) async-start(bf16[4,256,384]{2,1,0:T(8,128)(2,1)} %late.2), calls=%async_computation.1 | async-start | bytes 1572864 | tf_op jit(solution)/shard_map/all_to_all | solution.py:54
  102.5 12.8 %collective-permute-start.10 = (bf16[256,384]{1,0:T(8,128)(2,1)}, bf16[256,384]{1,0:T(8,128)(2,1)S(1)}, u32[]{:S(2)}, u32[]{:S(2)}) collective-permute-start(bf16[256,384]{1,0:T(8,128)(2,1)} %late.3.refs_0_), channel_id=1, source_target_pairs={{0,1},{1,2},{2,3},{3,0},{4,5},{5,6},{6,7},{7,4},{8,9},{9,10},{10,1... | collective-permute-start | bytes 589832 | tf_op jit(solution)/shard_map/ppermute | solution.py:58
  104.5 18.4 %collective-permute-start.11 = (bf16[256,384]{1,0:T(8,128)(2,1)}, bf16[256,384]{1,0:T(8,128)(2,1)}, u32[]{:S(2)}, u32[]{:S(2)}) collective-permute-start(bf16[256,384]{1,0:T(8,128)(2,1)} %late.3.refs_0_), channel_id=1, source_target_pairs={{0,2},{1,3},{2,0},{3,1},{4,6},{5,7},{6,4},{7,5},{8,10},{9,11},{10,... | collective-permute-start | bytes 589832 | tf_op jit(solution)/shard_map/ppermute | solution.py:58
  107.2 15.8 %collective-permute-start.12 = (bf16[256,384]{1,0:T(8,128)(2,1)}, bf16[256,384]{1,0:T(8,128)(2,1)}, u32[]{:S(2)}, u32[]{:S(2)}) collective-permute-start(bf16[256,384]{1,0:T(8,128)(2,1)} %late.3.refs_0_), channel_id=1, source_target_pairs={{0,3},{1,0},{2,1},{3,2},{4,7},{5,4},{6,5},{7,6},{8,11},{9,8},{10,9... | collective-permute-start | bytes 589832 | tf_op jit(solution)/shard_map/ppermute | solution.py:58
  112.4 10.5 %collective-permute-start.13 = (bf16[8,768]{1,0:T(8,128)(2,1)}, bf16[8,768]{1,0:T(8,128)(2,1)}, u32[]{:S(2)}, u32[]{:S(2)}) collective-permute-start(bf16[8,768]{1,0:T(8,128)(2,1)} %get-tuple-element.23), channel_id=1, source_target_pairs={{0,1},{1,2},{2,3},{3,0},{4,5},{5,6},{6,7},{7,4},{8,9},{9,10},{10,1... | collective-permute-start | bytes 36872 | tf_op jit(solution)/shard_map/ppermute | solution.py:58
  115.3 7.6 %collective-permute-start.14 = (bf16[8,768]{1,0:T(8,128)(2,1)}, bf16[8,768]{1,0:T(8,128)(2,1)}, u32[]{:S(2)}, u32[]{:S(2)}) collective-permute-start(bf16[8,768]{1,0:T(8,128)(2,1)} %get-tuple-element.24), channel_id=1, source_target_pairs={{0,2},{1,3},{2,0},{3,1},{4,6},{5,7},{6,4},{7,5},{8,10},{9,11},{10,... | collective-permute-start | bytes 36872 | tf_op jit(solution)/shard_map/ppermute | solution.py:58
  119.8 4.0 %copy-start = (bf16[256,384]{1,0:T(8,128)(2,1)S(1)}, bf16[256,384]{1,0:T(8,128)(2,1)}, u32[]{:S(2)}) copy-start(bf16[256,384]{1,0:T(8,128)(2,1)} %late.3.refs_0_) | copy-start | bytes 589828
  119.8 4.0 %copy-start.1 = (bf16[8,768]{1,0:T(8,128)(2,1)S(1)}, bf16[8,768]{1,0:T(8,128)(2,1)}, u32[]{:S(2)}) copy-start(bf16[8,768]{1,0:T(8,128)(2,1)} %get-tuple-element.22.refs_6_) | copy-start | bytes 36868
  119.8 4.0 %collective-permute-start.15 = (bf16[8,768]{1,0:T(8,128)(2,1)}, bf16[8,768]{1,0:T(8,128)(2,1)}, u32[]{:S(2)}, u32[]{:S(2)}) collective-permute-start(bf16[8,768]{1,0:T(8,128)(2,1)} %get-tuple-element.25), channel_id=1, source_target_pairs={{0,3},{1,0},{2,1},{3,2},{4,7},{5,4},{6,5},{7,6},{8,11},{9,8},{10,9... | collective-permute-start | bytes 36872 | tf_op jit(solution)/shard_map/ppermute | solution.py:58
  127.2 10.1 %collective-permute-start.16 = (bf16[272,384]{1,0:T(8,128)(2,1)S(1)}, bf16[272,384]{1,0:T(8,128)(2,1)S(1)}, u32[]{:S(2)}, u32[]{:S(2)}) collective-permute-start(bf16[272,384]{1,0:T(8,128)(2,1)S(1)} %get-tuple-element.27), channel_id=1, source_target_pairs={{0,4},{1,5},{2,6},{3,7},{4,0},{5,1},{6,2},{7,3},{8,12},{9,13},{10,... | collective-permute-start | bytes 626696 | tf_op jit(solution)/shard_map/ppermute | solution.py:62
  127.3 10.0 %collective-permute-start.9 = (bf16[256,384]{1,0:T(8,128)(2,1)S(1)}, bf16[256,384]{1,0:T(8,128)(2,1)S(1)}, u32[]{:S(2)}, u32[]{:S(2)}) collective-permute-start(bf16[256,384]{1,0:T(8,128)(2,1)S(1)} %get-tuple-element.21.refs_10_), channel_id=1, source_target_pairs={{0,4},{1,5},{2,6},{3,7},{4,0},{5,1},{6,2},{7,3},{8,12},{9,13},{10,... | collective-permute-start | bytes 589832 | tf_op jit(solution)/shard_map/ppermute | solution.py:62

commit v5 on v3

--- a/solution.py
+++ b/solution.py
@@ -381,14 +381,14 @@
     pass
 
 
-def after(x, *deps):
+def after(x, *deps, mib=60):
     return pl.pallas_call(
         after_kernel,
         out_shape=jax.ShapeDtypeStruct(x.shape, x.dtype),
         in_specs=[ANY] * (1 + len(deps)),
         out_specs=ANY,
         input_output_aliases={0: 0},
-        compiler_params=params(60),
+        compiler_params=params(mib),
         cost_estimate=cost(0, 1),
         name="after",
     )(x, *deps)
@@ -477,9 +477,9 @@
     every = lax.all_to_all(text, "tile", 0, 0, tiled=True).reshape(TEXT, 3 * W)
     far_up, far_dn = rows_on(far, 1), rows_on(far, -1)
     msg = text_part(every, kv)
-    pieces = split_proj(video_proj, msg)
+    pieces = split_proj(video_proj, side)
     proj = x_swap(pieces)
-    up, dn = after(up, msg, pieces), after(dn, msg, pieces)
+    up, dn = (after(r, msg, pieces, mib=1) for r in (up, dn))
     side_up, side_dn = other_core(up), other_core(dn)
     acc, m, l = early(
         window_mask, text_length, video_q, every, (kv, up, dn, side, side_up, side_dn)

time: 128 us -> 126 us (0.984)
  waiting for transfers between devices: 43.5 us -> 39.9 us
  starting transfers between devices: 41.8 us -> 43.6 us
    all_to_all x1, waiting for transfers between devices: 15.3 us -> 11.2 us  [per_device(): every = lax.all_to_all(text, 'tile', 0, 0, tiled=True).reshape(TEXT, 3 * W)]
    unnamed x16 -> x18, local copies, waits for them, and re-layouts: 5.85 us -> 4.93 us
  transfers between devices with their start and end apart: 17 -> 17, of which waited for: 4 -> 5; matrix products, arithmetic and copies ran while one was open for 0% -> 0% of each run, Pallas kernels for 22% -> 22%
where the time goes in v5:
time: 126 us; the launch traced here: 124 us
  starting transfers between devices  43.6 us (35%)
  waiting for transfers between devices  39.9 us (32%)
  Pallas kernels  34.5 us (27%)
  local copies, waits for them, and re-layouts  4.93 us (4%)
  between operations  1.42 us (1%)
    ppermute x3, waiting for transfers between devices, x_on(): lax.ppermute(x, 'head', [(i, i // 4 * 4 + (i + d) % 4) for i in range(8)])  12.2 us
    all_to_all x1, waiting for transfers between devices, per_device(): every = lax.all_to_all(text, 'tile', 0, 0, tiled=True).reshape(TEXT, 3 * W)  11.2 us
    pallas_call x1, Pallas kernels, early(): pl.pallas_call(early_kernel, out_shape=(part, part, part), in_specs=[SM,...  11 us
    all_to_all x1, starting transfers between devices, per_device(): every = lax.all_to_all(text, 'tile', 0, 0, tiled=True).reshape(TEXT, 3 * W)  10.6 us
    ppermute x1, waiting for transfers between devices, z_pair(): return lax.ppermute(x, 'head', [(i, i ^ 4) for i in range(8)])  9.71 us
    all_to_all x2, starting transfers between devices, x_swap(): return lax.all_to_all(x, 'head', 0, 0, tiled=True, axis_index_groups=groups)  8.58 us
    pallas_call x1, Pallas kernels, late(): pl.pallas_call(late_kernel, grid=(NH,), out_shape=jax.ShapeDtypeStruct((4...  6.97 us
    ppermute x4, starting transfers between devices, rows_on(): lax.ppermute(x, 'tile', [(i, (i // 8 + d) % 4 * 8 + i % 8) for i in range...  6.17 us
  transfers between devices with their start and end apart: 17, of which 5 were waited for; matrix products, arithmetic and copies ran while one was open for 0% of the time, Pallas kernels for 22%

profile of v5, /device:TPU:32, one launch (start us, length us, event | category | flops | bytes accessed | tf_op | source)
XLA Modules:
  0.0 124.3 jit_solution(8808709640442129838)
XLA Ops:
  0.6 2.2 %pack.1 = (bf16[1024,384]{1,0:T(8,128)(2,1)}, bf16[32,8,1152]{2,1,0:T(8,128)(2,1)}) custom-call(bf16[512,384]{1,0:T(8,128)(2,1)} %k_ref.1, bf16[512,384]{1,0:T(8,128)(2,1)} %v_ref.1, bf16[8,384]{1,0:T(8,128)(2,1)} %tq_ref.3, bf16[8,384]{1,0:T(8,128)(2,1)} %tk_ref.1, bf16[8,384]{1,0:T(8,128)(2,1)} %tv_ref.1), custom_call_target="tpu_custom_call" | custom-call | flops 1 | bytes 1 | tf_op jit(solution)/shard_map/pack/pallas_call | solution.py:365
  2.9 10.6 %all-to-all-start = ((bf16[32,8,1152]{2,1,0:T(8,128)(2,1)}), bf16[32,8,1152]{2,1,0:T(8,128)(2,1)S(1)}, u32[]{:S(2)}, u32[]{:S(2)}) async-start(bf16[32,8,1152]{2,1,0:T(8,128)(2,1)} %get-tuple-element.14), calls=%async_computation | async-start | bytes 1179648 | tf_op jit(solution)/shard_map/all_to_all | solution.py:477
  13.8 2.9 %collective-permute-start.5 = (bf16[1024,384]{1,0:T(8,128)(2,1)}, bf16[1024,384]{1,0:T(8,128)(2,1)}, u32[]{:S(2)}, u32[]{:S(2)}) collective-permute-start(bf16[1024,384]{1,0:T(8,128)(2,1)} %get-tuple-element.13.kv_ref.b0), channel_id=1, source_target_pairs={{0,192},{8,200},{16,208},{24,216},{32,224},{40,232},{48,240},{56,2... | collective-permute-start | bytes 2359304 | tf_op jit(solution)/shard_map/ppermute | solution.py:39
  16.8 3.3 %collective-permute-start = (bf16[1024,384]{1,0:T(8,128)(2,1)}, bf16[1024,384]{1,0:T(8,128)(2,1)}, u32[]{:S(2)}, u32[]{:S(2)}) collective-permute-start(bf16[1024,384]{1,0:T(8,128)(2,1)} %get-tuple-element.13.kv_ref.b0), channel_id=1, source_target_pairs={{0,56},{8,16},{16,8},{24,32},{32,24},{40,48},{48,40},{56,0},{64,12... | collective-permute-start | bytes 2359304 | tf_op jit(solution)/shard_map/ppermute | solution.py:43
  20.0 0.9 copy-done.6
  20.9 2.8 %split_proj.1.rest_1_ = bf16[4,192,768]{2,1,0:T(8,128)(2,1)} custom-call(bf16[384,3072]{1,0:T(8,128)(2,1)} %proj_ref.2, bf16[1024,384]{1,0:T(8,128)(2,1)} %copy-done.6), custom_call_target="tpu_custom_call" | custom-call | flops 1 | bytes 1 | tf_op jit(solution)/shard_map/split_proj/pallas_call | solution.py:329
  23.7 11.2 %all-to-all-done = bf16[32,8,1152]{2,1,0:T(8,128)(2,1)S(1)} async-done(((bf16[32,8,1152]{2,1,0:T(8,128)(2,1)}), bf16[32,8,1152]{2,1,0:T(8,128)(2,1)S(1)}, u32[]{:S(2)}, u32[]{:S(2)}) %all-to-all-start) | async-done | bytes 589856 | tf_op jit(solution)/shard_map/all_to_all | solution.py:477
  35.0 0.8 copy-done.5
  35.8 4.3 %all-to-all-start.2 = ((bf16[4,192,768]{2,1,0:T(8,128)(2,1)}), bf16[4,192,768]{2,1,0:T(8,128)(2,1)S(1)}, u32[]{:S(2)}, u32[]{:S(2)}) async-start(bf16[4,192,768]{2,1,0:T(8,128)(2,1)} %split_proj.1.rest_1_), calls=%async_computation.2 | async-start | bytes 2359296 | tf_op jit(solution)/shard_map/all_to_all | solution.py:54
  40.1 3.1 %text_part.1.rest_0_ = bf16[256,512]{1,0:T(8,128)(2,1)} custom-call(bf16[256,1152]{1,0:T(8,128)(2,1)} %bitcast.4, bf16[1024,384]{1,0:T(8,128)(2,1)} %get-tuple-element.13.kv_ref.b0), custom_call_target="tpu_custom_call" | custom-call | flops 1 | bytes 1 | tf_op jit(solution)/shard_map/text_part/pallas_call | solution.py:263
  43.2 0.9 copy-done.1
  44.2 1.8 %collective-permute-start.7 = (bf16[1024,384]{1,0:T(8,128)(2,1)}, bf16[1024,384]{1,0:T(8,128)(2,1)}, u32[]{:S(2)}, u32[]{:S(2)}) collective-permute-start(bf16[1024,384]{1,0:T(8,128)(2,1)} %after.4.b2), channel_id=1, source_target_pairs={{0,8},{8,0},{16,24},{24,16},{32,40},{40,32},{48,56},{56,48},{64,72... | collective-permute-start | bytes 2359304 | tf_op jit(solution)/shard_map/ppermute | solution.py:49
  46.0 0.9 collective-permute-start.6
  46.9 1.1 collective-permute-done.b0
  48.1 1.5 %collective-permute-start.1 = (bf16[1024,384]{1,0:T(8,128)(2,1)}, bf16[1024,384]{1,0:T(8,128)(2,1)}, u32[]{:S(2)}, u32[]{:S(2)}) collective-permute-start(bf16[1024,384]{1,0:T(8,128)(2,1)} %collective-permute-done.b0), channel_id=1, source_target_pairs={{0,64},{8,72},{16,80},{24,88},{32,96},{40,104},{48,112},{56,120},{... | collective-permute-start | bytes 2359304 | tf_op jit(solution)/shard_map/ppermute | solution.py:39
  49.5 1.8 %collective-permute-start.2 = (bf16[1024,384]{1,0:T(8,128)(2,1)}, bf16[1024,384]{1,0:T(8,128)(2,1)}, u32[]{:S(2)}, u32[]{:S(2)}) collective-permute-start(bf16[1024,384]{1,0:T(8,128)(2,1)} %collective-permute-done.b0), channel_id=1, source_target_pairs={{0,192},{8,200},{16,208},{24,216},{32,224},{40,232},{48,240},{56,2... | collective-permute-start | bytes 2359304 | tf_op jit(solution)/shard_map/ppermute | solution.py:39
  52.0 0.9 copy-done.8
  52.9 11.0 %early.1 = (f32[512,384]{1,0:T(8,128)}, f32[512,384]{1,0:T(8,128)}, f32[512,384]{1,0:T(8,128)}) custom-call(s32[2,27]{1,0:T(2,128)} %wm.3, s32[1]{0:T(128)S(6)} %copy.18.tlen, bf16[512,384]{1,0:T(8,128)(2,1)} %q_ref.3, bf16[256,1152]{1,0:T(8,128)(2,1)} %bitcast.5, bf16[1024,384]{1,0:T(8,128)(2,1)} %get-tuple-element.13.kv_ref.b0, ...), custom_call_target="tpu_custom_call" | custom-call | flops 1 | bytes 1 | tf_op jit(solution)/shard_map/early/pallas_call | solution.py:165
  63.9 5.3 %all-to-all-start.3 = ((bf16[32,8,512]{2,1,0:T(8,128)(2,1)}), bf16[32,8,512]{2,1,0:T(8,128)(2,1)S(1)}, u32[]{:S(2)}, u32[]{:S(2)}) async-start(bf16[32,8,512]{2,1,0:T(8,128)(2,1)} %after.5), calls=%async_computation.3 | async-start | bytes 524288 | tf_op jit(solution)/shard_map/all_to_all | solution.py:488
  69.6 7.0 %late.1 = bf16[4,512,384]{2,1,0:T(8,128)(2,1)} custom-call(s32[2,27]{1,0:T(2,128)} %wm.3, bf16[512,384]{1,0:T(8,128)(2,1)} %q_ref.3, bf16[1024,384]{1,0:T(8,128)(2,1)} %collective-permute-done.b0, bf16[1024,384]{1,0:T(8,128)(2,1)} %collective-permute-done.1.b1, bf16[1024,384]{1,0:T(8,128)(2,1)} %collective-permute-done.2.b2, ...), custom_call_target="tpu_custom_call" | custom-call | flops 1 | bytes 1 | tf_op jit(solution)/shard_map/late/pallas_call | solution.py:222
  76.5 5.5 %all-to-all-done.3 = bf16[32,8,512]{2,1,0:T(8,128)(2,1)S(1)} async-done(((bf16[32,8,512]{2,1,0:T(8,128)(2,1)}), bf16[32,8,512]{2,1,0:T(8,128)(2,1)S(1)}, u32[]{:S(2)}, u32[]{:S(2)}) %all-to-all-start.3) | async-done | bytes 262176 | tf_op jit(solution)/shard_map/all_to_all | solution.py:488
  82.1 0.7 copy-done.7
  82.8 4.3 %all-to-all-start.1 = ((bf16[4,512,384]{2,1,0:T(8,128)(2,1)}), bf16[4,512,384]{2,1,0:T(8,128)(2,1)S(1)}, u32[]{:S(2)}, u32[]{:S(2)}) async-start(bf16[4,512,384]{2,1,0:T(8,128)(2,1)} %late.1), calls=%async_computation.1 | async-start | bytes 3145728 | tf_op jit(solution)/shard_map/all_to_all | solution.py:54
  87.1 3.8 %text_merge.1 = (bf16[8,768]{1,0:T(8,128)(2,1)}, bf16[8,768]{1,0:T(8,128)(2,1)}, bf16[8,768]{1,0:T(8,128)(2,1)}, bf16[8,768]{1,0:T(8,128)(2,1)}) custom-call(s32[1]{0:T(128)S(6)} %copy.18.tlen, bf16[256,512]{1,0:T(8,128)(2,1)} %bitcast.7, bf16[8,384]{1,0:T(8,128)(2,1)} %tq_ref.3, bf16[256,1152]{1,0:T(8,128)(2,1)} %bitcast.6, bf16[384,3072]{1,0:T(8,128)(2,1)} %proj_ref.3), custom_call_target="tpu_custom_call" | custom-call | flops 1 | bytes 1 | tf_op jit(solution)/shard_map/text_merge/pallas_call | solution.py:308
  90.9 3.5 %collective-permute-start.10 = (bf16[8,768]{1,0:T(8,128)(2,1)}, bf16[8,768]{1,0:T(8,128)(2,1)S(1)}, u32[]{:S(2)}, u32[]{:S(2)}) collective-permute-start(bf16[8,768]{1,0:T(8,128)(2,1)} %get-tuple-element.20), channel_id=1, source_target_pairs={{0,2},{1,3},{2,0},{3,1},{4,6},{5,7},{6,4},{7,5},{8,10},{9,11},{10,... | collective-permute-start | bytes 36872 | tf_op jit(solution)/shard_map/ppermute | solution.py:58
  94.4 1.2 collective-permute-start.11
  95.6 0.9 collective-permute-start.9
  96.4 12.2 %collective-permute-done.10.t2 = bf16[8,768]{1,0:T(8,128)(2,1)S(1)} collective-permute-done((bf16[8,768]{1,0:T(8,128)(2,1)}, bf16[8,768]{1,0:T(8,128)(2,1)S(1)}, u32[]{:S(2)}, u32[]{:S(2)}) %collective-permute-start.10) | collective-permute-done | bytes 12320 | tf_op jit(solution)/shard_map/ppermute | solution.py:58
  108.7 0.7 copy-done.4
  109.4 3.7 %project.1 = (f32[528,384]{1,0:T(8,128)S(1)}, bf16[528,384]{1,0:T(8,128)(2,1)S(1)}) custom-call(bf16[4,512,384]{2,1,0:T(8,128)(2,1)S(1)} %all-to-all-done.1.a_ref, bf16[4,192,768]{2,1,0:T(8,128)(2,1)S(1)} %all-to-all-done.2.w_ref, bf16[4,192,768]{2,1,0:T(8,128)(2,1)} %collective-permute-done.8.v_ref, bf16[8,768]{1,0:T(8,128)(2,1)S(1)} %copy-done.4, ...), custom_call_target="tpu_custom_call" | custom-call | flops 1 | bytes 1 | tf_op jit(solution)/shard_map/project/pallas_call | solution.py:430
  113.7 9.7 %collective-permute-done.12.got_ref = bf16[528,384]{1,0:T(8,128)(2,1)S(1)} collective-permute-done((bf16[528,384]{1,0:T(8,128)(2,1)S(1)}, bf16[528,384]{1,0:T(8,128)(2,1)S(1)}, u32[]{:S(2)}, u32[]{:S(2)}) %collective-permute-start.12) | collective-permute-done | bytes 405536 | tf_op jit(solution)/shard_map/ppermute | solution.py:62
  123.5 0.8 add_up.1
  (31 shorter events, 1.5 us)
Async XLA Ops:
  2.9 32.1 %all-to-all-start = ((bf16[32,8,1152]{2,1,0:T(8,128)(2,1)}), bf16[32,8,1152]{2,1,0:T(8,128)(2,1)S(1)}, u32[]{:S(2)}, u32[]{:S(2)}) async-start(bf16[32,8,1152]{2,1,0:T(8,128)(2,1)} %get-tuple-element.14), calls=%async_computation | async-start | bytes 1179648 | tf_op jit(solution)/shard_map/all_to_all | solution.py:477
  13.5 6.6 %collective-permute-start.4 = (bf16[1024,384]{1,0:T(8,128)(2,1)}, bf16[1024,384]{1,0:T(8,128)(2,1)S(1)}, u32[]{:S(2)}, u32[]{:S(2)}) collective-permute-start(bf16[1024,384]{1,0:T(8,128)(2,1)} %get-tuple-element.13.kv_ref.b0), channel_id=1, source_target_pairs={{0,8},{8,0},{16,24},{24,16},{32,40},{40,32},{48,56},{56,48},{64,72... | collective-permute-start | bytes 2359304 | tf_op jit(solution)/shard_map/ppermute | solution.py:49
  13.8 29.4 %collective-permute-start.5 = (bf16[1024,384]{1,0:T(8,128)(2,1)}, bf16[1024,384]{1,0:T(8,128)(2,1)}, u32[]{:S(2)}, u32[]{:S(2)}) collective-permute-start(bf16[1024,384]{1,0:T(8,128)(2,1)} %get-tuple-element.13.kv_ref.b0), channel_id=1, source_target_pairs={{0,192},{8,200},{16,208},{24,216},{32,224},{40,232},{48,240},{56,2... | collective-permute-start | bytes 2359304 | tf_op jit(solution)/shard_map/ppermute | solution.py:39
  16.8 29.2 %collective-permute-start.3 = (bf16[1024,384]{1,0:T(8,128)(2,1)}, bf16[1024,384]{1,0:T(8,128)(2,1)S(1)}, u32[]{:S(2)}, u32[]{:S(2)}) collective-permute-start(bf16[1024,384]{1,0:T(8,128)(2,1)} %get-tuple-element.13.kv_ref.b0), channel_id=1, source_target_pairs={{0,64},{8,72},{16,80},{24,88},{32,96},{40,104},{48,112},{56,120},{... | collective-permute-start | bytes 2359304 | tf_op jit(solution)/shard_map/ppermute | solution.py:39
  16.8 31.3 %collective-permute-start = (bf16[1024,384]{1,0:T(8,128)(2,1)}, bf16[1024,384]{1,0:T(8,128)(2,1)}, u32[]{:S(2)}, u32[]{:S(2)}) collective-permute-start(bf16[1024,384]{1,0:T(8,128)(2,1)} %get-tuple-element.13.kv_ref.b0), channel_id=1, source_target_pairs={{0,56},{8,16},{16,8},{24,32},{32,24},{40,48},{48,40},{56,0},{64,12... | collective-permute-start | bytes 2359304 | tf_op jit(solution)/shard_map/ppermute | solution.py:43
  20.0 0.9 copy-start.6
  23.7 19.5 %copy-start = (bf16[4,192,768]{2,1,0:T(8,128)(2,1)S(1)}, bf16[4,192,768]{2,1,0:T(8,128)(2,1)}, u32[]{:S(2)}) copy-start(bf16[4,192,768]{2,1,0:T(8,128)(2,1)} %split_proj.1.rest_1_) | copy-start | bytes 3538948
  35.0 0.8 copy-start.5
  35.8 28.1 %all-to-all-start.2 = ((bf16[4,192,768]{2,1,0:T(8,128)(2,1)}), bf16[4,192,768]{2,1,0:T(8,128)(2,1)S(1)}, u32[]{:S(2)}, u32[]{:S(2)}) async-start(bf16[4,192,768]{2,1,0:T(8,128)(2,1)} %split_proj.1.rest_1_), calls=%async_computation.2 | async-start | bytes 2359296 | tf_op jit(solution)/shard_map/all_to_all | solution.py:54
  43.2 1.0 copy-start.1
  44.2 1.8 %copy-start.2 = (bf16[256,512]{1,0:T(8,128)(2,1)S(1)}, bf16[256,512]{1,0:T(8,128)(2,1)}, u32[]{:S(2)}) copy-start(bf16[256,512]{1,0:T(8,128)(2,1)} %text_part.1.rest_0_) | copy-start | bytes 786436
  44.2 7.7 %collective-permute-start.7 = (bf16[1024,384]{1,0:T(8,128)(2,1)}, bf16[1024,384]{1,0:T(8,128)(2,1)}, u32[]{:S(2)}, u32[]{:S(2)}) collective-permute-start(bf16[1024,384]{1,0:T(8,128)(2,1)} %after.4.b2), channel_id=1, source_target_pairs={{0,8},{8,0},{16,24},{24,16},{32,40},{40,32},{48,56},{56,48},{64,72... | collective-permute-start | bytes 2359304 | tf_op jit(solution)/shard_map/ppermute | solution.py:49
  46.0 6.0 %copy-start.3 = (bf16[1024,384]{1,0:T(8,128)(2,1)}, bf16[1024,384]{1,0:T(8,128)(2,1)S(1)}, u32[]{:S(2)}) copy-start(bf16[1024,384]{1,0:T(8,128)(2,1)S(1)} %after.3.b1) | copy-start | bytes 2359300
  46.0 6.0 %collective-permute-start.6 = (bf16[1024,384]{1,0:T(8,128)(2,1)S(1)}, bf16[1024,384]{1,0:T(8,128)(2,1)S(1)}, u32[]{:S(2)}, u32[]{:S(2)}) collective-permute-start(bf16[1024,384]{1,0:T(8,128)(2,1)S(1)} %after.3.b1), channel_id=1, source_target_pairs={{0,8},{8,0},{16,24},{24,16},{32,40},{40,32},{48,56},{56,48},{64,72... | collective-permute-start | bytes 2359304 | tf_op jit(solution)/shard_map/ppermute | solution.py:49
  48.1 21.5 %collective-permute-start.1 = (bf16[1024,384]{1,0:T(8,128)(2,1)}, bf16[1024,384]{1,0:T(8,128)(2,1)}, u32[]{:S(2)}, u32[]{:S(2)}) collective-permute-start(bf16[1024,384]{1,0:T(8,128)(2,1)} %collective-permute-done.b0), channel_id=1, source_target_pairs={{0,64},{8,72},{16,80},{24,88},{32,96},{40,104},{48,112},{56,120},{... | collective-permute-start | bytes 2359304 | tf_op jit(solution)/shard_map/ppermute | solution.py:39
  49.5 20.1 %collective-permute-start.2 = (bf16[1024,384]{1,0:T(8,128)(2,1)}, bf16[1024,384]{1,0:T(8,128)(2,1)}, u32[]{:S(2)}, u32[]{:S(2)}) collective-permute-start(bf16[1024,384]{1,0:T(8,128)(2,1)} %collective-permute-done.b0), channel_id=1, source_target_pairs={{0,192},{8,200},{16,208},{24,216},{32,224},{40,232},{48,240},{56,2... | collective-permute-start | bytes 2359304 | tf_op jit(solution)/shard_map/ppermute | solution.py:39
  52.0 0.9 copy-start.8
  63.9 18.2 %all-to-all-start.3 = ((bf16[32,8,512]{2,1,0:T(8,128)(2,1)}), bf16[32,8,512]{2,1,0:T(8,128)(2,1)S(1)}, u32[]{:S(2)}, u32[]{:S(2)}) async-start(bf16[32,8,512]{2,1,0:T(8,128)(2,1)} %after.5), calls=%async_computation.3 | async-start | bytes 524288 | tf_op jit(solution)/shard_map/all_to_all | solution.py:488
  69.2 39.4 %collective-permute-start.8 = (bf16[4,192,768]{2,1,0:T(8,128)(2,1)S(1)}, bf16[4,192,768]{2,1,0:T(8,128)(2,1)}, u32[]{:S(2)}, u32[]{:S(2)}) collective-permute-start(bf16[4,192,768]{2,1,0:T(8,128)(2,1)S(1)} %all-to-all-done.2.w_ref), channel_id=1, source_target_pairs={{0,8},{8,0},{16,24},{24,16},{32,40},{40,32},{48,56},{56,48},{64,72... | collective-permute-start | bytes 3538952 | tf_op jit(solution)/shard_map/ppermute | solution.py:49
  82.1 0.7 copy-start.7
  82.8 25.9 %all-to-all-start.1 = ((bf16[4,512,384]{2,1,0:T(8,128)(2,1)}), bf16[4,512,384]{2,1,0:T(8,128)(2,1)S(1)}, u32[]{:S(2)}, u32[]{:S(2)}) async-start(bf16[4,512,384]{2,1,0:T(8,128)(2,1)} %late.1), calls=%async_computation.1 | async-start | bytes 3145728 | tf_op jit(solution)/shard_map/all_to_all | solution.py:54
  90.9 17.8 %collective-permute-start.10 = (bf16[8,768]{1,0:T(8,128)(2,1)}, bf16[8,768]{1,0:T(8,128)(2,1)S(1)}, u32[]{:S(2)}, u32[]{:S(2)}) collective-permute-start(bf16[8,768]{1,0:T(8,128)(2,1)} %get-tuple-element.20), channel_id=1, source_target_pairs={{0,2},{1,3},{2,0},{3,1},{4,6},{5,7},{6,4},{7,5},{8,10},{9,11},{10,... | collective-permute-start | bytes 36872 | tf_op jit(solution)/shard_map/ppermute | solution.py:58
  94.4 14.2 %collective-permute-start.11 = (bf16[8,768]{1,0:T(8,128)(2,1)}, bf16[8,768]{1,0:T(8,128)(2,1)S(1)}, u32[]{:S(2)}, u32[]{:S(2)}) collective-permute-start(bf16[8,768]{1,0:T(8,128)(2,1)} %get-tuple-element.21), channel_id=1, source_target_pairs={{0,3},{1,0},{2,1},{3,2},{4,7},{5,4},{6,5},{7,6},{8,11},{9,8},{10,9... | collective-permute-start | bytes 36872 | tf_op jit(solution)/shard_map/ppermute | solution.py:58
  95.6 13.1 %collective-permute-start.9 = (bf16[8,768]{1,0:T(8,128)(2,1)}, bf16[8,768]{1,0:T(8,128)(2,1)S(1)}, u32[]{:S(2)}, u32[]{:S(2)}) collective-permute-start(bf16[8,768]{1,0:T(8,128)(2,1)} %get-tuple-element.19), channel_id=1, source_target_pairs={{0,1},{1,2},{2,3},{3,0},{4,5},{5,6},{6,7},{7,4},{8,9},{9,10},{10,1... | collective-permute-start | bytes 36872 | tf_op jit(solution)/shard_map/ppermute | solution.py:58
  108.7 0.7 copy-start.4
  113.1 10.4 %collective-permute-start.12 = (bf16[528,384]{1,0:T(8,128)(2,1)S(1)}, bf16[528,384]{1,0:T(8,128)(2,1)S(1)}, u32[]{:S(2)}, u32[]{:S(2)}) collective-permute-start(bf16[528,384]{1,0:T(8,128)(2,1)S(1)} %get-tuple-element.23), channel_id=1, source_target_pairs={{0,4},{1,5},{2,6},{3,7},{4,0},{5,1},{6,2},{7,3},{8,12},{9,13},{10,... | collective-permute-start | bytes 1216520 | tf_op jit(solution)/shard_map/ppermute | solution.py:62

commit v6 on v5

--- a/solution.py
+++ b/solution.py
@@ -212,8 +212,7 @@
             tot += fold(p, jnp.add)
             acc += jnp.dot(p.astype(BF16), blocks[b][ROWS:, :], preferred_element_type=F32)
         o = (acc / jnp.sum(tot, axis=1, keepdims=True)).astype(BF16)
-        for x in range(4):
-            o_ref[x, rs, :] = o
+        o_ref[rs, :] = o
 
 
 def late(wm, q, far, acc, m, l, *deps):
@@ -222,9 +221,9 @@
     return pl.pallas_call(
         late_kernel,
         grid=(NH,),
-        out_shape=jax.ShapeDtypeStruct((4, ROWS, W), BF16),
+        out_shape=jax.ShapeDtypeStruct((ROWS, W), BF16),
         in_specs=[SM, head, block, block, block, head, head, head] + [ANY] * len(deps),
-        out_specs=pl.BlockSpec((4, ROWS, HD), lambda i: (0, 0, i)),
+        out_specs=head,
         compiler_params=params(60),
         cost_estimate=cost(12 * ROWS * ROWS * W, 2 * 2**20, 3 * ROWS * ROWS),
         name="late",
@@ -395,19 +394,21 @@
 
 
 def project_kernel(
-    a_ref, w_ref, v_ref, t0, t1, t2, t3, own_ref, away_ref, abuf, wbuf, acc, sem
+    a0, a1, a2, a3, w_ref, v_ref, t0, t1, t2, t3, own_ref, away_ref, abuf, wbuf, acc, sem
 ):
     core = lax.rem(lax.axis_index("tile"), 2)
+    me = lax.rem(lax.axis_index("head"), 4)
     copies = []
-    for x in range(4):
+    for d, a_ref in enumerate((a0, a1, a2, a3)):
+        x = lax.rem(me + 4 - d, 4)
         for i, (src, dst) in enumerate(
             (
-                (w_ref, wbuf.at[x, pl.ds(pl.multiple_of(core * HALF, 16), HALF)]),
-                (v_ref, wbuf.at[x, pl.ds(pl.multiple_of((1 - core) * HALF, 16), HALF)]),
-                (a_ref, abuf.at[x]),
+                (w_ref.at[x], wbuf.at[d, pl.ds(pl.multiple_of(core * HALF, 16), HALF)]),
+                (v_ref.at[x], wbuf.at[d, pl.ds(pl.multiple_of((1 - core) * HALF, 16), HALF)]),
+                (a_ref, abuf.at[d]),
             )
         ):
-            copies.append(pltpu.make_async_copy(src.at[x], dst, sem.at[3 * x + i]))
+            copies.append(pltpu.make_async_copy(src, dst, sem.at[3 * d + i]))
             copies[-1].start()
     t = sum(r[...].astype(F32) for r in (t0, t1, t2, t3))
     t = jnp.concatenate([t, jnp.zeros_like(t)], axis=0)
@@ -433,7 +434,7 @@
             jax.ShapeDtypeStruct((ROWS + 16, W), F32),
             jax.ShapeDtypeStruct((ROWS + 16, W), BF16),
         ),
-        in_specs=[ANY] * 3 + [VM] * 4,
+        in_specs=[ANY] * 6 + [VM] * 4,
         out_specs=(VM, VM),
         scratch_shapes=[
             pltpu.VMEM((4, ROWS, W), BF16),
@@ -444,7 +445,7 @@
         compiler_params=params(24),
         cost_estimate=cost(2 * ROWS * 4 * W * 2 * W, 6 * 2**20),
         name="project",
-    )(attn, *proj, *text)
+    )(*attn, *proj, *text)
 
 
 def add_kernel(own_ref, got_ref, video_ref, text_ref):
@@ -487,7 +488,8 @@
     msg = after(msg.reshape(32, TL, W + HD), acc)
     got = lax.all_to_all(msg, "tile", 0, 0, tiled=True).reshape(TEXT, W + HD)
 
-    attn = x_swap(late(window_mask, video_q, (far, far_up, far_dn), acc, m, l))
+    attn = late(window_mask, video_q, (far, far_up, far_dn), acc, m, l)
+    attn = [x_on(attn, d) if d else attn for d in range(4)]
     parts = text_merge(text_length, got, text_q, every, text_proj)
     parts = [x_on(p, d) if d else p for d, p in enumerate(parts)]
     own, away = project(attn, (proj, other_core(proj)), parts)

time: 126 us -> 135 us (1.071)
  waiting for transfers between devices: 39.9 us -> 50 us
  starting transfers between devices: 43.6 us -> 39.2 us
  local copies, waits for them, and re-layouts: 4.93 us -> 6.85 us
    ppermute x1, waiting for transfers between devices: 1.13 us -> 12.9 us  [over_chip(): lax.ppermute(x, 'tile', [(i, i // 8 * 8 + (i % 8 + (1 if i % 2 else -1))...]
    all_to_all x1, waiting for transfers between devices: 5.54 us -> 0.01 us  [per_device(): got = lax.all_to_all(msg, 'tile', 0, 0, tiled=True).reshape(TEXT, W + HD)]
    all_to_all x2 -> x1, starting transfers between devices: 8.58 us -> 4.29 us  [x_swap(): return lax.all_to_all(x, 'head', 0, 0, tiled=True, axis_index_groups=groups)]
    ppermute x3 -> x6, waiting for transfers between devices: 12.2 us -> 15.9 us  [x_on(): lax.ppermute(x, 'head', [(i, i // 4 * 4 + (i + d) % 4) for i in range(8)])]
    ppermute x1, starting transfers between devices: 3.28 us -> 0.01 us  [over_chip(): lax.ppermute(x, 'tile', [(i, i // 8 * 8 + (i % 8 + (1 if i % 2 else -1))...]
    ppermute x1, waiting for transfers between devices: 9.71 us -> 6.97 us  [z_pair(): return lax.ppermute(x, 'head', [(i, i ^ 4) for i in range(8)])]
    unnamed x18 -> x24, local copies, waits for them, and re-layouts: 4.93 us -> 6.85 us
    all_to_all x1, waiting for transfers between devices: 11.2 us -> 13.2 us  [per_device(): every = lax.all_to_all(text, 'tile', 0, 0, tiled=True).reshape(TEXT, 3 * W)]
  transfers between devices with their start and end apart: 17 -> 19, of which waited for: 5 -> 9; matrix products, arithmetic and copies ran while one was open for 0% -> 0% of each run, Pallas kernels for 22% -> 21%
where the time goes in v6:
time: 135 us; the launch traced here: 132 us
  waiting for transfers between devices  50 us (37%)
  starting transfers between devices  39.2 us (29%)
  Pallas kernels  34.7 us (26%)
  local copies, waits for them, and re-layouts  6.85 us (5%)
  between operations  1.4 us (1%)
    ppermute x6, waiting for transfers between devices, x_on(): lax.ppermute(x, 'head', [(i, i // 4 * 4 + (i + d) % 4) for i in range(8)])  15.9 us
    all_to_all x1, waiting for transfers between devices, per_device(): every = lax.all_to_all(text, 'tile', 0, 0, tiled=True).reshape(TEXT, 3 * W)  13.2 us
    ppermute x1, waiting for transfers between devices, over_chip(): lax.ppermute(x, 'tile', [(i, i // 8 * 8 + (i % 8 + (1 if i % 2 else -1))...  12.9 us
    pallas_call x1, Pallas kernels, early(): pl.pallas_call(early_kernel, out_shape=(part, part, part), in_specs=[SM,...  11 us
    all_to_all x1, starting transfers between devices, per_device(): every = lax.all_to_all(text, 'tile', 0, 0, tiled=True).reshape(TEXT, 3 * W)  10.6 us
    ppermute x6, starting transfers between devices, x_on(): lax.ppermute(x, 'head', [(i, i // 4 * 4 + (i + d) % 4) for i in range(8)])  7.32 us
    ppermute x1, waiting for transfers between devices, z_pair(): return lax.ppermute(x, 'head', [(i, i ^ 4) for i in range(8)])  6.97 us
    unnamed x24, local copies, waits for them, and re-layouts  6.85 us
  transfers between devices with their start and end apart: 19, of which 9 were waited for; matrix products, arithmetic and copies ran while one was open for 0% of the time, Pallas kernels for 21%

profile of v6, /device:TPU:32, one launch (start us, length us, event | category | flops | bytes accessed | tf_op | source)
XLA Modules:
  0.0 132.2 jit_solution(2277220888571790291)
XLA Ops:
  0.6 2.3 %pack.1 = (bf16[1024,384]{1,0:T(8,128)(2,1)}, bf16[32,8,1152]{2,1,0:T(8,128)(2,1)}) custom-call(bf16[512,384]{1,0:T(8,128)(2,1)} %k_ref.1, bf16[512,384]{1,0:T(8,128)(2,1)} %v_ref.1, bf16[8,384]{1,0:T(8,128)(2,1)} %tq_ref.3, bf16[8,384]{1,0:T(8,128)(2,1)} %tk_ref.1, bf16[8,384]{1,0:T(8,128)(2,1)} %tv_ref.1), custom_call_target="tpu_custom_call" | custom-call | flops 1 | bytes 1 | tf_op jit(solution)/shard_map/pack/pallas_call | solution.py:364
  2.9 10.6 %all-to-all-start = ((bf16[32,8,1152]{2,1,0:T(8,128)(2,1)}), bf16[32,8,1152]{2,1,0:T(8,128)(2,1)S(1)}, u32[]{:S(2)}, u32[]{:S(2)}) async-start(bf16[32,8,1152]{2,1,0:T(8,128)(2,1)} %get-tuple-element.14), calls=%async_computation | async-start | bytes 1179648 | tf_op jit(solution)/shard_map/all_to_all | solution.py:478
  13.9 2.9 %collective-permute-start.5 = (bf16[1024,384]{1,0:T(8,128)(2,1)}, bf16[1024,384]{1,0:T(8,128)(2,1)}, u32[]{:S(2)}, u32[]{:S(2)}) collective-permute-start(bf16[1024,384]{1,0:T(8,128)(2,1)} %get-tuple-element.13.kv_ref.b0), channel_id=1, source_target_pairs={{0,192},{8,200},{16,208},{24,216},{32,224},{40,232},{48,240},{56,2... | collective-permute-start | bytes 2359304 | tf_op jit(solution)/shard_map/ppermute | solution.py:39
  16.8 0.9 copy-done.11
  17.7 2.8 %split_proj.1.rest_1_ = bf16[4,192,768]{2,1,0:T(8,128)(2,1)} custom-call(bf16[384,3072]{1,0:T(8,128)(2,1)} %proj_ref.2, bf16[1024,384]{1,0:T(8,128)(2,1)} %copy-done.11), custom_call_target="tpu_custom_call" | custom-call | flops 1 | bytes 1 | tf_op jit(solution)/shard_map/split_proj/pallas_call | solution.py:328
  20.5 13.2 %all-to-all-done = bf16[32,8,1152]{2,1,0:T(8,128)(2,1)S(1)} async-done(((bf16[32,8,1152]{2,1,0:T(8,128)(2,1)}), bf16[32,8,1152]{2,1,0:T(8,128)(2,1)S(1)}, u32[]{:S(2)}, u32[]{:S(2)}) %all-to-all-start) | async-done | bytes 589856 | tf_op jit(solution)/shard_map/all_to_all | solution.py:478
  33.7 0.8 copy-done.10
  34.5 4.3 %all-to-all-start.1 = ((bf16[4,192,768]{2,1,0:T(8,128)(2,1)}), bf16[4,192,768]{2,1,0:T(8,128)(2,1)S(1)}, u32[]{:S(2)}, u32[]{:S(2)}) async-start(bf16[4,192,768]{2,1,0:T(8,128)(2,1)} %split_proj.1.rest_1_), calls=%async_computation.1 | async-start | bytes 2359296 | tf_op jit(solution)/shard_map/all_to_all | solution.py:54
  38.8 3.2 %text_part.1.rest_0_ = bf16[256,512]{1,0:T(8,128)(2,1)} custom-call(bf16[256,1152]{1,0:T(8,128)(2,1)} %bitcast.4, bf16[1024,384]{1,0:T(8,128)(2,1)} %get-tuple-element.13.kv_ref.b0), custom_call_target="tpu_custom_call" | custom-call | flops 1 | bytes 1 | tf_op jit(solution)/shard_map/text_part/pallas_call | solution.py:262
  42.1 0.9 copy-done.1
  43.0 1.4 %collective-permute-start.7 = (bf16[1024,384]{1,0:T(8,128)(2,1)}, bf16[1024,384]{1,0:T(8,128)(2,1)}, u32[]{:S(2)}, u32[]{:S(2)}) collective-permute-start(bf16[1024,384]{1,0:T(8,128)(2,1)} %after.4.b2), channel_id=1, source_target_pairs={{0,8},{8,0},{16,24},{24,16},{32,40},{40,32},{48,56},{56,48},{64,72... | collective-permute-start | bytes 2359304 | tf_op jit(solution)/shard_map/ppermute | solution.py:49
  44.4 0.9 collective-permute-start.6
  45.3 12.9 %collective-permute-done.b0 = bf16[1024,384]{1,0:T(8,128)(2,1)} collective-permute-done((bf16[1024,384]{1,0:T(8,128)(2,1)}, bf16[1024,384]{1,0:T(8,128)(2,1)}, u32[]{:S(2)}, u32[]{:S(2)}) %collective-permute-start) | collective-permute-done | bytes 786464 | tf_op jit(solution)/shard_map/ppermute | solution.py:43
  58.2 1.7 %collective-permute-start.1 = (bf16[1024,384]{1,0:T(8,128)(2,1)}, bf16[1024,384]{1,0:T(8,128)(2,1)}, u32[]{:S(2)}, u32[]{:S(2)}) collective-permute-start(bf16[1024,384]{1,0:T(8,128)(2,1)} %collective-permute-done.b0), channel_id=1, source_target_pairs={{0,64},{8,72},{16,80},{24,88},{32,96},{40,104},{48,112},{56,120},{... | collective-permute-start | bytes 2359304 | tf_op jit(solution)/shard_map/ppermute | solution.py:39
  59.9 1.5 %collective-permute-start.2 = (bf16[1024,384]{1,0:T(8,128)(2,1)}, bf16[1024,384]{1,0:T(8,128)(2,1)}, u32[]{:S(2)}, u32[]{:S(2)}) collective-permute-start(bf16[1024,384]{1,0:T(8,128)(2,1)} %collective-permute-done.b0), channel_id=1, source_target_pairs={{0,192},{8,200},{16,208},{24,216},{32,224},{40,232},{48,240},{56,2... | collective-permute-start | bytes 2359304 | tf_op jit(solution)/shard_map/ppermute | solution.py:39
  61.5 1.1 collective-permute-start.11
  63.3 11.0 %early.1 = (f32[512,384]{1,0:T(8,128)}, f32[512,384]{1,0:T(8,128)}, f32[512,384]{1,0:T(8,128)}) custom-call(s32[2,27]{1,0:T(2,128)} %wm.3, s32[1]{0:T(128)S(6)} %copy.18.tlen, bf16[512,384]{1,0:T(8,128)(2,1)} %q_ref.3, bf16[256,1152]{1,0:T(8,128)(2,1)} %bitcast.5, bf16[1024,384]{1,0:T(8,128)(2,1)} %get-tuple-element.13.kv_ref.b0, ...), custom_call_target="tpu_custom_call" | custom-call | flops 1 | bytes 1 | tf_op jit(solution)/shard_map/early/pallas_call | solution.py:165
  74.3 4.6 %all-to-all-start.2 = ((bf16[32,8,512]{2,1,0:T(8,128)(2,1)}), bf16[32,8,512]{2,1,0:T(8,128)(2,1)}, u32[]{:S(2)}, u32[]{:S(2)}) async-start(bf16[32,8,512]{2,1,0:T(8,128)(2,1)} %after.5), calls=%async_computation.2 | async-start | bytes 524288 | tf_op jit(solution)/shard_map/all_to_all | solution.py:489
  80.0 6.7 %late.1.a0 = bf16[512,384]{1,0:T(8,128)(2,1)} custom-call(s32[2,27]{1,0:T(2,128)} %wm.3, bf16[512,384]{1,0:T(8,128)(2,1)} %q_ref.3, bf16[1024,384]{1,0:T(8,128)(2,1)} %collective-permute-done.b0, bf16[1024,384]{1,0:T(8,128)(2,1)} %collective-permute-done.1.b1, bf16[1024,384]{1,0:T(8,128)(2,1)} %collective-permute-done.2.b2, ...), custom_call_target="tpu_custom_call" | custom-call | flops 1 | bytes 1 | tf_op jit(solution)/shard_map/late/pallas_call | solution.py:221
  86.7 3.1 %collective-permute-start.10 = (bf16[512,384]{1,0:T(8,128)(2,1)}, bf16[512,384]{1,0:T(8,128)(2,1)S(1)}, u32[]{:S(2)}, u32[]{:S(2)}) collective-permute-start(bf16[512,384]{1,0:T(8,128)(2,1)} %late.1.a0), channel_id=1, source_target_pairs={{0,3},{1,0},{2,1},{3,2},{4,7},{5,4},{6,5},{7,6},{8,11},{9,8},{10,9... | collective-permute-start | bytes 1179656 | tf_op jit(solution)/shard_map/ppermute | solution.py:58
  89.8 2.3 %collective-permute-start.9 = (bf16[512,384]{1,0:T(8,128)(2,1)}, bf16[512,384]{1,0:T(8,128)(2,1)S(1)}, u32[]{:S(2)}, u32[]{:S(2)}) collective-permute-start(bf16[512,384]{1,0:T(8,128)(2,1)} %late.1.a0), channel_id=1, source_target_pairs={{0,2},{1,3},{2,0},{3,1},{4,6},{5,7},{6,4},{7,5},{8,10},{9,11},{10,... | collective-permute-start | bytes 1179656 | tf_op jit(solution)/shard_map/ppermute | solution.py:58
  92.1 3.8 %text_merge.1 = (bf16[8,768]{1,0:T(8,128)(2,1)}, bf16[8,768]{1,0:T(8,128)(2,1)}, bf16[8,768]{1,0:T(8,128)(2,1)}, bf16[8,768]{1,0:T(8,128)(2,1)}) custom-call(s32[1]{0:T(128)S(6)} %copy.18.tlen, bf16[256,512]{1,0:T(8,128)(2,1)} %bitcast.2.msg_ref, bf16[8,384]{1,0:T(8,128)(2,1)} %tq_ref.3, bf16[256,1152]{1,0:T(8,128)(2,1)} %bitcast.6, bf16[384,3072]{1,0:T(8,128)(2,1)} %proj_ref.3), custom_call_target="tpu_custom_call" | custom-call | flops 1 | bytes 1 | tf_op jit(solution)/shard_map/text_merge/pallas_call | solution.py:307
  95.9 1.8 %collective-permute-start.12 = (bf16[8,768]{1,0:T(8,128)(2,1)}, bf16[8,768]{1,0:T(8,128)(2,1)S(1)}, u32[]{:S(2)}, u32[]{:S(2)}) collective-permute-start(bf16[8,768]{1,0:T(8,128)(2,1)} %get-tuple-element.19), channel_id=1, source_target_pairs={{0,1},{1,2},{2,3},{3,0},{4,5},{5,6},{6,7},{7,4},{8,9},{9,10},{10,1... | collective-permute-start | bytes 36872 | tf_op jit(solution)/shard_map/ppermute | solution.py:58
  97.7 9.5 %collective-permute-done.10.a3 = bf16[512,384]{1,0:T(8,128)(2,1)S(1)} collective-permute-done((bf16[512,384]{1,0:T(8,128)(2,1)}, bf16[512,384]{1,0:T(8,128)(2,1)S(1)}, u32[]{:S(2)}, u32[]{:S(2)}) %collective-permute-start.10) | collective-permute-done | bytes 393248 | tf_op jit(solution)/shard_map/ppermute | solution.py:58
  107.2 3.4 %collective-permute-done.8.a1 = bf16[512,384]{1,0:T(8,128)(2,1)S(1)} collective-permute-done((bf16[512,384]{1,0:T(8,128)(2,1)}, bf16[512,384]{1,0:T(8,128)(2,1)S(1)}, u32[]{:S(2)}, u32[]{:S(2)}) %collective-permute-start.8) | collective-permute-done | bytes 393248 | tf_op jit(solution)/shard_map/ppermute | solution.py:58
  112.7 2.7 %collective-permute-done.14.t3 = bf16[8,768]{1,0:T(8,128)(2,1)S(1)} collective-permute-done((bf16[8,768]{1,0:T(8,128)(2,1)}, bf16[8,768]{1,0:T(8,128)(2,1)S(1)}, u32[]{:S(2)}, u32[]{:S(2)}) %collective-permute-start.14) | collective-permute-done | bytes 12320 | tf_op jit(solution)/shard_map/ppermute | solution.py:58
  115.3 1.0 copy-done.6
  116.3 1.0 copy-done.8
  118.0 3.9 %project.1 = (f32[528,384]{1,0:T(8,128)S(1)}, bf16[528,384]{1,0:T(8,128)(2,1)S(1)}) custom-call(bf16[512,384]{1,0:T(8,128)(2,1)S(1)} %copy-done.4, bf16[512,384]{1,0:T(8,128)(2,1)S(1)} %copy-done.6, bf16[512,384]{1,0:T(8,128)(2,1)S(1)} %copy-done.8, bf16[512,384]{1,0:T(8,128)(2,1)S(1)} %collective-permute-done.10.a3, ...), custom_call_target="tpu_custom_call" | custom-call | flops 1 | bytes 1 | tf_op jit(solution)/shard_map/project/pallas_call | solution.py:431
  122.0 2.4 %collective-permute-start.15 = (bf16[528,384]{1,0:T(8,128)(2,1)S(1)}, bf16[528,384]{1,0:T(8,128)(2,1)S(1)}, u32[]{:S(2)}, u32[]{:S(2)}) collective-permute-start(bf16[528,384]{1,0:T(8,128)(2,1)S(1)} %get-tuple-element.23), channel_id=1, source_target_pairs={{0,4},{1,5},{2,6},{3,7},{4,0},{5,1},{6,2},{7,3},{8,12},{9,13},{10,... | collective-permute-start | bytes 1216520 | tf_op jit(solution)/shard_map/ppermute | solution.py:62
  124.4 7.0 %collective-permute-done.15.got_ref = bf16[528,384]{1,0:T(8,128)(2,1)S(1)} collective-permute-done((bf16[528,384]{1,0:T(8,128)(2,1)S(1)}, bf16[528,384]{1,0:T(8,128)(2,1)S(1)}, u32[]{:S(2)}, u32[]{:S(2)}) %collective-permute-start.15) | collective-permute-done | bytes 405536 | tf_op jit(solution)/shard_map/ppermute | solution.py:62
  131.4 0.8 add_up.1
  (41 shorter events, 4.2 us)
Async XLA Ops:
  2.9 30.8 %all-to-all-start = ((bf16[32,8,1152]{2,1,0:T(8,128)(2,1)}), bf16[32,8,1152]{2,1,0:T(8,128)(2,1)S(1)}, u32[]{:S(2)}, u32[]{:S(2)}) async-start(bf16[32,8,1152]{2,1,0:T(8,128)(2,1)} %get-tuple-element.14), calls=%async_computation | async-start | bytes 1179648 | tf_op jit(solution)/shard_map/all_to_all | solution.py:478
  13.5 3.3 %collective-permute-start.4 = (bf16[1024,384]{1,0:T(8,128)(2,1)}, bf16[1024,384]{1,0:T(8,128)(2,1)S(1)}, u32[]{:S(2)}, u32[]{:S(2)}) collective-permute-start(bf16[1024,384]{1,0:T(8,128)(2,1)} %get-tuple-element.13.kv_ref.b0), channel_id=1, source_target_pairs={{0,8},{8,0},{16,24},{24,16},{32,40},{40,32},{48,56},{56,48},{64,72... | collective-permute-start | bytes 2359304 | tf_op jit(solution)/shard_map/ppermute | solution.py:49
  13.9 28.2 %collective-permute-start.5 = (bf16[1024,384]{1,0:T(8,128)(2,1)}, bf16[1024,384]{1,0:T(8,128)(2,1)}, u32[]{:S(2)}, u32[]{:S(2)}) collective-permute-start(bf16[1024,384]{1,0:T(8,128)(2,1)} %get-tuple-element.13.kv_ref.b0), channel_id=1, source_target_pairs={{0,192},{8,200},{16,208},{24,216},{32,224},{40,232},{48,240},{56,2... | collective-permute-start | bytes 2359304 | tf_op jit(solution)/shard_map/ppermute | solution.py:39
  16.8 27.6 %collective-permute-start.3 = (bf16[1024,384]{1,0:T(8,128)(2,1)}, bf16[1024,384]{1,0:T(8,128)(2,1)S(1)}, u32[]{:S(2)}, u32[]{:S(2)}) collective-permute-start(bf16[1024,384]{1,0:T(8,128)(2,1)} %get-tuple-element.13.kv_ref.b0), channel_id=1, source_target_pairs={{0,64},{8,72},{16,80},{24,88},{32,96},{40,104},{48,112},{56,120},{... | collective-permute-start | bytes 2359304 | tf_op jit(solution)/shard_map/ppermute | solution.py:39
  16.8 0.9 copy-start.11
  33.7 0.8 copy-start.10
  34.5 27.0 %all-to-all-start.1 = ((bf16[4,192,768]{2,1,0:T(8,128)(2,1)}), bf16[4,192,768]{2,1,0:T(8,128)(2,1)S(1)}, u32[]{:S(2)}, u32[]{:S(2)}) async-start(bf16[4,192,768]{2,1,0:T(8,128)(2,1)} %split_proj.1.rest_1_), calls=%async_computation.1 | async-start | bytes 2359296 | tf_op jit(solution)/shard_map/all_to_all | solution.py:54
  38.8 3.3 %copy-start = (bf16[4,192,768]{2,1,0:T(8,128)(2,1)S(1)}, bf16[4,192,768]{2,1,0:T(8,128)(2,1)}, u32[]{:S(2)}) copy-start(bf16[4,192,768]{2,1,0:T(8,128)(2,1)} %split_proj.1.rest_1_) | copy-start | bytes 3538948
  38.8 19.4 %collective-permute-start = (bf16[1024,384]{1,0:T(8,128)(2,1)}, bf16[1024,384]{1,0:T(8,128)(2,1)}, u32[]{:S(2)}, u32[]{:S(2)}) collective-permute-start(bf16[1024,384]{1,0:T(8,128)(2,1)} %get-tuple-element.13.kv_ref.b0), channel_id=1, source_target_pairs={{0,56},{8,16},{16,8},{24,32},{32,24},{40,48},{48,40},{56,0},{64,12... | collective-permute-start | bytes 2359304 | tf_op jit(solution)/shard_map/ppermute | solution.py:43
  42.1 1.0 copy-start.1
  43.0 1.4 %copy-start.2 = (bf16[256,512]{1,0:T(8,128)(2,1)S(1)}, bf16[256,512]{1,0:T(8,128)(2,1)}, u32[]{:S(2)}) copy-start(bf16[256,512]{1,0:T(8,128)(2,1)} %text_part.1.rest_0_) | copy-start | bytes 786436
  43.0 20.2 %collective-permute-start.7 = (bf16[1024,384]{1,0:T(8,128)(2,1)}, bf16[1024,384]{1,0:T(8,128)(2,1)}, u32[]{:S(2)}, u32[]{:S(2)}) collective-permute-start(bf16[1024,384]{1,0:T(8,128)(2,1)} %after.4.b2), channel_id=1, source_target_pairs={{0,8},{8,0},{16,24},{24,16},{32,40},{40,32},{48,56},{56,48},{64,72... | collective-permute-start | bytes 2359304 | tf_op jit(solution)/shard_map/ppermute | solution.py:49
  44.4 18.9 %copy-start.3 = (bf16[1024,384]{1,0:T(8,128)(2,1)}, bf16[1024,384]{1,0:T(8,128)(2,1)S(1)}, u32[]{:S(2)}) copy-start(bf16[1024,384]{1,0:T(8,128)(2,1)S(1)} %after.3.b1) | copy-start | bytes 2359300
  44.4 18.8 %collective-permute-start.6 = (bf16[1024,384]{1,0:T(8,128)(2,1)S(1)}, bf16[1024,384]{1,0:T(8,128)(2,1)}, u32[]{:S(2)}, u32[]{:S(2)}) collective-permute-start(bf16[1024,384]{1,0:T(8,128)(2,1)S(1)} %after.3.b1), channel_id=1, source_target_pairs={{0,8},{8,0},{16,24},{24,16},{32,40},{40,32},{48,56},{56,48},{64,72... | collective-permute-start | bytes 2359304 | tf_op jit(solution)/shard_map/ppermute | solution.py:49
  58.2 21.3 %collective-permute-start.1 = (bf16[1024,384]{1,0:T(8,128)(2,1)}, bf16[1024,384]{1,0:T(8,128)(2,1)}, u32[]{:S(2)}, u32[]{:S(2)}) collective-permute-start(bf16[1024,384]{1,0:T(8,128)(2,1)} %collective-permute-done.b0), channel_id=1, source_target_pairs={{0,64},{8,72},{16,80},{24,88},{32,96},{40,104},{48,112},{56,120},{... | collective-permute-start | bytes 2359304 | tf_op jit(solution)/shard_map/ppermute | solution.py:39
  59.9 20.1 %collective-permute-start.2 = (bf16[1024,384]{1,0:T(8,128)(2,1)}, bf16[1024,384]{1,0:T(8,128)(2,1)}, u32[]{:S(2)}, u32[]{:S(2)}) collective-permute-start(bf16[1024,384]{1,0:T(8,128)(2,1)} %collective-permute-done.b0), channel_id=1, source_target_pairs={{0,192},{8,200},{16,208},{24,216},{32,224},{40,232},{48,240},{56,2... | collective-permute-start | bytes 2359304 | tf_op jit(solution)/shard_map/ppermute | solution.py:39
  61.5 53.9 %collective-permute-start.11 = (bf16[4,192,768]{2,1,0:T(8,128)(2,1)S(1)}, bf16[4,192,768]{2,1,0:T(8,128)(2,1)S(1)}, u32[]{:S(2)}, u32[]{:S(2)}) collective-permute-start(bf16[4,192,768]{2,1,0:T(8,128)(2,1)S(1)} %all-to-all-done.1.w_ref), channel_id=1, source_target_pairs={{0,8},{8,0},{16,24},{24,16},{32,40},{40,32},{48,56},{56,48},{64,72... | collective-permute-start | bytes 3538952 | tf_op jit(solution)/shard_map/ppermute | solution.py:49
  74.3 17.8 %all-to-all-start.2 = ((bf16[32,8,512]{2,1,0:T(8,128)(2,1)}), bf16[32,8,512]{2,1,0:T(8,128)(2,1)}, u32[]{:S(2)}, u32[]{:S(2)}) async-start(bf16[32,8,512]{2,1,0:T(8,128)(2,1)} %after.5), calls=%async_computation.2 | async-start | bytes 524288 | tf_op jit(solution)/shard_map/all_to_all | solution.py:489
  86.7 20.5 %collective-permute-start.10 = (bf16[512,384]{1,0:T(8,128)(2,1)}, bf16[512,384]{1,0:T(8,128)(2,1)S(1)}, u32[]{:S(2)}, u32[]{:S(2)}) collective-permute-start(bf16[512,384]{1,0:T(8,128)(2,1)} %late.1.a0), channel_id=1, source_target_pairs={{0,3},{1,0},{2,1},{3,2},{4,7},{5,4},{6,5},{7,6},{8,11},{9,8},{10,9... | collective-permute-start | bytes 1179656 | tf_op jit(solution)/shard_map/ppermute | solution.py:58
  89.8 20.9 %collective-permute-start.8 = (bf16[512,384]{1,0:T(8,128)(2,1)}, bf16[512,384]{1,0:T(8,128)(2,1)S(1)}, u32[]{:S(2)}, u32[]{:S(2)}) collective-permute-start(bf16[512,384]{1,0:T(8,128)(2,1)} %late.1.a0), channel_id=1, source_target_pairs={{0,1},{1,2},{2,3},{3,0},{4,5},{5,6},{6,7},{7,4},{8,9},{9,10},{10,1... | collective-permute-start | bytes 1179656 | tf_op jit(solution)/shard_map/ppermute | solution.py:58
  89.8 21.8 %collective-permute-start.9 = (bf16[512,384]{1,0:T(8,128)(2,1)}, bf16[512,384]{1,0:T(8,128)(2,1)S(1)}, u32[]{:S(2)}, u32[]{:S(2)}) collective-permute-start(bf16[512,384]{1,0:T(8,128)(2,1)} %late.1.a0), channel_id=1, source_target_pairs={{0,2},{1,3},{2,0},{3,1},{4,6},{5,7},{6,4},{7,5},{8,10},{9,11},{10,... | collective-permute-start | bytes 1179656 | tf_op jit(solution)/shard_map/ppermute | solution.py:58
  92.1 23.2 %copy-start.4 = (bf16[512,384]{1,0:T(8,128)(2,1)S(1)}, bf16[512,384]{1,0:T(8,128)(2,1)}, u32[]{:S(2)}) copy-start(bf16[512,384]{1,0:T(8,128)(2,1)} %late.1.a0) | copy-start | bytes 1179652
  95.9 16.4 %collective-permute-start.12 = (bf16[8,768]{1,0:T(8,128)(2,1)}, bf16[8,768]{1,0:T(8,128)(2,1)S(1)}, u32[]{:S(2)}, u32[]{:S(2)}) collective-permute-start(bf16[8,768]{1,0:T(8,128)(2,1)} %get-tuple-element.19), channel_id=1, source_target_pairs={{0,1},{1,2},{2,3},{3,0},{4,5},{5,6},{6,7},{7,4},{8,9},{9,10},{10,1... | collective-permute-start | bytes 36872 | tf_op jit(solution)/shard_map/ppermute | solution.py:58
  107.2 5.4 %collective-permute-start.13 = (bf16[8,768]{1,0:T(8,128)(2,1)}, bf16[8,768]{1,0:T(8,128)(2,1)S(1)}, u32[]{:S(2)}, u32[]{:S(2)}) collective-permute-start(bf16[8,768]{1,0:T(8,128)(2,1)} %get-tuple-element.20), channel_id=1, source_target_pairs={{0,2},{1,3},{2,0},{3,1},{4,6},{5,7},{6,4},{7,5},{8,10},{9,11},{10,... | collective-permute-start | bytes 36872 | tf_op jit(solution)/shard_map/ppermute | solution.py:58
  110.7 0.7 copy-start.5
  111.4 3.9 %collective-permute-start.14 = (bf16[8,768]{1,0:T(8,128)(2,1)}, bf16[8,768]{1,0:T(8,128)(2,1)S(1)}, u32[]{:S(2)}, u32[]{:S(2)}) collective-permute-start(bf16[8,768]{1,0:T(8,128)(2,1)} %get-tuple-element.21), channel_id=1, source_target_pairs={{0,3},{1,0},{2,1},{3,2},{4,7},{5,4},{6,5},{7,6},{8,11},{9,8},{10,9... | collective-permute-start | bytes 36872 | tf_op jit(solution)/shard_map/ppermute | solution.py:58
  111.6 0.8 copy-start.7
  115.3 1.0 copy-start.6
  116.3 1.0 copy-start.8
  117.3 0.7 copy-start.9
  122.0 9.4 %collective-permute-start.15 = (bf16[528,384]{1,0:T(8,128)(2,1)S(1)}, bf16[528,384]{1,0:T(8,128)(2,1)S(1)}, u32[]{:S(2)}, u32[]{:S(2)}) collective-permute-start(bf16[528,384]{1,0:T(8,128)(2,1)S(1)} %get-tuple-element.23), channel_id=1, source_target_pairs={{0,4},{1,5},{2,6},{3,7},{4,0},{5,1},{6,2},{7,3},{8,12},{9,13},{10,... | collective-permute-start | bytes 1216520 | tf_op jit(solution)/shard_map/ppermute | solution.py:62
